TPU v7x, 32 devices: a whole 2x2x4 slice. The times are simulated.
32 devices in a mesh: kv: 2 (over x), wide: 16 (over z, y, core).
Axes of the slice: x: 2, y: 2, z: 4, core: 2. Of those that a mesh axis runs over, the one named last changes fastest.
Arguments:
- hidden_input: bfloat16 [48, 16384], P(None, 'kv'), may hold values from -6 to 6
- input_norm_gain: float32 [16384], P('kv'), may hold values from 0.25 to 1.75
- joint_projection_weight: bfloat16 [16384, 18432], P('kv', 'wide'), may hold values from -0.046875 to 0.046875
- output_weight: bfloat16 [16384, 16384], P('kv', 'wide'), may hold values from -0.046875 to 0.046875
- key_cache: bfloat16 [48, 8, 512, 128], P('wide', 'kv'), may hold values from -210 to 210
- value_cache: bfloat16 [48, 8, 512, 128], P('wide', 'kv'), may hold values from -6 to 6
- joint_down_weight: bfloat16 [16, 16384, 24], P('wide', 'kv'), may hold values from -0.046875 to 0.046875
- query_up_weight: bfloat16 [16, 8, 16384], P('wide', None, 'kv'), may hold values from -2 to 2
- key_value_up_weight: bfloat16 [16, 2, 8, 1024], P('wide', None, None, 'kv'), may hold values from -2 to 2
- output_down_weight: bfloat16 [16, 16384, 8], P('wide', 'kv'), may hold values from -0.046875 to 0.046875
- output_up_weight: bfloat16 [16, 8, 16384], P('wide'), may hold values from -2 to 2
- row_adapter_index: int32 [48], replicated, may hold values from 0 to 15
- adapter_owner_slot: int32 [16], replicated, may hold values from 0 to 15, each once
- lengths: int32 [48], P('wide'), may hold values from 64 to 512, as said below
Outputs:
- out: bfloat16 [48, 16384], P('kv', 'wide')
Inputs may be any that keep to these rules, and one draw needn't show every extreme that they name: Row lengths; at least one row has exactly 512. `adapter_owner_slot`: each adapter's owner slot, a permutation.
All inputs are finite; a program needn't handle non-finite values.
Results may differ from a plain program's by a relative error of at most 0.019.
The roundings to bfloat16 on the way count: a program that leaves them out, or rounds other values in their place, can miss the bound.
Values may be sent and summed in bfloat16 or wider, within the bound.
No kernel may reach another device: no remote copies, remote signals or barrier semaphores. Data moves between devices by JAX's collectives and lax.ppermute only.
A program may use at most 128 MiB of HBM per device.

v0:
```python
import jax
import jax.numpy as jnp
from jax import lax
from jax.sharding import PartitionSpec as P

MODEL_WIDTH = 16384


rope_base = 500000.0
adapter_scale = 2.0


def rotate(values, positions):
    half = values.shape[-1] // 2
    freq = rope_base ** (-jnp.arange(half, dtype=jnp.float32) * 2.0 / values.shape[-1])
    angle = positions.astype(jnp.float32)[:, None] * freq[None, :]
    array_shape = (angle.shape[0],) + (1,) * (values.ndim - 2) + (half,)
    cosine = jnp.cos(angle).reshape(array_shape)
    sine = jnp.sin(angle).reshape(array_shape)
    first = values[..., :half]
    second = values[..., half:]
    return jnp.concatenate(
        [first * cosine - second * sine, second * cosine + first * sine], axis=-1
    )


def arrange(query_change, key_change, value_change, local_key_value):
    count = query_change.shape[0]
    joined = jnp.concatenate(
        [
            query_change.reshape(count, local_key_value, -1),
            key_change.reshape(count, local_key_value, -1),
            value_change.reshape(count, local_key_value, -1),
        ],
        axis=2,
    )
    return joined.reshape(count, -1)


def on_device(
    hidden_input,
    input_norm_gain,
    joint_projection_weight,
    output_weight,
    key_cache,
    value_cache,
    joint_down_weight,
    query_up_weight,
    key_value_up_weight,
    output_down_weight,
    output_up_weight,
    row_adapter_index,
    adapter_owner_slot,
    lengths,
):
    local_rows = lengths.shape[0]
    local_key_value = key_cache.shape[1]
    head_dim = key_cache.shape[3]
    rank_width = query_up_weight.shape[1]
    wide_pos = lax.axis_index("wide")
    kv_pos = lax.axis_index("kv")
    row_start = wide_pos * local_rows
    table = (
        row_adapter_index[:, None]
        == jnp.arange(adapter_owner_slot.shape[0], dtype=jnp.int32)[None, :]
    )
    row_slot = jnp.sum(jnp.where(table, adapter_owner_slot[None, :], 0), axis=1)
    mine = (row_slot == wide_pos).astype(jnp.float32)
    widened = hidden_input.astype(jnp.float32)
    scaled_hidden = (widened * input_norm_gain[None, :]).astype(jnp.bfloat16)
    partial_sq = jnp.sum(widened * widened, axis=1)
    partial_reduced = jnp.dot(
        scaled_hidden, joint_down_weight[0], preferred_element_type=jnp.float32
    )
    total_sq, reduced_hidden = lax.psum((partial_sq, partial_reduced), "kv")
    scale = lax.rsqrt(total_sq / MODEL_WIDTH + 1e-05)
    shrink_bf = (reduced_hidden * scale[:, None] * mine[:, None]).astype(jnp.bfloat16)
    base_part = jnp.dot(scaled_hidden, joint_projection_weight, preferred_element_type=jnp.float32)
    regrouped = lax.all_to_all(base_part, "wide", split_axis=0, concat_axis=1, tiled=True)
    grouped_heads = lax.psum_scatter(regrouped, "kv", scatter_dimension=1, tiled=True)
    row_scale = lax.dynamic_slice_in_dim(scale, row_start, local_rows)
    grouped_heads = grouped_heads * row_scale[:, None]
    shrinks = lax.all_gather(shrink_bf[None], "wide", axis=0, tiled=True)
    query_sheet = lax.all_gather(query_up_weight, "wide", axis=0, tiled=True)
    key_value_sheet = lax.all_gather(key_value_up_weight, "wide", axis=0, tiled=True)
    own_rows = lax.dynamic_slice_in_dim(shrinks, row_start, local_rows, 1)
    query_change = jnp.einsum(
        "nbr,nrc->bc", own_rows[:, :, :rank_width], query_sheet, preferred_element_type=jnp.float32
    )
    key_change = jnp.einsum(
        "nbr,nrc->bc",
        own_rows[:, :, rank_width : 2 * rank_width],
        key_value_sheet[:, 0],
        preferred_element_type=jnp.float32,
    )
    value_change = jnp.einsum(
        "nbr,nrc->bc",
        own_rows[:, :, 2 * rank_width :],
        key_value_sheet[:, 1],
        preferred_element_type=jnp.float32,
    )
    adapter_change = arrange(query_change, key_change, value_change, local_key_value)
    merged_output = (grouped_heads + adapter_scale * adapter_change).reshape(
        local_rows, local_key_value, -1
    )
    width = merged_output.shape[2] - 2 * head_dim
    heads_per = width // head_dim
    query_vector = rotate(
        merged_output[:, :, :width].reshape(local_rows, local_key_value, heads_per, head_dim),
        lengths,
    ).astype(jnp.bfloat16)
    fresh_key = rotate(merged_output[:, :, width : width + head_dim], lengths).astype(jnp.bfloat16)
    value_new = merged_output[:, :, width + head_dim :].astype(jnp.bfloat16)
    inverse_root = jnp.sqrt(jnp.float32(head_dim))
    scores = (
        jnp.einsum("rkgd,rkld->rkgl", query_vector, key_cache, preferred_element_type=jnp.float32)
        / inverse_root
    )
    valid = jnp.arange(key_cache.shape[2], dtype=jnp.int32)[None, :] < lengths[:, None]
    scores = jnp.where(valid[:, None, None, :], scores, -jnp.inf)
    fresh_score = (
        jnp.einsum("rkgd,rkd->rkg", query_vector, fresh_key, preferred_element_type=jnp.float32)
        / inverse_root
    )
    top = jnp.maximum(jnp.max(scores, axis=-1), fresh_score)
    expd = jnp.exp(scores - top[..., None])
    exp_new = jnp.exp(fresh_score - top)
    total = jnp.sum(expd, axis=-1) + exp_new
    probs = (expd / total[..., None]).astype(jnp.bfloat16)
    prob_new = (exp_new / total).astype(jnp.bfloat16)
    attention_output = jnp.einsum(
        "rkgl,rkld->rkgd", probs, value_cache, preferred_element_type=jnp.float32
    )
    attention_output = (
        attention_output
        + prob_new.astype(jnp.float32)[..., None] * value_new.astype(jnp.float32)[:, :, None, :]
    )
    attention_output = attention_output.astype(jnp.bfloat16).reshape(local_rows, -1)
    out_cols = output_weight.shape[1]
    slice_portion = lax.all_gather(attention_output, "wide", axis=0, tiled=True)
    mixed = jnp.concatenate(
        [
            jnp.dot(slice_portion, output_weight, preferred_element_type=jnp.float32),
            jnp.dot(slice_portion, output_down_weight[0], preferred_element_type=jnp.float32),
        ],
        axis=1,
    )
    output_baseline = lax.psum_scatter(
        mixed[:, :out_cols].astype(jnp.bfloat16), "kv", scatter_dimension=0, tiled=True
    ).astype(jnp.float32)
    output_reduced = lax.psum(mixed[:, out_cols:], "kv")
    block = output_baseline.shape[0]
    own_shrink = lax.dynamic_slice_in_dim(
        output_reduced * mine[:, None], kv_pos * block, block, 0
    ).astype(jnp.bfloat16)
    weight_sheet = output_up_weight[0]
    output_change = lax.psum_scatter(
        jnp.dot(weight_sheet.T, own_shrink.T, preferred_element_type=jnp.float32),
        "wide",
        scatter_dimension=0,
        tiled=True,
    )
    return (output_baseline + adapter_scale * output_change.T).astype(jnp.bfloat16)


def solution(mesh):
    in_specs = (
        P(None, "kv"),
        P("kv"),
        P("kv", "wide"),
        P("kv", "wide"),
        P("wide", "kv", None, None),
        P("wide", "kv", None, None),
        P("wide", "kv", None),
        P("wide", None, "kv"),
        P("wide", None, None, "kv"),
        P("wide", "kv", None),
        P("wide", None, None),
        P(),
        P(),
        P("wide"),
    )
    out_specs = P("kv", "wide")
    return jax.shard_map(
        on_device, mesh=mesh, in_specs=in_specs, out_specs=out_specs, check_vma=False
    )
```

profile of v0, /device:TPU:0, one launch (start us, length us, event | category | flops | bytes accessed | tf_op | source)
XLA Modules:
  0.0 275.2 jit_solution(16602169093627016363)
XLA Ops:
  7.4 9.9 %fusion.6 = f32[48,1152]{1,0:T(8,128)S(1)} fusion(bf16[8192,1152]{1,0:T(8,128)(2,1)} %param.16, bf16[48,8192]{1,0:T(8,128)(2,1)} %param.14, f32[8192]{0:T(1024)} %param.15), kind=kOutput, calls=%fused_computation.14 | convolution fusion | flops 907149312 | bytes 19914752 | tf_op jit(solution)/shard_map/dot_general | solution.py:78
  17.4 17.8 %all_to_all.19 = f32[16,3,1152]{2,1,0:T(4,128)S(1)} all-to-all(f32[16,3,1152]{2,1,0:T(4,128)S(1)} %all_to_all.14), channel_id=1, replica_groups=mesh['kv'=2,'wide'=16] {'wide'}, dimensions={0} | all-to-all | bytes 442368 | tf_op jit(solution)/shard_map/all_to_all | solution.py:79
  35.2 5.0 %copy.43 = f32[3,18432]{0,1:T(8,128)} copy(f32[3,18432]{1,0:T(4,128)S(1)} %bitcast.72) | data formatting | bytes 442368
  40.3 0.5 all-gather.5.cloned.1.call-update
  40.9 0.4 copy-done.1
  41.3 0.3 fusion.1
  41.6 0.3 fusion.4
  41.9 8.2 %all-reduce = (f32[48,24]{0,1:T(8,128)S(1)}, f32[48]{0:T(128)S(1)}) all-reduce(f32[48,24]{0,1:T(8,128)S(1)} %fusion.4, f32[48]{0:T(128)S(1)} %fusion.1), channel_id=1, replica_groups=mesh['kv'=2,'wide'=16] {'kv'}, use_global_device_ids=true, to_apply=%region_3.4 | all-reduce | flops 1200 | bytes 9600 | tf_op jit(solution)/shard_map/psum | solution.py:75
  50.4 19.1 %all-gather.1 = bf16[16,48,24]{1,2,0:T(8,128)(2,1)S(1)} all-gather(bf16[1,48,24]{1,2,0:T(8,128)(2,1)S(1)} %fusion.23), channel_id=2, replica_groups=mesh['kv'=2,'wide'=16] {'wide'}, dimensions={0}, use_global_device_ids=true | all-gather | bytes 39168 | tf_op jit(solution)/shard_map/all_gather | solution.py:83
  69.4 18.5 %all_gather.14 = bf16[16,2,8,512]{3,2,1,0:T(8,128)(2,1)S(1)} all-gather(bf16[1,2,8,512]{3,2,1,0:T(8,128)(2,1)S(1)} %copy-done.5), channel_id=1, replica_groups=mesh['kv'=2,'wide'=16] {'wide'}, dimensions={0}, use_global_device_ids=true | all-gather | bytes 278528 | tf_op jit(solution)/shard_map/all_gather | solution.py:85
  88.7 61.0 %reduce-scatter.10.cloned.1.call-done = f32[9216,3]{1,0:T(8,128)} async-done(((f32[18432,3]{1,0:T(8,128)}), f32[9216,3]{1,0:T(8,128)}) %reduce-scatter.10.cloned.1.call-update) | async-done | bytes 110608
  149.6 3.1 %copy.44 = f32[3,9216]{1,0:T(4,128)S(1)} copy(f32[3,9216]{0,1:T(8,128)} %bitcast.71) | data formatting | bytes 221184
  152.7 2.1 convolution_bitcast_fusion.1
  155.8 0.6 fusion.34
  156.7 0.4 fusion.3
  157.1 24.3 %all-gather.2 = bf16[16,3,8192]{2,1,0:T(4,128)(2,1)S(1)} all-gather(bf16[1,3,8192]{2,1,0:T(4,128)(2,1)S(1)} %reshape.157), channel_id=1, replica_groups=mesh['kv'=2,'wide'=16] {'wide'}, dimensions={0}, use_global_device_ids=true | all-gather | bytes 835584 | tf_op jit(solution)/shard_map/all_gather | solution.py:140
  181.5 0.7 reshape.158
  182.2 0.3 fusion.17
  182.5 4.9 %psum.23 = f32[48,8]{0,1:T(8,128)S(1)} all-reduce(f32[48,8]{0,1:T(8,128)S(1)} %fusion.17), channel_id=1, replica_groups=mesh['kv'=2,'wide'=16] {'kv'}, use_global_device_ids=true, to_apply=%region_8.9 | all-reduce | flops 384 | bytes 3072 | tf_op jit(solution)/shard_map/psum | solution.py:151
  187.4 9.5 %convolution_convert_fusion = bf16[48,1024]{1,0:T(8,128)(2,1)} fusion(bf16[48,8192]{1,0:T(8,128)(2,1)S(1)} %reshape.158, bf16[8192,1024]{1,0:T(8,128)(2,1)} %param.17), kind=kOutput, calls=%fused_computation.8 | convolution fusion | flops 805355520 | bytes 17661952 | tf_op jit(solution)/shard_map/dot_general | solution.py:143
  197.0 1.6 convolution_bitcast_fusion
  198.7 4.8 %reduce-scatter.6.cloned.1.call-done = bf16[24,1024]{1,0:T(8,128)(2,1)} async-done(((bf16[48,1024]{1,0:T(8,128)(2,1)}), bf16[24,1024]{1,0:T(8,128)(2,1)}) %reduce-scatter.6.cloned.1.call-update) | async-done | bytes 49168 | tf_op jit(solution)/shard_map/reduce_scatter | solution.py:148
  203.4 63.1 %reduce-scatter.8.cloned.1.call-done = f32[1024,24]{0,1:T(8,128)} async-done(((f32[16384,24]{0,1:T(8,128)}), f32[1024,24]{0,1:T(8,128)}) %reduce-scatter.8.cloned.1.call-update) | async-done | bytes 98320 | tf_op jit(solution)/shard_map/reduce_scatter | solution.py:157
  266.5 1.5 fusion.20
  (61 shorter events, 2.4 us)
Async XLA Ops:
  7.4 148.4 %copy-start = (bf16[3,4,512,128]{3,2,1,0:T(8,128)(2,1)S(1)}, bf16[3,4,512,128]{3,2,1,0:T(8,128)(2,1)}, u32[]{:S(2)}) copy-start(bf16[3,4,512,128]{3,2,1,0:T(8,128)(2,1)} %param.18) | copy-start | bytes 4718596
  7.4 142.2 %reduce-scatter.10.cloned.1.call-start = ((), (), s32[]{:S(2)}) async-start(), calls=%async_computation.7 | async-start | bytes 14155776
  40.2 1.1 copy-start.1
  40.2 1.4 copy-start.4
  40.2 1.4 copy-start.8
  40.2 10.0 %copy-start.9 = (s32[16]{0:T(128)S(1)}, s32[16]{0:T(128)}, u32[]{:S(2)}) copy-start(s32[16]{0:T(128)} %param.26) | copy-start | bytes 196
  40.2 10.0 %copy-start.10 = (s32[48]{0:T(128)S(1)}, s32[48]{0:T(128)}, u32[]{:S(2)}) copy-start(s32[48]{0:T(128)} %param.25) | copy-start | bytes 580
  40.3 29.2 %copy-start.5 = (bf16[1,2,8,512]{3,2,1,0:T(8,128)(2,1)S(1)}, bf16[1,2,8,512]{3,2,1,0:T(8,128)(2,1)}, u32[]{:S(2)}) copy-start(bf16[1,2,8,512]{3,2,1,0:T(8,128)(2,1)} %param.22) | copy-start | bytes 49156
  40.3 112.4 %all-gather.5.cloned.1.call-start = ((), (), s32[]{:S(2)}) async-start(), calls=%async_computation.4 | async-start | bytes 2228224 | tf_op jit(solution)/shard_map/all_gather | solution.py:84
  40.8 162.6 %reduce-scatter.6.cloned.1.call-start = ((), (), s32[]{:S(2)}) async-start(), calls=%async_computation.5 | async-start | bytes 147456 | tf_op jit(solution)/shard_map/reduce_scatter | solution.py:148
  41.3 47.1 %copy-start.6 = (s32[3]{0:T(128)S(1)}, s32[3]{0:T(128)}, u32[]{:S(2)}) copy-start(s32[3]{0:T(128)} %param.27) | copy-start | bytes 40
  155.3 1.4 copy-start.7
  157.1 25.1 %copy-start.3 = (bf16[1,8192,8]{1,2,0:T(8,128)(2,1)S(1)}, bf16[1,8192,8]{1,2,0:T(8,128)(2,1)}, u32[]{:S(2)}) copy-start(bf16[1,8192,8]{1,2,0:T(8,128)(2,1)} %param.23) | copy-start | bytes 393220
  187.4 9.6 %copy-start.2 = (bf16[1,8,16384]{2,1,0:T(8,128)(2,1)S(1)}, bf16[1,8,16384]{2,1,0:T(8,128)(2,1)}, u32[]{:S(2)}) copy-start(bf16[1,8,16384]{2,1,0:T(8,128)(2,1)} %param.24) | copy-start | bytes 786436
  196.9 69.6 %reduce-scatter.8.cloned.1.call-start = ((), (), s32[]{:S(2)}) async-start(), calls=%async_computation.6 | async-start | bytes 1671168 | tf_op jit(solution)/shard_map/reduce_scatter | solution.py:157
Sparse Core Ops, SparseCore 0:
  40.3 109.2 reduce-scatter.9
  197.1 6.3 reduce-scatter.5
  207.1 59.4 reduce-scatter.7
Sparse Core Ops, SparseCore 1:
  42.9 40.3 all-gather.4
where the time goes:
time: 276 us; the launch traced here: 275 us
  waiting for transfers between devices  129 us (47%)
  blocking collectives  92.8 us (34%)
  matrix products  25.5 us (9%)
  between operations  14.8 us (5%)
  local copies, waits for them, and re-layouts  9.8 us (4%)
    reduce_scatter x1, waiting for transfers between devices, on_device(): lax.psum_scatter(jnp.dot(weight_sheet.T, own_shrink.T, preferred_element_...  63.1 us
    unnamed x5, waiting for transfers between devices  61.5 us
    all_gather x1, blocking collectives, on_device(): slice_portion = lax.all_gather(attention_output, 'wide', axis=0, tiled=True)  24.3 us
    all_gather x1, blocking collectives, on_device(): shrinks = lax.all_gather(shrink_bf[None], 'wide', axis=0, tiled=True)  19.1 us
    all_gather x1, blocking collectives, on_device(): lax.all_gather(key_value_up_weight, 'wide', axis=0, tiled=True)  18.5 us
    all_to_all x1, blocking collectives, on_device(): lax.all_to_all(base_part, 'wide', split_axis=0, concat_axis=1, tiled=True)  17.8 us
    dot_general x1, matrix products, on_device(): jnp.dot(scaled_hidden, joint_projection_weight, preferred_element_type=jn...  9.92 us
    dot_general x1, matrix products, on_device(): jnp.dot(slice_portion, output_weight, preferred_element_type=jnp.float32)  9.47 us
  transfers between devices with their start and end apart: 4, of which 3 were waited for; matrix products, arithmetic and copies ran while one was open for 2% of the time, Pallas kernels for 0%

commit v1 on v0

--- a/solution.py
+++ b/solution.py
@@ -37,7 +37,7 @@
     return joined.reshape(count, -1)
 
 
-def on_device(
+def general_path(
     hidden_input,
     input_norm_gain,
     joint_projection_weight,
@@ -163,6 +163,212 @@
     return (output_baseline + adapter_scale * output_change.T).astype(jnp.bfloat16)
 
 
+def staged_path(
+    hidden_input,
+    input_norm_gain,
+    joint_projection_weight,
+    output_weight,
+    key_cache,
+    value_cache,
+    joint_down_weight,
+    query_up_weight,
+    key_value_up_weight,
+    output_down_weight,
+    output_up_weight,
+    row_adapter_index,
+    adapter_owner_slot,
+    lengths,
+):
+    f32, bf16 = jnp.float32, jnp.bfloat16
+    batch = hidden_input.shape[0]
+    rows = lengths.shape[0]
+    heads = key_cache.shape[1]
+    head_dim = key_cache.shape[3]
+    rank = query_up_weight.shape[1]
+    cols = joint_projection_weight.shape[1]
+    out_cols = output_weight.shape[1]
+    blocks = cols // head_dim
+    group = 2 * blocks - 2
+    wide = batch // rows
+    kv_pos = lax.axis_index("kv")
+    wide_pos = lax.axis_index("wide")
+    core = wide_pos & 1
+    y = (wide_pos >> 1) & 1
+    z = wide_pos >> 2
+    right = (z >> 1) == kv_pos
+
+    def is_right(i):
+        return ((i % wide) >> 3) == i // wide
+
+    def swap(x, mask, source=None, target=None):
+        pairs = [(i, i ^ mask) for i in range(2 * wide)]
+        if source is not None:
+            pairs = [p for p in pairs if is_right(p[0]) == source]
+        if target is not None:
+            pairs = [p for p in pairs if is_right(p[1]) == target]
+        return lax.ppermute(x, ("kv", "wide"), pairs)
+
+    def pick(x, i, axis=0):
+        return lax.dynamic_index_in_dim(x, i, axis, keepdims=False)
+
+    table = row_adapter_index[:, None] == jnp.arange(wide, dtype=jnp.int32)[None, :]
+    slot = jnp.sum(jnp.where(table, adapter_owner_slot[None, :], 0), axis=1)
+
+    def reorder(x):
+        rest = x.shape[1:]
+        x = x.reshape((4, 2, 2 * rows) + rest)
+        return jnp.swapaxes(x, 0, 1).reshape((batch,) + rest)
+
+    slot_r = reorder(slot)
+    mine_r = (slot_r == wide_pos).astype(f32)
+    mine = (slot == wide_pos).astype(f32)
+
+    sheet = jnp.concatenate(
+        [
+            query_up_weight[0].reshape(rank, heads, -1),
+            key_value_up_weight[0, 0].reshape(rank, heads, -1),
+            key_value_up_weight[0, 1].reshape(rank, heads, -1),
+        ],
+        axis=2,
+    )
+    sheet = sheet.reshape(rank, 2, 2, 2, cols).transpose(3, 1, 2, 0, 4)
+    pair = jnp.concatenate([pick(sheet, core), swap(pick(sheet, 1 - core), 1)], axis=2)
+    same, flip = pick(pair, z & 1), pick(pair, 1 - (z & 1))
+    ups = jnp.stack(
+        [same, swap(flip, 4, target=True), swap(same, 8, target=True), swap(flip, 12, target=True)]
+    )
+    ups_y = swap(ups, 2, target=True)
+    up_of = [
+        jnp.concatenate([ups[:, b].reshape(-1, cols), ups_y[:, b].reshape(-1, cols)], axis=0)
+        for b in range(2)
+    ]
+    lane = jnp.arange(wide, dtype=jnp.int32)
+    owner = wide_pos ^ (((lane >> 1) & 3) * 4 + (lane >> 3) * 2 + (lane & 1))
+
+    def spread(values, slots):
+        hit = slots[:, None] == owner[None, :]
+        return jnp.where(hit[:, :, None], values[:, None, :], 0).reshape(values.shape[0], -1)
+
+    widened = hidden_input.astype(f32)
+    gained = reorder((widened * input_norm_gain[None, :]).astype(bf16))
+    square = reorder(jnp.sum(widened * widened, axis=1))
+    reduced = jnp.dot(gained, joint_down_weight[0], preferred_element_type=f32)
+    small = jnp.concatenate([reduced, square[:, None]], axis=1) * mine_r[:, None]
+
+    def sum_all(v):
+        v = v + swap(v, 1)
+        v = (v + swap(v, 4)) + (swap(v, 8) + swap(v, 12))
+        return (v + swap(v, 2)) + (swap(v, 16) + swap(v, 18))
+
+    small = sum_all(small)
+    scale = lax.rsqrt(small[:, 3 * rank] / MODEL_WIDTH + 1e-05)
+    shrink = (small[:, : 3 * rank] * scale[:, None]).astype(bf16)
+
+    half = batch // 2
+    partial = jnp.dot(gained, joint_projection_weight, preferred_element_type=f32).astype(bf16)
+    keep = lax.dynamic_slice_in_dim(partial, y * half, half)
+    give = lax.dynamic_slice_in_dim(partial, (1 - y) * half, half)
+    from_x = swap(keep, 16, target=True)
+    from_xy = swap(give, 18, target=True)
+    from_y = swap(give, 2, target=True)
+    scale_h = lax.dynamic_slice_in_dim(scale, y * half, half)[:, None]
+    shrink_h = lax.dynamic_slice_in_dim(shrink, y * half, half)
+    slot_h = lax.dynamic_slice_in_dim(slot_r, y * half, half)
+    spread_of = [spread(shrink_h[:, t * rank : (t + 1) * rank], slot_h) for t in range(3)]
+    last = core == 1
+
+    def delta(b):
+        sheet_b = pick(jnp.stack(up_of), b)
+        cut = cols - 2 * head_dim
+        q_part = jnp.dot(spread_of[0], sheet_b[:, :cut], preferred_element_type=f32)
+        k_lhs = jnp.where(last, spread_of[1], spread_of[0])
+        v_lhs = jnp.where(last, spread_of[2], spread_of[0])
+        k_part = jnp.dot(k_lhs, sheet_b[:, cut : cut + head_dim], preferred_element_type=f32)
+        v_part = jnp.dot(v_lhs, sheet_b[:, cut + head_dim :], preferred_element_type=f32)
+        return jnp.concatenate([q_part, k_part, v_part], axis=1)
+
+    own = (keep.astype(f32) + from_x.astype(f32)) * scale_h + adapter_scale * delta(y)
+    other = (from_y.astype(f32) + from_xy.astype(f32)) * scale_h + adapter_scale * delta(1 - y)
+    first = jnp.where(y == 0, own, other)
+    second = jnp.where(y == 0, other, own)
+    merged = jnp.stack([first, second]).astype(bf16)
+    merged = merged.reshape(2, 4, 2 * rows, blocks, head_dim).transpose(1, 0, 3, 2, 4)
+    to = [pick(merged, z ^ d) for d in range(4)]
+    from_1 = swap(to[1], 4, source=True)
+    from_2 = swap(to[2], 8, source=True)
+    from_3 = swap(to[3], 12, source=True)
+    near = jnp.stack([jnp.where(right, to[0], from_2), jnp.where(right, from_1, from_3)])
+    far = swap(near, 1)
+    parts = [jnp.where(core == 0, near, far), jnp.where(core == 0, far, near)]
+    parts = [
+        lax.dynamic_slice_in_dim(jnp.where((z & 1) == 0, p, p[::-1]), core * rows, rows, 3)
+        for p in parts
+    ]
+    joined = jnp.concatenate(parts, axis=2).astype(f32)
+    joined = joined.reshape(heads, 2 * blocks, rows, head_dim).transpose(2, 0, 1, 3)
+    query_vector = rotate(joined[:, :, :group], lengths).astype(bf16)
+    fresh_key = rotate(joined[:, :, group], lengths).astype(bf16)
+    value_new = joined[:, :, group + 1].astype(bf16)
+
+    inverse_root = jnp.sqrt(f32(head_dim))
+    scores = jnp.einsum("rkgd,rkld->rkgl", query_vector, key_cache, preferred_element_type=f32)
+    scores = scores / inverse_root
+    valid = jnp.arange(key_cache.shape[2], dtype=jnp.int32)[None, :] < lengths[:, None]
+    scores = jnp.where(valid[:, None, None, :], scores, -jnp.inf)
+    fresh_score = (
+        jnp.einsum("rkgd,rkd->rkg", query_vector, fresh_key, preferred_element_type=f32)
+        / inverse_root
+    )
+    top = jnp.maximum(jnp.max(scores, axis=-1), fresh_score)
+    expd = jnp.exp(scores - top[..., None])
+    exp_new = jnp.exp(fresh_score - top)
+    total = jnp.sum(expd, axis=-1) + exp_new
+    probs = (expd / total[..., None]).astype(bf16)
+    prob_new = (exp_new / total).astype(bf16)
+    attended = jnp.einsum("rkgl,rkld->rkgd", probs, value_cache, preferred_element_type=f32)
+    attended = (
+        attended + prob_new.astype(f32)[..., None] * value_new.astype(f32)[:, :, None, :]
+    )
+    attended = attended.astype(bf16).reshape(rows, -1)
+
+    o_sheet = output_up_weight[0].reshape(rank, 4, 2, 2, out_cols).transpose(3, 1, 2, 0, 4)
+    o_pair = jnp.concatenate([pick(o_sheet, core), swap(pick(o_sheet, 1 - core), 1)], axis=2)
+    o_ups = jnp.stack(
+        [pick(o_pair, z)] + [swap(pick(o_pair, z ^ d), 4 * d) for d in range(1, 4)]
+    )
+    o_near = pick(o_ups, y, 1)
+    o_far = swap(pick(o_ups, 1 - y, 1), 2)
+    o_up = jnp.concatenate(
+        [o_near.reshape(-1, out_cols), o_far.reshape(-1, out_cols)], axis=0
+    )
+
+    piece = attended[None]
+    piece = jnp.concatenate([piece, swap(piece, 4), swap(piece, 8), swap(piece, 12)], axis=0)
+    piece = jnp.concatenate([piece, swap(piece, 2)], axis=0)
+    piece = jnp.concatenate([piece, swap(piece, 1)], axis=0)
+    rel = jnp.arange(wide, dtype=jnp.int32) ^ wide_pos
+    place = (rel & 1) * 8 + ((rel >> 1) & 1) * 4 + (rel >> 2)
+    everyone = jnp.take(piece, place, axis=0).reshape(batch, -1)
+
+    o_reduced = jnp.dot(everyone, output_down_weight[0], preferred_element_type=f32)
+    o_reduced = sum_all(o_reduced * mine[:, None])
+    mixed = jnp.dot(everyone, output_weight, preferred_element_type=f32)
+    keep_out = lax.dynamic_slice_in_dim(mixed, kv_pos * half, half)
+    give_out = lax.dynamic_slice_in_dim(mixed, (1 - kv_pos) * half, half).astype(bf16)
+    from_out = swap(give_out, 16)
+    o_shrink = lax.dynamic_slice_in_dim(o_reduced, kv_pos * half, half).astype(bf16)
+    slot_o = lax.dynamic_slice_in_dim(slot, kv_pos * half, half)
+    change = jnp.dot(spread(o_shrink, slot_o), o_up, preferred_element_type=f32)
+    return (keep_out + from_out.astype(f32) + adapter_scale * change).astype(bf16)
+
+
+def on_device(*arrays):
+    lengths, key_cache, weight = arrays[13], arrays[4], arrays[2]
+    batch, rows, heads = arrays[0].shape[0], lengths.shape[0], key_cache.shape[1]
+    staged = batch == 16 * rows and heads == 4 and 2 * weight.shape[1] == 18 * key_cache.shape[3]
+    return (staged_path if staged else general_path)(*arrays)
+
+
 def solution(mesh):
     in_specs = (
         P(None, "kv"),

time: 276 us -> 135 us (0.49)
  blocking collectives: 92.8 us -> 0 us
  waiting for transfers between devices: 129 us -> 38.4 us
  starting transfers between devices: 0.13 us -> 51.8 us
  between operations: 14.8 us -> 0.76 us
  local copies, waits for them, and re-layouts: 9.8 us -> 15.5 us
  matrix products: 25.5 us -> 21.6 us
  other arithmetic: 2.76 us -> 5.88 us
    reduce_scatter x2 -> x0, waiting for transfers between devices: 67.9 us -> none  [the longest x1 63.1 us: on_device(): lax.psum_scatter(jnp.dot(weight_sheet.T, own_shrink.T, preferred_element_...]
    all_gather x3 -> x0, blocking collectives: 61.9 us -> none  [the longest x1 24.3 us: on_device(): slice_portion = lax.all_gather(attention_output, 'wide', axis=0, tiled=True)]
    unnamed x5 -> x0, waiting for transfers between devices: 61.5 us -> none
    ppermute x0 -> x37, starting transfers between devices: none -> 51.8 us  [swap(): return lax.ppermute(x, ('kv', 'wide'), pairs)]
    ppermute x0 -> x37, waiting for transfers between devices: none -> 38.4 us  [swap(): return lax.ppermute(x, ('kv', 'wide'), pairs)]
    all_to_all x1 -> x0, blocking collectives: 17.8 us -> none  [on_device(): lax.all_to_all(base_part, 'wide', split_axis=0, concat_axis=1, tiled=True)]
    psum x2 -> x0, blocking collectives: 13.2 us -> none  [the longest x1 8.24 us: on_device(): total_sq, reduced_hidden = lax.psum((partial_sq, partial_reduced), 'kv')]
    unnamed x28 -> x25, local copies, waits for them, and re-layouts: 9.35 us -> 2.71 us
  transfers between devices with their start and end apart: 4 -> 37, of which waited for: 3 -> 18; matrix products, arithmetic and copies ran while one was open for 2% -> 16% of each run, Pallas kernels for 0% -> 0%
where the time goes in v1:
time: 135 us; the launch traced here: 134 us
  starting transfers between devices  51.8 us (38%)
  waiting for transfers between devices  38.4 us (28%)
  matrix products  21.6 us (16%)
  local copies, waits for them, and re-layouts  15.5 us (11%)
  other arithmetic  5.88 us (4%)
    ppermute x37, starting transfers between devices, swap(): return lax.ppermute(x, ('kv', 'wide'), pairs)  51.8 us
    ppermute x37, waiting for transfers between devices, swap(): return lax.ppermute(x, ('kv', 'wide'), pairs)  38.4 us
    dot_general x1, matrix products, staged_path(): mixed = jnp.dot(everyone, output_weight, preferred_element_type=f32)  8.86 us
    dot_general x1, matrix products, staged_path(): jnp.dot(gained, joint_projection_weight, preferred_element_type=f32)  8.09 us
    gather x2, local copies, waits for them, and re-layouts, staged_path(): everyone = jnp.take(piece, place, axis=0).reshape(batch, -1)  3.36 us
    unnamed x25, local copies, waits for them, and re-layouts  2.71 us
  transfers between devices with their start and end apart: 37, of which 18 were waited for; matrix products, arithmetic and copies ran while one was open for 16% of the time, Pallas kernels for 0%

profile of v1, /device:TPU:0, one launch (start us, length us, event | category | flops | bytes accessed | tf_op | source)
XLA Modules:
  0.0 134.0 jit_solution(7565951396395983828)
XLA Ops:
  4.6 8.1 %convolution_convert_fusion = bf16[48,1152]{1,0:T(8,128)(2,1)S(1)} fusion(bf16[48,8192]{1,0:T(8,128)(2,1)S(1)} %reshape.346, bf16[8192,1152]{1,0:T(8,128)(2,1)} %param.16), kind=kOutput, calls=%fused_computation.1 | convolution fusion | flops 906024960 | bytes 19771392 | tf_op jit(solution)/shard_map/dot_general | solution.py:268
  14.2 4.9 %collective-permute-start.13 = (bf16[24,1152]{1,0:T(8,128)(2,1)S(1)}, bf16[24,1152]{1,0:T(8,128)(2,1)S(1)}, u32[]{:S(2)}, u32[]{:S(2)}) collective-permute-start(bf16[24,1152]{1,0:T(8,128)(2,1)S(1)} %get-tuple-element.39), channel_id=1, source_target_pairs={{0,2},{1,3},{2,0},{3,1},{4,6},{5,7},{6,4},{7,5},{24,26},{25,27},{2... | collective-permute-start | bytes 165896 | tf_op jit(solution)/shard_map/ppermute | solution.py:209
  21.2 3.0 %collective-permute-start.3 = (f32[48,25]{0,1:T(8,128)S(1)}, f32[48,25]{0,1:T(8,128)S(1)}, u32[]{:S(2)}, u32[]{:S(2)}) collective-permute-start(f32[48,25]{0,1:T(8,128)S(1)} %fusion.110), channel_id=1, source_target_pairs={{0,8},{1,9},{2,10},{3,11},{4,12},{5,13},{6,14},{7,15},{8,0},{9,1},... | collective-permute-start | bytes 14408 | tf_op jit(solution)/shard_map/ppermute | solution.py:209
  25.9 3.8 %collective-permute-done.4 = f32[48,25]{0,1:T(8,128)S(1)} collective-permute-done((f32[48,25]{0,1:T(8,128)S(1)}, f32[48,25]{0,1:T(8,128)S(1)}, u32[]{:S(2)}, u32[]{:S(2)}) %collective-permute-start.4) | collective-permute-done | bytes 4832 | tf_op jit(solution)/shard_map/ppermute | solution.py:209
  33.5 2.1 %collective-permute-done.7 = f32[48,25]{0,1:T(8,128)S(1)} collective-permute-done((f32[48,25]{0,1:T(8,128)S(1)}, f32[48,25]{0,1:T(8,128)S(1)}, u32[]{:S(2)}, u32[]{:S(2)}) %collective-permute-start.7) | collective-permute-done | bytes 4832 | tf_op jit(solution)/shard_map/ppermute | solution.py:209
  37.2 1.9 %collective-permute-start.9 = (bf16[2,16,1152]{2,1,0:T(8,128)(2,1)S(1)}, bf16[2,16,1152]{2,1,0:T(8,128)(2,1)S(1)}, u32[]{:S(2)}, u32[]{:S(2)}) collective-permute-start(bf16[2,16,1152]{2,1,0:T(8,128)(2,1)S(1)} %get-tuple-element.35), channel_id=1, source_target_pairs={{0,4},{1,5},{2,6},{3,7},{4,0},{5,1},{6,2},{7,3},{24,28},{25,29},{2... | collective-permute-start | bytes 221192 | tf_op jit(solution)/shard_map/ppermute | solution.py:209
  40.5 3.6 %collective-permute-done.11 = bf16[2,16,1152]{2,1,0:T(8,128)(2,1)S(1)} collective-permute-done((bf16[2,16,1152]{2,1,0:T(8,128)(2,1)S(1)}, bf16[2,16,1152]{2,1,0:T(8,128)(2,1)S(1)}, u32[]{:S(2)}, u32[]{:S(2)}) %collective-permute-start.11) | collective-permute-done | bytes 73760 | tf_op jit(solution)/shard_map/ppermute | solution.py:209
  46.4 3.2 %collective-permute-start.12 = (bf16[4,2,16,1152]{3,2,1,0:T(8,128)(2,1)S(1)}, bf16[4,2,16,1152]{3,2,1,0:T(8,128)(2,1)S(1)}, u32[]{:S(2)}, u32[]{:S(2)}) collective-permute-start(bf16[4,2,16,1152]{3,2,1,0:T(8,128)(2,1)S(1)} %pad_maximum_fusion), channel_id=1, source_target_pairs={{0,2},{1,3},{2,0},{3,1},{4,6},{5,7},{6,4},{7,5},{24,26},{25,27},{2... | collective-permute-start | bytes 884744 | tf_op jit(solution)/shard_map/ppermute | solution.py:209
  49.6 8.1 %collective-permute-done.12 = bf16[4,2,16,1152]{3,2,1,0:T(8,128)(2,1)S(1)} collective-permute-done((bf16[4,2,16,1152]{3,2,1,0:T(8,128)(2,1)S(1)}, bf16[4,2,16,1152]{3,2,1,0:T(8,128)(2,1)S(1)}, u32[]{:S(2)}, u32[]{:S(2)}) %collective-permute-start.12) | collective-permute-done | bytes 294944 | tf_op jit(solution)/shard_map/ppermute | solution.py:209
  59.4 3.8 %collective-permute-start.16 = (bf16[2,9,6,128]{3,1,2,0:T(8,128)(2,1)S(1)}, bf16[2,9,6,128]{3,1,2,0:T(8,128)(2,1)S(1)}, u32[]{:S(2)}, u32[]{:S(2)}) collective-permute-start(bf16[2,9,6,128]{3,1,2,0:T(8,128)(2,1)S(1)} %get-tuple-element.31), channel_id=1, source_target_pairs={{0,4},{1,5},{2,6},{3,7},{4,0},{5,1},{6,2},{7,3},{24,28},{25,29},{2... | collective-permute-start | bytes 82952 | tf_op jit(solution)/shard_map/ppermute | solution.py:209
  71.1 1.9 %collective-permute-start.19 = (bf16[1,3,8192]{2,1,0:T(4,128)(2,1)S(1)}, bf16[1,3,8192]{2,1,0:T(4,128)(2,1)S(1)}, u32[]{:S(2)}, u32[]{:S(2)}) collective-permute-start(bf16[1,3,8192]{2,1,0:T(4,128)(2,1)S(1)} %broadcast_in_dim_reshape.7), channel_id=1, source_target_pairs={{0,4},{1,5},{2,6},{3,7},{4,0},{5,1},{6,2},{7,3},{8,12},{9,13},{10,... | collective-permute-start | bytes 147464 | tf_op jit(solution)/shard_map/ppermute | solution.py:209
  73.0 3.4 %collective-permute-start.20 = (bf16[1,3,8192]{2,1,0:T(4,128)(2,1)S(1)}, bf16[1,3,8192]{2,1,0:T(4,128)(2,1)S(1)}, u32[]{:S(2)}, u32[]{:S(2)}) collective-permute-start(bf16[1,3,8192]{2,1,0:T(4,128)(2,1)S(1)} %broadcast_in_dim_reshape.7), channel_id=1, source_target_pairs={{0,8},{1,9},{2,10},{3,11},{4,12},{5,13},{6,14},{7,15},{8,0},{9,1},... | collective-permute-start | bytes 147464 | tf_op jit(solution)/shard_map/ppermute | solution.py:209
  77.0 3.4 %collective-permute-done.20 = bf16[1,3,8192]{2,1,0:T(4,128)(2,1)S(1)} collective-permute-done((bf16[1,3,8192]{2,1,0:T(4,128)(2,1)S(1)}, bf16[1,3,8192]{2,1,0:T(4,128)(2,1)S(1)}, u32[]{:S(2)}, u32[]{:S(2)}) %collective-permute-start.20) | collective-permute-done | bytes 49184 | tf_op jit(solution)/shard_map/ppermute | solution.py:209
  80.4 2.1 %collective-permute-done.21 = bf16[1,3,8192]{2,1,0:T(4,128)(2,1)S(1)} collective-permute-done((bf16[1,3,8192]{2,1,0:T(4,128)(2,1)S(1)}, bf16[1,3,8192]{2,1,0:T(4,128)(2,1)S(1)}, u32[]{:S(2)}, u32[]{:S(2)}) %collective-permute-start.21) | collective-permute-done | bytes 49184 | tf_op jit(solution)/shard_map/ppermute | solution.py:209
  86.0 3.4 %collective-permute-done.22 = bf16[4,3,8192]{2,1,0:T(4,128)(2,1)S(1)} collective-permute-done((bf16[4,3,8192]{2,1,0:T(4,128)(2,1)S(1)}, bf16[4,3,8192]{2,1,0:T(4,128)(2,1)S(1)}, u32[]{:S(2)}, u32[]{:S(2)}) %collective-permute-start.22) | collective-permute-done | bytes 196640 | tf_op jit(solution)/shard_map/ppermute | solution.py:209
  93.3 1.7 %collective-permute-start.33 = (bf16[2,16,1024]{2,1,0:T(8,128)(2,1)S(1)}, bf16[2,16,1024]{2,1,0:T(8,128)(2,1)S(1)}, u32[]{:S(2)}, u32[]{:S(2)}) collective-permute-start(bf16[2,16,1024]{2,1,0:T(8,128)(2,1)S(1)} %get-tuple-element.20), channel_id=1, source_target_pairs={{0,4},{1,5},{2,6},{3,7},{4,0},{5,1},{6,2},{7,3},{8,12},{9,13},{10,... | collective-permute-start | bytes 196616 | tf_op jit(solution)/shard_map/ppermute | solution.py:209
  95.0 2.4 %collective-permute-done.35 = bf16[2,16,1024]{2,1,0:T(8,128)(2,1)S(1)} collective-permute-done((bf16[2,16,1024]{2,1,0:T(8,128)(2,1)S(1)}, bf16[2,16,1024]{2,1,0:T(8,128)(2,1)S(1)}, u32[]{:S(2)}, u32[]{:S(2)}) %collective-permute-start.35) | collective-permute-done | bytes 65568 | tf_op jit(solution)/shard_map/ppermute | solution.py:209
  97.5 2.5 %collective-permute-done.34 = bf16[2,16,1024]{2,1,0:T(8,128)(2,1)S(1)} collective-permute-done((bf16[2,16,1024]{2,1,0:T(8,128)(2,1)S(1)}, bf16[2,16,1024]{2,1,0:T(8,128)(2,1)S(1)}, u32[]{:S(2)}, u32[]{:S(2)}) %collective-permute-start.34) | collective-permute-done | bytes 65568 | tf_op jit(solution)/shard_map/ppermute | solution.py:209
  101.8 2.7 %gather_fusion = bf16[16,3,8192]{2,1,0:T(4,128)(2,1)S(1)} fusion(bf16[16,3,8192]{2,1,0:T(4,128)(2,1)} %constant_dynamic-update-slice_fusion.7, s32[1024]{0:T(1024)S(1)} %pad_clamp_fusion), kind=kCustom, calls=%fused_computation | custom fusion | bytes 1572928 | tf_op jit(solution)/shard_map/jit(_take)/gather | solution.py:351
  106.0 1.7 %select_n.239 = bf16[48,8192]{1,0:T(8,128)(2,1)S(1)} reshape(bf16[16,3,8192]{2,1,0:T(4,128)(2,1)} %broadcast_select_fusion) | data formatting | bytes 1572864 | tf_op jit(solution)/shard_map/jit(_take)/select_n | solution.py:351
  112.3 2.0 %collective-permute-start.28 = (f32[48,8]{0,1:T(8,128)S(1)}, f32[48,8]{0,1:T(8,128)S(1)}, u32[]{:S(2)}, u32[]{:S(2)}) collective-permute-start(f32[48,8]{0,1:T(8,128)S(1)} %add.247), channel_id=1, source_target_pairs={{0,12},{1,13},{2,14},{3,15},{4,8},{5,9},{6,10},{7,11},{8,4},{9,5},... | collective-permute-start | bytes 4616 | tf_op jit(solution)/shard_map/ppermute | solution.py:209
  115.3 8.9 %fusion.4 = f32[48,1024]{1,0:T(8,128)S(1)} fusion(bf16[8192,1024]{1,0:T(8,128)(2,1)} %param.17, bf16[48,8192]{1,0:T(8,128)(2,1)S(1)} %gather.7, pred[48]{0:T(512)(128)(4,1)S(1)} %broadcast_in_dim.127), kind=kOutput, calls=%fused_computation.13 | convolution fusion | flops 805699584 | bytes 17760304 | tf_op jit(solution)/shard_map/dot_general | solution.py:355
  124.2 2.5 %collective-permute-start.30 = (f32[48,8]{0,1:T(8,128)S(1)}, f32[48,8]{0,1:T(8,128)S(1)}, u32[]{:S(2)}, u32[]{:S(2)}) collective-permute-start(f32[48,8]{0,1:T(8,128)S(1)} %add_add_fusion.3), channel_id=1, source_target_pairs={{0,16},{1,17},{2,18},{3,19},{4,20},{5,21},{6,22},{7,23},{8,24},{9,... | collective-permute-start | bytes 4616 | tf_op jit(solution)/shard_map/ppermute | solution.py:209
  128.2 1.9 %collective-permute-start.24 = (bf16[24,1024]{1,0:T(8,128)(2,1)S(1)}, bf16[24,1024]{1,0:T(8,128)(2,1)S(1)}, u32[]{:S(2)}, u32[]{:S(2)}) collective-permute-start(bf16[24,1024]{1,0:T(8,128)(2,1)S(1)} %dynamic-slice_convert_fusion), channel_id=1, source_target_pairs={{0,16},{1,17},{2,18},{3,19},{4,20},{5,21},{6,22},{7,23},{8,24},{9,... | collective-permute-start | bytes 147464 | tf_op jit(solution)/shard_map/ppermute | solution.py:209
  (177 shorter events, 50.2 us)
Async XLA Ops:
  12.7 46.4 %collective-permute-start.14 = (bf16[24,1152]{1,0:T(8,128)(2,1)S(1)}, bf16[24,1152]{1,0:T(8,128)(2,1)S(1)}, u32[]{:S(2)}, u32[]{:S(2)}) collective-permute-start(bf16[24,1152]{1,0:T(8,128)(2,1)S(1)} %get-tuple-element.39), channel_id=1, source_target_pairs={{8,26},{9,27},{10,24},{11,25},{12,30},{13,31},{14,28},{15,29},{16,... | collective-permute-start | bytes 165896 | tf_op jit(solution)/shard_map/ppermute | solution.py:209
  14.2 45.0 %collective-permute-start.13 = (bf16[24,1152]{1,0:T(8,128)(2,1)S(1)}, bf16[24,1152]{1,0:T(8,128)(2,1)S(1)}, u32[]{:S(2)}, u32[]{:S(2)}) collective-permute-start(bf16[24,1152]{1,0:T(8,128)(2,1)S(1)} %get-tuple-element.39), channel_id=1, source_target_pairs={{0,2},{1,3},{2,0},{3,1},{4,6},{5,7},{6,4},{7,5},{24,26},{25,27},{2... | collective-permute-start | bytes 165896 | tf_op jit(solution)/shard_map/ppermute | solution.py:209
  21.2 4.7 %collective-permute-start.3 = (f32[48,25]{0,1:T(8,128)S(1)}, f32[48,25]{0,1:T(8,128)S(1)}, u32[]{:S(2)}, u32[]{:S(2)}) collective-permute-start(f32[48,25]{0,1:T(8,128)S(1)} %fusion.110), channel_id=1, source_target_pairs={{0,8},{1,9},{2,10},{3,11},{4,12},{5,13},{6,14},{7,15},{8,0},{9,1},... | collective-permute-start | bytes 14408 | tf_op jit(solution)/shard_map/ppermute | solution.py:209
  24.1 5.5 %collective-permute-start.4 = (f32[48,25]{0,1:T(8,128)S(1)}, f32[48,25]{0,1:T(8,128)S(1)}, u32[]{:S(2)}, u32[]{:S(2)}) collective-permute-start(f32[48,25]{0,1:T(8,128)S(1)} %fusion.110), channel_id=1, source_target_pairs={{0,12},{1,13},{2,14},{3,15},{4,8},{5,9},{6,10},{7,11},{8,4},{9,5},... | collective-permute-start | bytes 14408 | tf_op jit(solution)/shard_map/ppermute | solution.py:209
  35.9 8.2 %collective-permute-start.11 = (bf16[2,16,1152]{2,1,0:T(8,128)(2,1)S(1)}, bf16[2,16,1152]{2,1,0:T(8,128)(2,1)S(1)}, u32[]{:S(2)}, u32[]{:S(2)}) collective-permute-start(bf16[2,16,1152]{2,1,0:T(8,128)(2,1)S(1)} %get-tuple-element.35), channel_id=1, source_target_pairs={{8,4},{9,5},{10,6},{11,7},{12,0},{13,1},{14,2},{15,3},{16,28},{17,... | collective-permute-start | bytes 221192 | tf_op jit(solution)/shard_map/ppermute | solution.py:209
  37.2 9.2 %collective-permute-start.9 = (bf16[2,16,1152]{2,1,0:T(8,128)(2,1)S(1)}, bf16[2,16,1152]{2,1,0:T(8,128)(2,1)S(1)}, u32[]{:S(2)}, u32[]{:S(2)}) collective-permute-start(bf16[2,16,1152]{2,1,0:T(8,128)(2,1)S(1)} %get-tuple-element.35), channel_id=1, source_target_pairs={{0,4},{1,5},{2,6},{3,7},{4,0},{5,1},{6,2},{7,3},{24,28},{25,29},{2... | collective-permute-start | bytes 221192 | tf_op jit(solution)/shard_map/ppermute | solution.py:209
  39.1 7.2 %collective-permute-start.10 = (bf16[2,16,1152]{2,1,0:T(8,128)(2,1)S(1)}, bf16[2,16,1152]{2,1,0:T(8,128)(2,1)S(1)}, u32[]{:S(2)}, u32[]{:S(2)}) collective-permute-start(bf16[2,16,1152]{2,1,0:T(8,128)(2,1)S(1)} %bitcast.149), channel_id=1, source_target_pairs={{8,0},{9,1},{10,2},{11,3},{12,4},{13,5},{14,6},{15,7},{16,24},{17,... | collective-permute-start | bytes 221192 | tf_op jit(solution)/shard_map/ppermute | solution.py:209
  44.0 15.1 %collective-permute-start = (bf16[24,1152]{1,0:T(8,128)(2,1)S(1)}, bf16[24,1152]{1,0:T(8,128)(2,1)S(1)}, u32[]{:S(2)}, u32[]{:S(2)}) collective-permute-start(bf16[24,1152]{1,0:T(8,128)(2,1)S(1)} %get-tuple-element.38), channel_id=1, source_target_pairs={{8,24},{9,25},{10,26},{11,27},{12,28},{13,29},{14,30},{15,31},{16,... | collective-permute-start | bytes 165896 | tf_op jit(solution)/shard_map/ppermute | solution.py:209
  46.3 44.2 %collective-permute-start.32 = (bf16[4,2,8,1024]{3,2,1,0:T(8,128)(2,1)S(1)}, bf16[4,2,8,1024]{3,2,1,0:T(8,128)(2,1)S(1)}, u32[]{:S(2)}, u32[]{:S(2)}) collective-permute-start(bf16[4,2,8,1024]{3,2,1,0:T(8,128)(2,1)S(1)} %get-tuple-element.23), channel_id=1, source_target_pairs={{0,1},{1,0},{2,3},{3,2},{4,5},{5,4},{6,7},{7,6},{8,9},{9,8},{10,11... | collective-permute-start | bytes 393224 | tf_op jit(solution)/shard_map/ppermute | solution.py:209
  46.4 11.3 %collective-permute-start.12 = (bf16[4,2,16,1152]{3,2,1,0:T(8,128)(2,1)S(1)}, bf16[4,2,16,1152]{3,2,1,0:T(8,128)(2,1)S(1)}, u32[]{:S(2)}, u32[]{:S(2)}) collective-permute-start(bf16[4,2,16,1152]{3,2,1,0:T(8,128)(2,1)S(1)} %pad_maximum_fusion), channel_id=1, source_target_pairs={{0,2},{1,3},{2,0},{3,1},{4,6},{5,7},{6,4},{7,5},{24,26},{25,27},{2... | collective-permute-start | bytes 884744 | tf_op jit(solution)/shard_map/ppermute | solution.py:209
  59.4 6.6 %collective-permute-start.16 = (bf16[2,9,6,128]{3,1,2,0:T(8,128)(2,1)S(1)}, bf16[2,9,6,128]{3,1,2,0:T(8,128)(2,1)S(1)}, u32[]{:S(2)}, u32[]{:S(2)}) collective-permute-start(bf16[2,9,6,128]{3,1,2,0:T(8,128)(2,1)S(1)} %get-tuple-element.31), channel_id=1, source_target_pairs={{0,4},{1,5},{2,6},{3,7},{4,0},{5,1},{6,2},{7,3},{24,28},{25,29},{2... | collective-permute-start | bytes 82952 | tf_op jit(solution)/shard_map/ppermute | solution.py:209
  71.1 5.9 %collective-permute-start.19 = (bf16[1,3,8192]{2,1,0:T(4,128)(2,1)S(1)}, bf16[1,3,8192]{2,1,0:T(4,128)(2,1)S(1)}, u32[]{:S(2)}, u32[]{:S(2)}) collective-permute-start(bf16[1,3,8192]{2,1,0:T(4,128)(2,1)S(1)} %broadcast_in_dim_reshape.7), channel_id=1, source_target_pairs={{0,4},{1,5},{2,6},{3,7},{4,0},{5,1},{6,2},{7,3},{8,12},{9,13},{10,... | collective-permute-start | bytes 147464 | tf_op jit(solution)/shard_map/ppermute | solution.py:209
  73.0 7.4 %collective-permute-start.20 = (bf16[1,3,8192]{2,1,0:T(4,128)(2,1)S(1)}, bf16[1,3,8192]{2,1,0:T(4,128)(2,1)S(1)}, u32[]{:S(2)}, u32[]{:S(2)}) collective-permute-start(bf16[1,3,8192]{2,1,0:T(4,128)(2,1)S(1)} %broadcast_in_dim_reshape.7), channel_id=1, source_target_pairs={{0,8},{1,9},{2,10},{3,11},{4,12},{5,13},{6,14},{7,15},{8,0},{9,1},... | collective-permute-start | bytes 147464 | tf_op jit(solution)/shard_map/ppermute | solution.py:209
  76.3 6.2 %collective-permute-start.21 = (bf16[1,3,8192]{2,1,0:T(4,128)(2,1)S(1)}, bf16[1,3,8192]{2,1,0:T(4,128)(2,1)S(1)}, u32[]{:S(2)}, u32[]{:S(2)}) collective-permute-start(bf16[1,3,8192]{2,1,0:T(4,128)(2,1)S(1)} %broadcast_in_dim_reshape.7), channel_id=1, source_target_pairs={{0,12},{1,13},{2,14},{3,15},{4,8},{5,9},{6,10},{7,11},{8,4},{9,5},... | collective-permute-start | bytes 147464 | tf_op jit(solution)/shard_map/ppermute | solution.py:209
  82.7 6.7 %collective-permute-start.22 = (bf16[4,3,8192]{2,1,0:T(4,128)(2,1)S(1)}, bf16[4,3,8192]{2,1,0:T(4,128)(2,1)S(1)}, u32[]{:S(2)}, u32[]{:S(2)}) collective-permute-start(bf16[4,3,8192]{2,1,0:T(4,128)(2,1)S(1)} %pad_maximum_fusion.1), channel_id=1, source_target_pairs={{0,2},{1,3},{2,0},{3,1},{4,6},{5,7},{6,4},{7,5},{8,10},{9,11},{10,... | collective-permute-start | bytes 589832 | tf_op jit(solution)/shard_map/ppermute | solution.py:209
  90.3 10.4 %collective-permute-start.23 = (bf16[8,3,8192]{2,1,0:T(4,128)(2,1)S(1)}, bf16[8,3,8192]{2,1,0:T(4,128)(2,1)S(1)}, u32[]{:S(2)}, u32[]{:S(2)}) collective-permute-start(bf16[8,3,8192]{2,1,0:T(4,128)(2,1)S(1)} %get-tuple-element.25), channel_id=1, source_target_pairs={{0,1},{1,0},{2,3},{3,2},{4,5},{5,4},{6,7},{7,6},{8,9},{9,8},{10,11... | collective-permute-start | bytes 1179656 | tf_op jit(solution)/shard_map/ppermute | solution.py:209
  90.6 6.9 %collective-permute-start.35 = (bf16[2,16,1024]{2,1,0:T(8,128)(2,1)S(1)}, bf16[2,16,1024]{2,1,0:T(8,128)(2,1)S(1)}, u32[]{:S(2)}, u32[]{:S(2)}) collective-permute-start(bf16[2,16,1024]{2,1,0:T(8,128)(2,1)S(1)} %get-tuple-element.22), channel_id=1, source_target_pairs={{0,12},{1,13},{2,14},{3,15},{4,8},{5,9},{6,10},{7,11},{8,4},{9,5},... | collective-permute-start | bytes 196616 | tf_op jit(solution)/shard_map/ppermute | solution.py:209
  92.3 7.7 %collective-permute-start.34 = (bf16[2,16,1024]{2,1,0:T(8,128)(2,1)S(1)}, bf16[2,16,1024]{2,1,0:T(8,128)(2,1)S(1)}, u32[]{:S(2)}, u32[]{:S(2)}) collective-permute-start(bf16[2,16,1024]{2,1,0:T(8,128)(2,1)S(1)} %get-tuple-element.21), channel_id=1, source_target_pairs={{0,8},{1,9},{2,10},{3,11},{4,12},{5,13},{6,14},{7,15},{8,0},{9,1},... | collective-permute-start | bytes 196616 | tf_op jit(solution)/shard_map/ppermute | solution.py:209
  93.3 6.7 %collective-permute-start.33 = (bf16[2,16,1024]{2,1,0:T(8,128)(2,1)S(1)}, bf16[2,16,1024]{2,1,0:T(8,128)(2,1)S(1)}, u32[]{:S(2)}, u32[]{:S(2)}) collective-permute-start(bf16[2,16,1024]{2,1,0:T(8,128)(2,1)S(1)} %get-tuple-element.20), channel_id=1, source_target_pairs={{0,4},{1,5},{2,6},{3,7},{4,0},{5,1},{6,2},{7,3},{8,12},{9,13},{10,... | collective-permute-start | bytes 196616 | tf_op jit(solution)/shard_map/ppermute | solution.py:209
  109.8 21.5 %collective-permute-start.36 = (bf16[4,16,1024]{2,1,0:T(8,128)(2,1)}, bf16[4,16,1024]{2,1,0:T(8,128)(2,1)}, u32[]{:S(2)}, u32[]{:S(2)}) collective-permute-start(bf16[4,16,1024]{2,1,0:T(8,128)(2,1)} %get-tuple-element.18), channel_id=1, source_target_pairs={{0,2},{1,3},{2,0},{3,1},{4,6},{5,7},{6,4},{7,5},{8,10},{9,11},{10,... | collective-permute-start | bytes 393224 | tf_op jit(solution)/shard_map/ppermute | solution.py:209
  111.7 12.4 %collective-permute-start.27 = (f32[48,8]{0,1:T(8,128)S(1)}, f32[48,8]{0,1:T(8,128)S(1)}, u32[]{:S(2)}, u32[]{:S(2)}) collective-permute-start(f32[48,8]{0,1:T(8,128)S(1)} %add.247), channel_id=1, source_target_pairs={{0,8},{1,9},{2,10},{3,11},{4,12},{5,13},{6,14},{7,15},{8,0},{9,1},... | collective-permute-start | bytes 4616 | tf_op jit(solution)/shard_map/ppermute | solution.py:209
  112.3 11.8 %collective-permute-start.28 = (f32[48,8]{0,1:T(8,128)S(1)}, f32[48,8]{0,1:T(8,128)S(1)}, u32[]{:S(2)}, u32[]{:S(2)}) collective-permute-start(f32[48,8]{0,1:T(8,128)S(1)} %add.247), channel_id=1, source_target_pairs={{0,12},{1,13},{2,14},{3,15},{4,8},{5,9},{6,10},{7,11},{8,4},{9,5},... | collective-permute-start | bytes 4616 | tf_op jit(solution)/shard_map/ppermute | solution.py:209
  114.3 9.8 %collective-permute-start.26 = (f32[48,8]{0,1:T(8,128)S(1)}, f32[48,8]{0,1:T(8,128)S(1)}, u32[]{:S(2)}, u32[]{:S(2)}) collective-permute-start(f32[48,8]{0,1:T(8,128)S(1)} %add.247), channel_id=1, source_target_pairs={{0,4},{1,5},{2,6},{3,7},{4,0},{5,1},{6,2},{7,3},{8,12},{9,13},{10,... | collective-permute-start | bytes 4616 | tf_op jit(solution)/shard_map/ppermute | solution.py:209
  124.2 6.0 %collective-permute-start.30 = (f32[48,8]{0,1:T(8,128)S(1)}, f32[48,8]{0,1:T(8,128)S(1)}, u32[]{:S(2)}, u32[]{:S(2)}) collective-permute-start(f32[48,8]{0,1:T(8,128)S(1)} %add_add_fusion.3), channel_id=1, source_target_pairs={{0,16},{1,17},{2,18},{3,19},{4,20},{5,21},{6,22},{7,23},{8,24},{9,... | collective-permute-start | bytes 4616 | tf_op jit(solution)/shard_map/ppermute | solution.py:209
  (23 other events, 222.6 us)

commit v2 on v0

--- a/solution.py
+++ b/solution.py
@@ -1,6 +1,8 @@
 import jax
 import jax.numpy as jnp
 from jax import lax
+from jax.experimental import pallas as pl
+from jax.experimental.pallas import tpu as pltpu
 from jax.sharding import PartitionSpec as P
 
 MODEL_WIDTH = 16384
@@ -37,7 +39,7 @@
     return joined.reshape(count, -1)
 
 
-def on_device(
+def general_path(
     hidden_input,
     input_norm_gain,
     joint_projection_weight,
@@ -163,6 +165,520 @@
     return (output_baseline + adapter_scale * output_change.T).astype(jnp.bfloat16)
 
 
+WHOLE = pl.BlockSpec(memory_space=pltpu.VMEM)
+SCALARS = pl.BlockSpec(memory_space=pltpu.SMEM)
+
+
+def prepare(place, hidden_input, gain, owned, swapped, adapters, owners, cols):
+    count, width = hidden_input.shape
+    entries = owned[0].shape[0]
+    rank, heads_width = owned[1].shape
+    head_dim = 128
+    lanes = 128
+    heads = owned[2].shape[2] // head_dim
+    group_width = heads_width // heads
+    each = count // 3
+    chunk = 1024
+    held = (hidden_input, gain, *owned, *swapped)
+
+    def kernel(place_ref, owner_ref, index_ref, *refs):
+        inputs, outputs = refs[: len(held)], refs[len(held) : len(held) + 5]
+        buffers, sem = refs[len(held) + 5 : -1], refs[-1]
+        same_ref, flip_ref, small_ref, slot_ref, mine_ref = outputs
+        copies = [
+            pltpu.make_async_copy(src, dst, sem.at[i])
+            for i, (src, dst) in enumerate(zip(inputs, buffers))
+        ]
+        for copy in copies:
+            copy.start()
+        x_ref, gain_ref = buffers[:2]
+        down_refs, q_refs, kv_refs = buffers[2::3], buffers[3::3], buffers[4::3]
+
+        row = lax.broadcasted_iota(jnp.int32, (count, count), 0)
+        column = lax.broadcasted_iota(jnp.int32, (count, count), 1)
+        across = jnp.where(row == column, index_ref[...].astype(jnp.float32), 0.0)
+        index = jnp.sum(across, axis=1, keepdims=True).astype(jnp.int32)
+        slot = jnp.zeros((count, 1), jnp.int32)
+        for a in range(owners.shape[0]):
+            slot = jnp.where(index == a, owner_ref[a], slot)
+        slot_ref[...] = slot
+        mine = [(slot == (place_ref[1] ^ dcore)).astype(jnp.float32) for dcore in range(2)]
+        for dcore in range(2):
+            mine_ref[:, dcore : dcore + 1] = mine[dcore]
+
+        for copy in copies:
+            copy.wait()
+        total = jnp.zeros((count, 1), jnp.float32)
+        reduced = [jnp.zeros((count, entries), jnp.float32) for _ in range(2)]
+        for at in range(0, width, chunk):
+            part = slice(at, at + chunk)
+            x = x_ref[:, part].astype(jnp.float32)
+            total = total + jnp.sum(x * x, axis=1, keepdims=True)
+            gained = (x * gain_ref[:, part]).astype(jnp.bfloat16)
+            for dcore in range(2):
+                reduced[dcore] = reduced[dcore] + lax.dot_general(
+                    gained, down_refs[dcore][:, part], (((1,), (1,)), ((), ())),
+                    preferred_element_type=jnp.float32,
+                )
+        small_ref[...] = jnp.zeros_like(small_ref)
+        small_ref[:, :entries] = reduced[0] * mine[0] + reduced[1] * mine[1]
+        small_ref[:, entries : entries + 1] = total * (mine[0] + mine[1])
+        small = small_ref[...]
+
+        for ref in (same_ref, flip_ref):
+            ref[:, cols:] = jnp.zeros((4 * rank, 3 * lanes), ref.dtype)
+            for g in range(3):
+                code_three(ref, slice(0, each), cols + g * lanes, small[g * each : (g + 1) * each])
+
+        def write(core, zb, ref):
+            for yb in range(2):
+                h = zb * 2 + yb
+                rows = slice(yb * 2 * rank, (yb + 1) * 2 * rank)
+                at = h * group_width
+                spans = [(at, at + cols), (at + cols, at + group_width)][core]
+                joined = jnp.concatenate([q[:, spans[0] : spans[1]] for q in q_refs], axis=0)
+                rest = spans[1] - spans[0]
+                ref[rows, :rest] = joined
+                if core == 1:
+                    for t in range(2):
+                        part = slice(h * head_dim, (h + 1) * head_dim)
+                        ref[rows, rest + t * head_dim : rest + (t + 1) * head_dim] = (
+                            jnp.concatenate([kv[t, :, part] for kv in kv_refs], axis=0)
+                        )
+
+        for core in range(2):
+            for low in range(2):
+
+                @pl.when((place_ref[0] == core) & ((place_ref[2] & 1) == low))
+                def _():
+                    write(core, low, same_ref)
+                    write(core, 1 - low, flip_ref)
+
+    message = jax.ShapeDtypeStruct((4 * rank, cols + 3 * lanes), owned[1].dtype)
+    return pl.pallas_call(
+        kernel,
+        in_specs=[SCALARS, SCALARS, WHOLE] + [pl.BlockSpec(memory_space=pl.ANY)] * len(held),
+        out_specs=[WHOLE] * 5,
+        out_shape=[
+            message,
+            message,
+            jax.ShapeDtypeStruct((count, 32), jnp.float32),
+            jax.ShapeDtypeStruct((count, 1), jnp.int32),
+            jax.ShapeDtypeStruct((count, 2), jnp.float32),
+        ],
+        scratch_shapes=[pltpu.VMEM(v.shape, v.dtype) for v in held]
+        + [pltpu.SemaphoreType.DMA((len(held),))],
+        compiler_params=pltpu.CompilerParams(vmem_limit_bytes=60 * 2**20),
+    )(place, owners, adapters, *held)
+
+
+def stream_product(rows_in, gain, weight, start, stop, before, marker):
+    count, cols = rows_in.shape[0], weight.shape[1]
+    chunk = 512
+    steps = (stop - start) // chunk
+    held = pl.BlockSpec(memory_space=pl.ANY)
+    operands, specs = [rows_in, weight, marker], [WHOLE, held, held]
+    for more in (gain, before):
+        if more is not None:
+            operands += [more]
+            specs += [WHOLE]
+
+    def kernel(*refs):
+        x_ref, w_ref = refs[:2]
+        out_ref, buf, sem = refs[-3:]
+
+        def fetch(i):
+            return pltpu.make_async_copy(
+                w_ref.at[pl.ds(start + i * chunk, chunk)], buf.at[i], sem.at[i]
+            )
+
+        for i in range(steps):
+            fetch(i).start()
+        if before is None:
+            out_ref[...] = jnp.zeros_like(out_ref)
+        else:
+            out_ref[...] = refs[len(operands) - 1][...]
+
+        def body(i, carry):
+            at = pl.multiple_of(start + i * chunk, chunk)
+            x = x_ref[:, pl.ds(at, chunk)]
+            if gain is not None:
+                x = (x.astype(jnp.float32) * refs[3][:, pl.ds(at, chunk)]).astype(jnp.bfloat16)
+            fetch(i).wait()
+            out_ref[...] += jnp.dot(x, buf[i], preferred_element_type=jnp.float32)
+            return carry
+
+        lax.fori_loop(0, steps, body, 0)
+
+    return pl.pallas_call(
+        kernel,
+        in_specs=specs,
+        out_specs=WHOLE,
+        out_shape=jax.ShapeDtypeStruct((count, cols), jnp.float32),
+        scratch_shapes=[
+            pltpu.VMEM((steps, chunk, cols), weight.dtype),
+            pltpu.SemaphoreType.DMA((steps,)),
+        ],
+        cost_estimate=pl.CostEstimate(
+            flops=2 * count * cols * (stop - start),
+            bytes_accessed=2 * cols * (stop - start),
+            transcendentals=0,
+        ),
+        compiler_params=pltpu.CompilerParams(vmem_limit_bytes=47 * 2**20),
+    )(*operands)
+
+
+def code_three(ref, rows, at, v):
+    width = v.shape[1]
+    for t in range(3):
+        top = v.astype(jnp.bfloat16)
+        ref[rows, at + t * width : at + (t + 1) * width] = top
+        v = v - top.astype(jnp.float32)
+
+
+def pack_y(place, parts, small, cols):
+    tall, wide_cols = parts[0].shape
+    count, entries = small.shape
+    lanes = 128
+    each = count // 3
+    rows = tall // 2
+
+    def kernel(place_ref, a_ref, b_ref, c_ref, d_ref, small_ref, away_ref, keep_ref, sum_ref):
+        total = small_ref[...]
+        for ref in (b_ref, c_ref, d_ref):
+            coded = jnp.concatenate(
+                [
+                    ref[:each, cols + g * lanes : cols + g * lanes + 3 * entries]
+                    for g in range(3)
+                ],
+                axis=0,
+            ).astype(jnp.float32)
+            total = total + (
+                (coded[:, :entries] + coded[:, entries : 2 * entries]) + coded[:, 2 * entries :]
+            )
+        sum_ref[...] = total
+
+        def write(yb):
+            for dz, ref in enumerate((a_ref, b_ref, c_ref, d_ref)):
+                keep_ref[dz] = ref[yb * rows : (yb + 1) * rows, :cols]
+                away_ref[dz * rows : (dz + 1) * rows, :cols] = ref[
+                    (1 - yb) * rows : (2 - yb) * rows, :cols
+                ]
+
+        @pl.when(place_ref[3] == 0)
+        def _():
+            write(0)
+
+        @pl.when(place_ref[3] == 1)
+        def _():
+            write(1)
+
+        away_ref[:, cols:] = jnp.zeros_like(away_ref[:, cols:])
+        code_three(away_ref, slice(0, count), cols, total)
+
+    dtype = parts[0].dtype
+    return pl.pallas_call(
+        kernel,
+        in_specs=[SCALARS] + [WHOLE] * 5,
+        out_specs=[WHOLE] * 3,
+        out_shape=[
+            jax.ShapeDtypeStruct((4 * rows, cols + lanes), dtype),
+            jax.ShapeDtypeStruct((4, rows, cols), dtype),
+            jax.ShapeDtypeStruct(small.shape, jnp.float32),
+        ],
+        compiler_params=pltpu.CompilerParams(vmem_limit_bytes=8 * 2**20),
+    )(place, *parts, small)
+
+
+def merge(place, partial, small, received, near, far, slot):
+    count, cols = partial.shape
+    lanes = 128
+    blocks = cols // lanes
+    each = count // 4
+    entries = 24
+    rank = entries // 3
+
+    def kernel(place_ref, p_ref, small_ref, r_ref, near_ref, far_ref, slot_ref, out_ref, acc_ref):
+        other = r_ref[:, cols : cols + 96].astype(jnp.float32)
+        small = small_ref[...] + ((other[:, :32] + other[:, 32:64]) + other[:, 64:96])
+        scale = lax.rsqrt(small[:, entries : entries + 1] / MODEL_WIDTH + 1e-05)
+        shrink = (small * scale).astype(jnp.bfloat16)
+        lane = lax.broadcasted_iota(jnp.int32, (count, lanes), 1)
+        owner = place_ref[1] ^ (((lane >> 4) & 3) * 4 + (lane >> 6) * 2 + ((lane >> 3) & 1))
+        hit = slot_ref[...] == owner
+        entry = lax.broadcasted_iota(jnp.int32, (32, lanes), 0)
+        to = lax.broadcasted_iota(jnp.int32, (32, lanes), 1) & (rank - 1)
+
+        def spread(t):
+            chosen = (entry == to + t * rank).astype(jnp.bfloat16)
+            value = jnp.dot(shrink, chosen, preferred_element_type=jnp.float32)
+            return jnp.where(hit, value, 0.0).astype(jnp.bfloat16)
+
+        last = place_ref[0] == 1
+        parts = [spread(t) for t in range(3)]
+        cut = cols - 2 * lanes
+        spans = ((0, cut, parts[0]), (cut, cut + lanes, parts[1]), (cut + lanes, cols, parts[2]))
+        for lo, hi, own in spans:
+            left = parts[0] if lo == 0 else jnp.where(last, own, parts[0])
+            up = jnp.concatenate(
+                [near_ref[dz, :, lo:hi] for dz in range(4)] + [far_ref[:, lo:hi]], axis=0
+            )
+            change = jnp.dot(left, up, preferred_element_type=jnp.float32)
+            base = p_ref[:, lo:hi] + r_ref[:, lo:hi].astype(jnp.float32)
+            acc_ref[:, lo:hi] = base * scale + adapter_scale * change
+        for a in range(4):
+            for b in range(blocks):
+                out_ref[a, b] = acc_ref[
+                    a * each : (a + 1) * each, b * lanes : (b + 1) * lanes
+                ].astype(out_ref.dtype)
+
+    return pl.pallas_call(
+        kernel,
+        in_specs=[SCALARS] + [WHOLE] * 6,
+        out_specs=WHOLE,
+        out_shape=jax.ShapeDtypeStruct((4, blocks, each, lanes), jnp.bfloat16),
+        scratch_shapes=[pltpu.VMEM((count, cols), jnp.float32)],
+        compiler_params=pltpu.CompilerParams(vmem_limit_bytes=12 * 2**20),
+    )(place, partial, small, received, near, far, slot)
+
+
+def in_order(groups, order, downs, mine):
+    pieces, tall, lanes = groups[0].shape
+    entries, depth = downs[0].shape
+    blocks = depth // lanes
+    count = 4 * pieces * (tall // blocks)
+
+    def kernel(
+        order_ref, a_ref, b_ref, c_ref, d_ref, near_ref, far_ref, mine_ref, rows_ref, small_ref,
+        wide_ref,
+    ):
+        for g, ref in enumerate((a_ref, b_ref, c_ref, d_ref)):
+            for p in range(pieces):
+                wide_ref[order_ref[g * pieces + p]] = ref[p].astype(jnp.float32)
+        flat = wide_ref.reshape(count * blocks, lanes)
+        for j in range(blocks):
+            rows_ref[:, j * lanes : (j + 1) * lanes] = flat[
+                pl.ds(j, count, stride=blocks), :
+            ].astype(rows_ref.dtype)
+        near, far = [
+            lax.dot_general(
+                rows_ref[...], ref[...], (((1,), (1,)), ((), ())),
+                preferred_element_type=jnp.float32,
+            )
+            for ref in (near_ref, far_ref)
+        ]
+        small_ref[...] = near * mine_ref[:, :1] + far * mine_ref[:, 1:]
+
+    return pl.pallas_call(
+        kernel,
+        in_specs=[SCALARS] + [WHOLE] * 7,
+        out_specs=[WHOLE, WHOLE],
+        out_shape=[
+            jax.ShapeDtypeStruct((count, depth), groups[0].dtype),
+            jax.ShapeDtypeStruct((count, entries), jnp.float32),
+        ],
+        scratch_shapes=[pltpu.VMEM((4 * pieces, tall, lanes), jnp.float32)],
+        cost_estimate=pl.CostEstimate(
+            flops=0, bytes_accessed=4 * count * depth, transcendentals=0
+        ),
+        compiler_params=pltpu.CompilerParams(vmem_limit_bytes=10 * 2**20),
+    )(order, *groups, *downs, mine)
+
+
+def in_three(v):
+    out = []
+    for _ in range(3):
+        top = lax.reduce_precision(v, 8, 7)
+        out.append(top.astype(jnp.bfloat16))
+        v = v - top
+    return jnp.concatenate(out, axis=1)
+
+
+def from_three(v):
+    n = v.shape[1] // 3
+    v = v.astype(jnp.float32)
+    return (v[:, :n] + v[:, n : 2 * n]) + v[:, 2 * n :]
+
+
+def staged_path(
+    hidden_input,
+    input_norm_gain,
+    joint_projection_weight,
+    output_weight,
+    key_cache,
+    value_cache,
+    joint_down_weight,
+    query_up_weight,
+    key_value_up_weight,
+    output_down_weight,
+    output_up_weight,
+    row_adapter_index,
+    adapter_owner_slot,
+    lengths,
+):
+    f32, bf16 = jnp.float32, jnp.bfloat16
+    batch = hidden_input.shape[0]
+    rows = lengths.shape[0]
+    heads = key_cache.shape[1]
+    head_dim = key_cache.shape[3]
+    rank = query_up_weight.shape[1]
+    cols = joint_projection_weight.shape[1]
+    out_cols = output_weight.shape[1]
+    blocks = cols // head_dim
+    group = 2 * blocks - 2
+    wide = batch // rows
+    kv_pos = lax.axis_index("kv")
+    wide_pos = lax.axis_index("wide")
+    core = wide_pos & 1
+    y = (wide_pos >> 1) & 1
+    z = wide_pos >> 2
+    right = (z >> 1) == kv_pos
+
+    def is_right(i):
+        return ((i % wide) >> 3) == i // wide
+
+    def swap(x, mask, source=None, target=None):
+        pairs = [(i, i ^ mask) for i in range(2 * wide)]
+        if source is not None:
+            pairs = [p for p in pairs if is_right(p[0]) == source]
+        if target is not None:
+            pairs = [p for p in pairs if is_right(p[1]) == target]
+        return lax.ppermute(x, ("kv", "wide"), pairs)
+
+    def pick(x, i, axis=0):
+        return lax.dynamic_index_in_dim(x, i, axis, keepdims=False)
+
+    half = batch // 2
+    place = jnp.stack([core, wide_pos, z, y])
+
+    owned = (joint_down_weight[0].T, query_up_weight[0], key_value_up_weight[0])
+    gain = input_norm_gain[None]
+    same, flip, small, slot, mine = prepare(
+        place,
+        hidden_input,
+        gain,
+        owned,
+        tuple(swap(v, 1) for v in owned),
+        row_adapter_index[None],
+        adapter_owner_slot,
+        cols,
+    )
+    parts = [same, swap(flip, 4), swap(same, 8), swap(flip, 12)]
+    depth = hidden_input.shape[1]
+    cut = depth * 5 // 8
+    weight = joint_projection_weight
+    partial = stream_product(hidden_input, gain, weight, 0, cut, None, same)
+    away, ups, small = pack_y(place, parts, small, cols)
+    away, partial = lax.optimization_barrier((away, partial))
+    from_y = swap(away, 2)
+    partial = stream_product(hidden_input, gain, weight, cut, depth, partial, away)
+    small = small + from_three(from_y[:batch, cols : cols + 96])
+    message = jnp.concatenate([partial.astype(bf16), in_three(small)], axis=1)
+    from_x = swap(message, 16, target=True)
+    merged = merge(place, partial, small, from_x, ups, from_y, slot)
+
+    to = [pick(merged, z ^ d) for d in range(4)]
+    from_1 = swap(to[1], 4, source=True)
+    from_2 = swap(to[2], 8, source=True)
+    from_3 = swap(to[3], 12, source=True)
+    near = jnp.stack([jnp.where(right, to[0], from_2), jnp.where(right, from_1, from_3)])
+    keep = lax.dynamic_slice_in_dim(near, y * 2 * rows, 2 * rows, 2)
+    give = lax.dynamic_slice_in_dim(near, (1 - y) * 2 * rows, 2 * rows, 2)
+    from_y = swap(give, 2)
+    near = jnp.stack([jnp.where(y == 0, keep, from_y), jnp.where(y == 0, from_y, keep)], axis=1)
+    far = swap(near, 1)
+    parts = [jnp.where(core == 0, near, far), jnp.where(core == 0, far, near)]
+    parts = [
+        lax.dynamic_slice_in_dim(jnp.where((z & 1) == 0, p, p[::-1]), core * rows, rows, 3)
+        for p in parts
+    ]
+    joined = jnp.concatenate(parts, axis=2).astype(f32)
+    joined = joined.reshape(heads, 2 * blocks, rows, head_dim).transpose(2, 0, 1, 3)
+    query_vector = rotate(joined[:, :, :group], lengths).astype(bf16)
+    fresh_key = rotate(joined[:, :, group], lengths).astype(bf16)
+    value_new = joined[:, :, group + 1].astype(bf16)
+
+    inverse_root = jnp.sqrt(f32(head_dim))
+    scores = jnp.einsum("rkgd,rkld->rkgl", query_vector, key_cache, preferred_element_type=f32)
+    scores = scores / inverse_root
+    valid = jnp.arange(key_cache.shape[2], dtype=jnp.int32)[None, :] < lengths[:, None]
+    scores = jnp.where(valid[:, None, None, :], scores, -jnp.inf)
+    fresh_score = (
+        jnp.einsum("rkgd,rkd->rkg", query_vector, fresh_key, preferred_element_type=f32)
+        / inverse_root
+    )
+    top = jnp.maximum(jnp.max(scores, axis=-1), fresh_score)
+    expd = jnp.exp(scores - top[..., None])
+    exp_new = jnp.exp(fresh_score - top)
+    total = jnp.sum(expd, axis=-1) + exp_new
+    probs = (expd / total[..., None]).astype(bf16)
+    prob_new = (exp_new / total).astype(bf16)
+    attended = jnp.einsum("rkgl,rkld->rkgd", probs, value_cache, preferred_element_type=f32)
+    attended = (
+        attended + prob_new.astype(f32)[..., None] * value_new.astype(f32)[:, :, None, :]
+    )
+    attended = attended.astype(bf16).reshape(-1, head_dim)
+
+    near = jnp.stack([attended, swap(attended, 4), swap(attended, 8), swap(attended, 12)])
+    near_y = swap(near, 2)
+    far, far_y = swap(near, 1), swap(near_y, 1)
+    offsets = [
+        dz * 4 + dy * 2 + dcore for dcore in range(2) for dy in range(2) for dz in range(4)
+    ]
+    order = wide_pos ^ jnp.array(offsets, jnp.int32)
+    o_down = output_down_weight[0].T
+    everyone, o_reduced = in_order(
+        (near, near_y, far, far_y), order, (o_down, swap(o_down, 1)), mine
+    )
+
+    o_sheet = output_up_weight[0].reshape(rank, 4, 2, 2, out_cols).transpose(3, 1, 2, 0, 4)
+    o_pair = jnp.concatenate([pick(o_sheet, core), swap(pick(o_sheet, 1 - core), 1)], axis=2)
+    o_pair = o_pair.reshape(4, 4 * rank, out_cols)
+    o_extra = 3 * batch // 4
+    coded = jnp.broadcast_to(
+        in_three(o_reduced).reshape(4 * rank, o_extra)[None], (4, 4 * rank, o_extra)
+    )
+    o_pair = jnp.concatenate([o_pair, coded], axis=2)
+    from_z = [swap(pick(o_pair, z ^ d), 4 * d) for d in range(1, 4)]
+    mixed = stream_product(everyone, None, output_weight, 0, cut, None, o_pair)
+    sums = [from_three(v[:, out_cols:].reshape(batch, 3 * rank)) for v in from_z]
+    o_reduced = (o_reduced + sums[0]) + (sums[1] + sums[2])
+    o_ups = jnp.stack([pick(o_pair, z)] + from_z)[:, :, :out_cols]
+    o_ups = o_ups.reshape(4, 2, 2 * rank, out_cols)
+    coded = in_three(o_reduced).reshape(8 * rank, -1)
+    away = pick(o_ups, 1 - y, 1).reshape(8 * rank, out_cols)
+    away = jnp.concatenate([away, coded], axis=1)
+    away, mixed = lax.optimization_barrier((away, mixed))
+    from_y = swap(away, 2)
+    mixed = stream_product(everyone, None, output_weight, cut, depth, mixed, away)
+    o_reduced = o_reduced + from_three(from_y[:, out_cols:].reshape(batch, 3 * rank))
+
+    keep_out = lax.dynamic_slice_in_dim(mixed, kv_pos * half, half)
+    give_out = lax.dynamic_slice_in_dim(mixed, (1 - kv_pos) * half, half).astype(bf16)
+    o_keep = lax.dynamic_slice_in_dim(o_reduced, kv_pos * half, half)
+    o_give = in_three(lax.dynamic_slice_in_dim(o_reduced, (1 - kv_pos) * half, half))
+    from_x = swap(jnp.concatenate([give_out, o_give], axis=1), 16)
+    o_far = from_y[:, :out_cols]
+    o_near = pick(o_ups, y, 1).reshape(8 * rank, out_cols)
+    o_up = jnp.concatenate([o_near, o_far], axis=0)
+    o_keep = o_keep + from_three(from_x[:, out_cols:])
+    lane = jnp.arange(wide, dtype=jnp.int32)
+    owner = wide_pos ^ (((lane >> 1) & 3) * 4 + (lane >> 3) * 2 + (lane & 1))
+    slot_o = lax.dynamic_slice_in_dim(slot, kv_pos * half, half)
+    hit = slot_o == owner[None, :]
+    shrink = jnp.where(hit[:, :, None], o_keep.astype(bf16)[:, None, :], 0).reshape(half, -1)
+    change = jnp.dot(shrink, o_up, preferred_element_type=f32)
+    base = keep_out + from_x[:, :out_cols].astype(f32)
+    return (base + adapter_scale * change).astype(bf16)
+
+
+def on_device(*arrays):
+    lengths, key_cache, weight = arrays[13], arrays[4], arrays[2]
+    batch, rows, heads = arrays[0].shape[0], lengths.shape[0], key_cache.shape[1]
+    staged = batch == 16 * rows and heads == 4 and 2 * weight.shape[1] == 18 * key_cache.shape[3]
+    return (staged_path if staged else general_path)(*arrays)
+
+
 def solution(mesh):
     in_specs = (
         P(None, "kv"),

time: 276 us -> 94 us (0.34)
  waiting for transfers between devices: 129 us -> 25.8 us
  blocking collectives: 92.8 us -> 0 us
  starting transfers between devices: 0.13 us -> 34.6 us
  matrix products: 25.5 us -> 2.05 us
  Pallas kernels: 0 us -> 22.9 us
  between operations: 14.8 us -> 0.61 us
  local copies, waits for them, and re-layouts: 9.8 us -> 2.77 us
    reduce_scatter x2 -> x0, waiting for transfers between devices: 67.9 us -> none  [the longest x1 63.1 us: on_device(): lax.psum_scatter(jnp.dot(weight_sheet.T, own_shrink.T, preferred_element_...]
    all_gather x3 -> x0, blocking collectives: 61.9 us -> none  [the longest x1 24.3 us: on_device(): slice_portion = lax.all_gather(attention_output, 'wide', axis=0, tiled=True)]
    unnamed x5 -> x0, waiting for transfers between devices: 61.5 us -> none
    ppermute x0 -> x26, starting transfers between devices: none -> 34.6 us  [swap(): return lax.ppermute(x, ('kv', 'wide'), pairs)]
    ppermute x0 -> x26, waiting for transfers between devices: none -> 25.8 us  [swap(): return lax.ppermute(x, ('kv', 'wide'), pairs)]
    dot_general x11 -> x4, matrix products: 25.5 us -> 2.05 us  [the longest x1 0.83 us: staged_path(): change = jnp.dot(shrink, o_up, preferred_element_type=f32)]
    pallas_call x0 -> x8, Pallas kernels: none -> 22.9 us  [the longest x4 15.8 us: stream_product(): pl.pallas_call(kernel, in_specs=specs, out_specs=WHOLE, out_shape=jax.Sha...]
    all_to_all x1 -> x0, blocking collectives: 17.8 us -> none  [on_device(): lax.all_to_all(base_part, 'wide', split_axis=0, concat_axis=1, tiled=True)]
  transfers between devices with their start and end apart: 4 -> 26, of which waited for: 3 -> 15; matrix products, arithmetic and copies ran while one was open for 2% -> 5% of each run, Pallas kernels for 0% -> 18%
where the time goes in v2:
time: 94 us; the launch traced here: 93.7 us
  starting transfers between devices  34.6 us (37%)
  waiting for transfers between devices  25.8 us (27%)
  Pallas kernels  22.9 us (24%)
  other arithmetic  4.99 us (5%)
  local copies, waits for them, and re-layouts  2.77 us (3%)
  matrix products  2.05 us (2%)
    ppermute x26, starting transfers between devices, swap(): return lax.ppermute(x, ('kv', 'wide'), pairs)  34.6 us
    ppermute x26, waiting for transfers between devices, swap(): return lax.ppermute(x, ('kv', 'wide'), pairs)  25.8 us
    pallas_call x4, Pallas kernels, stream_product(): pl.pallas_call(kernel, in_specs=specs, out_specs=WHOLE, out_shape=jax.Sha...  15.8 us
    pallas_call x1, Pallas kernels, prepare(): pl.pallas_call(kernel, in_specs=[SCALARS, SCALARS, WHOLE] + [pl.BlockSpec...  3.56 us
    concatenate x2, other arithmetic, staged_path(): o_pair = jnp.concatenate([o_pair, coded], axis=2)  1.94 us
  transfers between devices with their start and end apart: 26, of which 15 were waited for; matrix products, arithmetic and copies ran while one was open for 5% of the time, Pallas kernels for 18%

profile of v2, /device:TPU:0, one launch (start us, length us, event | category | flops | bytes accessed | tf_op | source)
XLA Modules:
  0.0 93.7 jit_solution(1715763826490540730)
XLA Ops:
  3.1 3.6 %shard_map.145 = (bf16[32,1536]{1,0:T(8,128)(2,1)}, bf16[32,1536]{1,0:T(8,128)(2,1)}, f32[48,32]{1,0:T(8,128)}, s32[48,1]{1,0:T(8,128)}, f32[48,2]{1,0:T(8,128)}) custom-call(s32[4]{0:T(128)} %pad_add_fusion.place_ref, s32[16]{0:T(128)} %owner_ref.1, s32[1,48]{1,0:T(1,128)} %bitcast.116, bf16[48,8192]{1,0:T(8,128)(2,1)} %refs_0_.5, f32[1,8192]{1,0:T(1,128)} %bitcast.83, ...), custom_call_target="tpu_custom_call" | custom-call | tf_op jit(solution)/shard_map/pallas_call | solution.py:258
  6.7 4.0 %collective-permute-start.4 = (bf16[32,1536]{1,0:T(8,128)(2,1)}, bf16[32,1536]{1,0:T(8,128)(2,1)S(1)}, u32[]{:S(2)}, u32[]{:S(2)}) collective-permute-start(bf16[32,1536]{1,0:T(8,128)(2,1)} %get-tuple-element.19.a_ref.refs_2_), channel_id=1, source_target_pairs={{0,8},{1,9},{2,10},{3,11},{4,12},{5,13},{6,14},{7,15},{8,0},{9,1},... | collective-permute-start | bytes 294920 | tf_op jit(solution)/shard_map/ppermute | solution.py:546
  10.7 1.6 %collective-permute-start.3 = (bf16[32,1536]{1,0:T(8,128)(2,1)}, bf16[32,1536]{1,0:T(8,128)(2,1)S(1)}, u32[]{:S(2)}, u32[]{:S(2)}) collective-permute-start(bf16[32,1536]{1,0:T(8,128)(2,1)} %get-tuple-element.20), channel_id=1, source_target_pairs={{0,4},{1,5},{2,6},{3,7},{4,0},{5,1},{6,2},{7,3},{8,12},{9,13},{10,... | collective-permute-start | bytes 294920 | tf_op jit(solution)/shard_map/ppermute | solution.py:546
  13.2 4.8 %shard_map.147.refs_4_ = f32[48,1152]{1,0:T(8,128)S(1)} custom-call(bf16[48,8192]{1,0:T(8,128)(2,1)S(1)} %copy-done.1, bf16[8192,1152]{1,0:T(8,128)(2,1)} %refs_1_.5, bf16[32,1536]{1,0:T(8,128)(2,1)S(1)} %copy-done.2, f32[1,8192]{1,0:T(1,128)S(1)} %bitcast.84), custom_call_target="tpu_custom_call" | custom-call | flops 566231040 | bytes 11796480 | tf_op jit(solution)/shard_map/pallas_call | solution.py:313
  18.0 1.4 %collective-permute-done.5.d_ref = bf16[32,1536]{1,0:T(8,128)(2,1)S(1)} collective-permute-done((bf16[32,1536]{1,0:T(8,128)(2,1)}, bf16[32,1536]{1,0:T(8,128)(2,1)S(1)}, u32[]{:S(2)}, u32[]{:S(2)}) %collective-permute-start.5) | collective-permute-done | bytes 98336 | tf_op jit(solution)/shard_map/ppermute | solution.py:546
  20.2 1.6 %collective-permute-start.6 = (bf16[64,1280]{1,0:T(8,128)(2,1)S(1)}, bf16[64,1280]{1,0:T(8,128)(2,1)S(1)}, u32[]{:S(2)}, u32[]{:S(2)}) collective-permute-start(bf16[64,1280]{1,0:T(8,128)(2,1)S(1)} %get-tuple-element.23.refs_2_), channel_id=1, source_target_pairs={{0,2},{1,3},{2,0},{3,1},{4,6},{5,7},{6,4},{7,5},{8,10},{9,11},{10,... | collective-permute-start | bytes 491528 | tf_op jit(solution)/shard_map/ppermute | solution.py:546
  21.8 3.4 %shard_map.148.p_ref = f32[48,1152]{1,0:T(8,128)S(1)} custom-call(bf16[48,8192]{1,0:T(8,128)(2,1)S(1)} %copy-done.1, bf16[8192,1152]{1,0:T(8,128)(2,1)} %refs_1_.5, bf16[64,1280]{1,0:T(8,128)(2,1)S(1)} %get-tuple-element.23.refs_2_, f32[1,8192]{1,0:T(1,128)S(1)} %bitcast.85, f32[48,1152]{1,0:T(8,128)S(1)} %shard_map.147.refs_4_), custom_call_target="tpu_custom_call" | custom-call | flops 339738624 | bytes 7077888 | tf_op jit(solution)/shard_map/pallas_call | solution.py:313
  27.3 5.4 %collective-permute-done.7.r_ref = bf16[48,1248]{1,0:T(8,128)(2,1)S(1)} collective-permute-done((bf16[48,1248]{1,0:T(8,128)(2,1)S(1)}, bf16[48,1248]{1,0:T(8,128)(2,1)S(1)}, u32[]{:S(2)}, u32[]{:S(2)}) %collective-permute-start.7) | collective-permute-done | bytes 119840 | tf_op jit(solution)/shard_map/ppermute | solution.py:546
  33.7 3.4 %collective-permute-start.10 = (bf16[9,12,128]{2,1,0:T(8,128)(2,1)S(1)}, bf16[9,12,128]{2,1,0:T(8,128)(2,1)S(1)}, u32[]{:S(2)}, u32[]{:S(2)}) collective-permute-start(bf16[9,12,128]{2,1,0:T(8,128)(2,1)S(1)} %get-tuple-element.51), channel_id=1, source_target_pairs={{0,12},{1,13},{2,14},{3,15},{4,8},{5,9},{6,10},{7,11},{24,20},{25,... | collective-permute-start | bytes 82952 | tf_op jit(solution)/shard_map/ppermute | solution.py:546
  37.0 4.3 %collective-permute-start.9 = (bf16[9,12,128]{2,1,0:T(8,128)(2,1)S(1)}, bf16[9,12,128]{2,1,0:T(8,128)(2,1)S(1)}, u32[]{:S(2)}, u32[]{:S(2)}) collective-permute-start(bf16[9,12,128]{2,1,0:T(8,128)(2,1)S(1)} %get-tuple-element.52), channel_id=1, source_target_pairs={{0,4},{1,5},{2,6},{3,7},{4,0},{5,1},{6,2},{7,3},{24,28},{25,29},{2... | collective-permute-start | bytes 82952 | tf_op jit(solution)/shard_map/ppermute | solution.py:546
  44.4 1.6 %collective-permute-start.11 = (bf16[2,9,6,128]{3,2,1,0:T(8,128)(2,1)S(1)}, bf16[2,9,6,128]{3,2,1,0:T(8,128)(2,1)S(1)}, u32[]{:S(2)}, u32[]{:S(2)}) collective-permute-start(bf16[2,9,6,128]{3,2,1,0:T(8,128)(2,1)S(1)} %fusion.17), channel_id=1, source_target_pairs={{0,2},{1,3},{2,0},{3,1},{4,6},{5,7},{6,4},{7,5},{8,10},{9,11},{10,... | collective-permute-start | bytes 82952 | tf_op jit(solution)/shard_map/ppermute | solution.py:546
  46.1 2.3 %collective-permute-done.11 = bf16[2,9,6,128]{3,2,1,0:T(8,128)(2,1)S(1)} collective-permute-done((bf16[2,9,6,128]{3,2,1,0:T(8,128)(2,1)S(1)}, bf16[2,9,6,128]{3,2,1,0:T(8,128)(2,1)S(1)}, u32[]{:S(2)}, u32[]{:S(2)}) %collective-permute-start.11) | collective-permute-done | bytes 27680 | tf_op jit(solution)/shard_map/ppermute | solution.py:546
  53.0 2.3 %collective-permute-start.14 = (bf16[192,128]{1,0:T(8,128)(2,1)S(1)}, bf16[192,128]{1,0:T(8,128)(2,1)S(1)}, u32[]{:S(2)}, u32[]{:S(2)}) collective-permute-start(bf16[192,128]{1,0:T(8,128)(2,1)S(1)} %bitcast.105), channel_id=1, source_target_pairs={{0,8},{1,9},{2,10},{3,11},{4,12},{5,13},{6,14},{7,15},{8,0},{9,1},... | collective-permute-start | bytes 147464 | tf_op jit(solution)/shard_map/ppermute | solution.py:546
  55.3 1.4 %collective-permute-start.15 = (bf16[192,128]{1,0:T(8,128)(2,1)S(1)}, bf16[192,128]{1,0:T(8,128)(2,1)S(1)}, u32[]{:S(2)}, u32[]{:S(2)}) collective-permute-start(bf16[192,128]{1,0:T(8,128)(2,1)S(1)} %bitcast.106), channel_id=1, source_target_pairs={{0,12},{1,13},{2,14},{3,15},{4,8},{5,9},{6,10},{7,11},{8,4},{9,5},... | collective-permute-start | bytes 147464 | tf_op jit(solution)/shard_map/ppermute | solution.py:546
  58.0 3.3 %collective-permute-done.15 = bf16[192,128]{1,0:T(8,128)(2,1)S(1)} collective-permute-done((bf16[192,128]{1,0:T(8,128)(2,1)S(1)}, bf16[192,128]{1,0:T(8,128)(2,1)S(1)}, u32[]{:S(2)}, u32[]{:S(2)}) %collective-permute-start.15) | collective-permute-done | bytes 49184 | tf_op jit(solution)/shard_map/ppermute | solution.py:546
  61.3 1.6 %collective-permute-start.16 = (bf16[4,192,128]{2,1,0:T(8,128)(2,1)S(1)}, bf16[4,192,128]{2,1,0:T(8,128)(2,1)S(1)}, u32[]{:S(2)}, u32[]{:S(2)}) collective-permute-start(bf16[4,192,128]{2,1,0:T(8,128)(2,1)S(1)} %pad_maximum_fusion.5.a_ref), channel_id=1, source_target_pairs={{0,2},{1,3},{2,0},{3,1},{4,6},{5,7},{6,4},{7,5},{8,10},{9,11},{10,... | collective-permute-start | bytes 589832 | tf_op jit(solution)/shard_map/ppermute | solution.py:546
  62.9 4.1 %collective-permute-done.16.b_ref = bf16[4,192,128]{2,1,0:T(8,128)(2,1)S(1)} collective-permute-done((bf16[4,192,128]{2,1,0:T(8,128)(2,1)S(1)}, bf16[4,192,128]{2,1,0:T(8,128)(2,1)S(1)}, u32[]{:S(2)}, u32[]{:S(2)}) %collective-permute-start.16) | collective-permute-done | bytes 196640 | tf_op jit(solution)/shard_map/ppermute | solution.py:546
  68.5 1.8 %shard_map.150 = (bf16[48,8192]{1,0:T(8,128)(2,1)S(1)}, f32[48,8]{1,0:T(8,128)S(1)}) custom-call(s32[16]{0:T(128)S(1)} %broadcast_xor_fusion.order_ref, bf16[4,192,128]{2,1,0:T(8,128)(2,1)S(1)} %pad_maximum_fusion.5.a_ref, bf16[4,192,128]{2,1,0:T(8,128)(2,1)S(1)} %collective-permute-done.16.b_ref, bf16[4,192,128]{2,1,0:T(8,128)(2,1)S(1)} %collective-permute-done.17.c_ref, ...), custom_call_target="tpu_custom_call" | custom-call | bytes 1572864 | tf_op jit(solution)/shard_map/pallas_call | solution.py:472
  73.7 2.1 %collective-permute-start.22 = (bf16[32,1060]{1,0:T(8,128)(2,1)S(1)}, bf16[32,1060]{1,0:T(8,128)(2,1)S(1)}, u32[]{:S(2)}, u32[]{:S(2)}) collective-permute-start(bf16[32,1060]{1,0:T(8,128)(2,1)S(1)} %get-tuple-element.41), channel_id=1, source_target_pairs={{0,8},{1,9},{2,10},{3,11},{4,12},{5,13},{6,14},{7,15},{8,0},{9,1},... | collective-permute-start | bytes 203528 | tf_op jit(solution)/shard_map/ppermute | solution.py:546
  77.0 4.4 %shard_map.151.refs_3_ = f32[48,1024]{1,0:T(8,128)S(1)} custom-call(bf16[48,8192]{1,0:T(8,128)(2,1)S(1)} %get-tuple-element.29.refs_0_, bf16[8192,1024]{1,0:T(8,128)(2,1)} %refs_1_.7, bf16[4,32,1060]{2,1,0:T(8,128)(2,1)S(1)} %pad_maximum_fusion.refs_2_), custom_call_target="tpu_custom_call" | custom-call | flops 503316480 | bytes 10485760 | tf_op jit(solution)/shard_map/pallas_call | solution.py:313
  83.0 1.6 %collective-permute-start.24 = (bf16[64,1042]{1,0:T(8,128)(2,1)S(1)}, bf16[64,1042]{1,0:T(8,128)(2,1)S(1)}, u32[]{:S(2)}, u32[]{:S(2)}) collective-permute-start(bf16[64,1042]{1,0:T(8,128)(2,1)S(1)} %pad_maximum_fusion.6.refs_2_), channel_id=1, source_target_pairs={{0,2},{1,3},{2,0},{3,1},{4,6},{5,7},{6,4},{7,5},{8,10},{9,11},{10,... | collective-permute-start | bytes 400136 | tf_op jit(solution)/shard_map/ppermute | solution.py:546
  84.6 3.1 %shard_map.152 = f32[48,1024]{1,0:T(8,128)S(1)} custom-call(bf16[48,8192]{1,0:T(8,128)(2,1)S(1)} %get-tuple-element.29.refs_0_, bf16[8192,1024]{1,0:T(8,128)(2,1)} %refs_1_.7, bf16[64,1042]{1,0:T(8,128)(2,1)S(1)} %pad_maximum_fusion.6.refs_2_, f32[48,1024]{1,0:T(8,128)S(1)} %shard_map.151.refs_3_), custom_call_target="tpu_custom_call" | custom-call | flops 301989888 | bytes 6291456 | tf_op jit(solution)/shard_map/pallas_call | solution.py:313
  88.5 1.8 %collective-permute-start.25 = (bf16[24,1048]{1,0:T(8,128)(2,1)S(1)}, bf16[24,1048]{1,0:T(8,128)(2,1)S(1)}, u32[]{:S(2)}, u32[]{:S(2)}) collective-permute-start(bf16[24,1048]{1,0:T(8,128)(2,1)S(1)} %concatenate.51), channel_id=1, source_target_pairs={{0,16},{1,17},{2,18},{3,19},{4,20},{5,21},{6,22},{7,23},{8,24},{9,... | collective-permute-start | bytes 150920 | tf_op jit(solution)/shard_map/ppermute | solution.py:546
  90.4 2.3 %collective-permute-done.25 = bf16[24,1048]{1,0:T(8,128)(2,1)S(1)} collective-permute-done((bf16[24,1048]{1,0:T(8,128)(2,1)S(1)}, bf16[24,1048]{1,0:T(8,128)(2,1)S(1)}, u32[]{:S(2)}, u32[]{:S(2)}) %collective-permute-start.25) | collective-permute-done | bytes 50336 | tf_op jit(solution)/shard_map/ppermute | solution.py:546
  (139 shorter events, 25.8 us)
Async XLA Ops:
  0.0 2.3 %collective-permute-start = (bf16[24,8192]{1,0:T(8,128)(2,1)}, bf16[24,8192]{1,0:T(8,128)(2,1)S(1)}, u32[]{:S(2)}, u32[]{:S(2)}) collective-permute-start(bf16[24,8192]{1,0:T(8,128)(2,1)} %bitcast.92), channel_id=1, source_target_pairs={{0,1},{1,0},{2,3},{3,2},{4,5},{5,4},{6,7},{7,6},{8,9},{9,8},{10,11... | collective-permute-start | bytes 1179656 | tf_op jit(solution)/shard_map/ppermute | solution.py:546
  0.5 1.8 %collective-permute-start.1 = (bf16[8,8192]{1,0:T(8,128)(2,1)}, bf16[8,8192]{1,0:T(8,128)(2,1)S(1)}, u32[]{:S(2)}, u32[]{:S(2)}) collective-permute-start(bf16[8,8192]{1,0:T(8,128)(2,1)} %bitcast.98), channel_id=1, source_target_pairs={{0,1},{1,0},{2,3},{3,2},{4,5},{5,4},{6,7},{7,6},{8,9},{9,8},{10,11... | collective-permute-start | bytes 393224 | tf_op jit(solution)/shard_map/ppermute | solution.py:546
  0.6 1.7 %collective-permute-start.2 = (bf16[2,8,512]{2,1,0:T(8,128)(2,1)}, bf16[2,8,512]{2,1,0:T(8,128)(2,1)S(1)}, u32[]{:S(2)}, u32[]{:S(2)}) collective-permute-start(bf16[2,8,512]{2,1,0:T(8,128)(2,1)} %bitcast.113), channel_id=1, source_target_pairs={{0,1},{1,0},{2,3},{3,2},{4,5},{5,4},{6,7},{7,6},{8,9},{9,8},{10,11... | collective-permute-start | bytes 49160 | tf_op jit(solution)/shard_map/ppermute | solution.py:546
  6.7 11.3 %collective-permute-start.4 = (bf16[32,1536]{1,0:T(8,128)(2,1)}, bf16[32,1536]{1,0:T(8,128)(2,1)S(1)}, u32[]{:S(2)}, u32[]{:S(2)}) collective-permute-start(bf16[32,1536]{1,0:T(8,128)(2,1)} %get-tuple-element.19.a_ref.refs_2_), channel_id=1, source_target_pairs={{0,8},{1,9},{2,10},{3,11},{4,12},{5,13},{6,14},{7,15},{8,0},{9,1},... | collective-permute-start | bytes 294920 | tf_op jit(solution)/shard_map/ppermute | solution.py:546
  10.7 7.3 %collective-permute-start.3 = (bf16[32,1536]{1,0:T(8,128)(2,1)}, bf16[32,1536]{1,0:T(8,128)(2,1)S(1)}, u32[]{:S(2)}, u32[]{:S(2)}) collective-permute-start(bf16[32,1536]{1,0:T(8,128)(2,1)} %get-tuple-element.20), channel_id=1, source_target_pairs={{0,4},{1,5},{2,6},{3,7},{4,0},{5,1},{6,2},{7,3},{8,12},{9,13},{10,... | collective-permute-start | bytes 294920 | tf_op jit(solution)/shard_map/ppermute | solution.py:546
  12.3 7.1 %collective-permute-start.5 = (bf16[32,1536]{1,0:T(8,128)(2,1)}, bf16[32,1536]{1,0:T(8,128)(2,1)S(1)}, u32[]{:S(2)}, u32[]{:S(2)}) collective-permute-start(bf16[32,1536]{1,0:T(8,128)(2,1)} %get-tuple-element.20), channel_id=1, source_target_pairs={{0,12},{1,13},{2,14},{3,15},{4,8},{5,9},{6,10},{7,11},{8,4},{9,5},... | collective-permute-start | bytes 294920 | tf_op jit(solution)/shard_map/ppermute | solution.py:546
  20.2 5.5 %collective-permute-start.6 = (bf16[64,1280]{1,0:T(8,128)(2,1)S(1)}, bf16[64,1280]{1,0:T(8,128)(2,1)S(1)}, u32[]{:S(2)}, u32[]{:S(2)}) collective-permute-start(bf16[64,1280]{1,0:T(8,128)(2,1)S(1)} %get-tuple-element.23.refs_2_), channel_id=1, source_target_pairs={{0,2},{1,3},{2,0},{3,1},{4,6},{5,7},{6,4},{7,5},{8,10},{9,11},{10,... | collective-permute-start | bytes 491528 | tf_op jit(solution)/shard_map/ppermute | solution.py:546
  25.9 6.8 %collective-permute-start.7 = (bf16[48,1248]{1,0:T(8,128)(2,1)S(1)}, bf16[48,1248]{1,0:T(8,128)(2,1)S(1)}, u32[]{:S(2)}, u32[]{:S(2)}) collective-permute-start(bf16[48,1248]{1,0:T(8,128)(2,1)S(1)} %concatenate.40), channel_id=1, source_target_pairs={{8,24},{9,25},{10,26},{11,27},{12,28},{13,29},{14,30},{15,31},{16,... | collective-permute-start | bytes 359432 | tf_op jit(solution)/shard_map/ppermute | solution.py:546
  27.2 40.7 %collective-permute-start.19 = (bf16[8,8192]{1,0:T(8,128)(2,1)S(1)}, bf16[8,8192]{1,0:T(8,128)(2,1)S(1)}, u32[]{:S(2)}, u32[]{:S(2)}) collective-permute-start(bf16[8,8192]{1,0:T(8,128)(2,1)S(1)} %bitcast.86), channel_id=1, source_target_pairs={{0,1},{1,0},{2,3},{3,2},{4,5},{5,4},{6,7},{7,6},{8,9},{9,8},{10,11... | collective-permute-start | bytes 393224 | tf_op jit(solution)/shard_map/ppermute | solution.py:546
  33.7 9.1 %collective-permute-start.10 = (bf16[9,12,128]{2,1,0:T(8,128)(2,1)S(1)}, bf16[9,12,128]{2,1,0:T(8,128)(2,1)S(1)}, u32[]{:S(2)}, u32[]{:S(2)}) collective-permute-start(bf16[9,12,128]{2,1,0:T(8,128)(2,1)S(1)} %get-tuple-element.51), channel_id=1, source_target_pairs={{0,12},{1,13},{2,14},{3,15},{4,8},{5,9},{6,10},{7,11},{24,20},{25,... | collective-permute-start | bytes 82952 | tf_op jit(solution)/shard_map/ppermute | solution.py:546
  37.0 6.3 %collective-permute-start.9 = (bf16[9,12,128]{2,1,0:T(8,128)(2,1)S(1)}, bf16[9,12,128]{2,1,0:T(8,128)(2,1)S(1)}, u32[]{:S(2)}, u32[]{:S(2)}) collective-permute-start(bf16[9,12,128]{2,1,0:T(8,128)(2,1)S(1)} %get-tuple-element.52), channel_id=1, source_target_pairs={{0,4},{1,5},{2,6},{3,7},{4,0},{5,1},{6,2},{7,3},{24,28},{25,29},{2... | collective-permute-start | bytes 82952 | tf_op jit(solution)/shard_map/ppermute | solution.py:546
  41.4 2.9 %collective-permute-start.8 = (bf16[9,12,128]{2,1,0:T(8,128)(2,1)S(1)}, bf16[9,12,128]{2,1,0:T(8,128)(2,1)S(1)}, u32[]{:S(2)}, u32[]{:S(2)}) collective-permute-start(bf16[9,12,128]{2,1,0:T(8,128)(2,1)S(1)} %get-tuple-element.53), channel_id=1, source_target_pairs={{0,8},{1,9},{2,10},{3,11},{4,12},{5,13},{6,14},{7,15},{24,16},{25,... | collective-permute-start | bytes 82952 | tf_op jit(solution)/shard_map/ppermute | solution.py:546
  44.4 4.0 %collective-permute-start.11 = (bf16[2,9,6,128]{3,2,1,0:T(8,128)(2,1)S(1)}, bf16[2,9,6,128]{3,2,1,0:T(8,128)(2,1)S(1)}, u32[]{:S(2)}, u32[]{:S(2)}) collective-permute-start(bf16[2,9,6,128]{3,2,1,0:T(8,128)(2,1)S(1)} %fusion.17), channel_id=1, source_target_pairs={{0,2},{1,3},{2,0},{3,1},{4,6},{5,7},{6,4},{7,5},{8,10},{9,11},{10,... | collective-permute-start | bytes 82952 | tf_op jit(solution)/shard_map/ppermute | solution.py:546
  51.9 4.9 %collective-permute-start.13 = (bf16[192,128]{1,0:T(8,128)(2,1)S(1)}, bf16[192,128]{1,0:T(8,128)(2,1)S(1)}, u32[]{:S(2)}, u32[]{:S(2)}) collective-permute-start(bf16[192,128]{1,0:T(8,128)(2,1)S(1)} %bitcast.104), channel_id=1, source_target_pairs={{0,4},{1,5},{2,6},{3,7},{4,0},{5,1},{6,2},{7,3},{8,12},{9,13},{10,... | collective-permute-start | bytes 147464 | tf_op jit(solution)/shard_map/ppermute | solution.py:546
  53.0 5.0 %collective-permute-start.14 = (bf16[192,128]{1,0:T(8,128)(2,1)S(1)}, bf16[192,128]{1,0:T(8,128)(2,1)S(1)}, u32[]{:S(2)}, u32[]{:S(2)}) collective-permute-start(bf16[192,128]{1,0:T(8,128)(2,1)S(1)} %bitcast.105), channel_id=1, source_target_pairs={{0,8},{1,9},{2,10},{3,11},{4,12},{5,13},{6,14},{7,15},{8,0},{9,1},... | collective-permute-start | bytes 147464 | tf_op jit(solution)/shard_map/ppermute | solution.py:546
  55.3 6.0 %collective-permute-start.15 = (bf16[192,128]{1,0:T(8,128)(2,1)S(1)}, bf16[192,128]{1,0:T(8,128)(2,1)S(1)}, u32[]{:S(2)}, u32[]{:S(2)}) collective-permute-start(bf16[192,128]{1,0:T(8,128)(2,1)S(1)} %bitcast.106), channel_id=1, source_target_pairs={{0,12},{1,13},{2,14},{3,15},{4,8},{5,9},{6,10},{7,11},{8,4},{9,5},... | collective-permute-start | bytes 147464 | tf_op jit(solution)/shard_map/ppermute | solution.py:546
  56.7 10.4 %collective-permute-start.20 = (bf16[4,2,8,1024]{3,2,1,0:T(8,128)(2,1)S(1)}, bf16[4,2,8,1024]{3,2,1,0:T(8,128)(2,1)S(1)}, u32[]{:S(2)}, u32[]{:S(2)}) collective-permute-start(bf16[4,2,8,1024]{3,2,1,0:T(8,128)(2,1)S(1)} %get-tuple-element.46), channel_id=1, source_target_pairs={{0,1},{1,0},{2,3},{3,2},{4,5},{5,4},{6,7},{7,6},{8,9},{9,8},{10,11... | collective-permute-start | bytes 393224 | tf_op jit(solution)/shard_map/ppermute | solution.py:546
  61.3 5.7 %collective-permute-start.16 = (bf16[4,192,128]{2,1,0:T(8,128)(2,1)S(1)}, bf16[4,192,128]{2,1,0:T(8,128)(2,1)S(1)}, u32[]{:S(2)}, u32[]{:S(2)}) collective-permute-start(bf16[4,192,128]{2,1,0:T(8,128)(2,1)S(1)} %pad_maximum_fusion.5.a_ref), channel_id=1, source_target_pairs={{0,2},{1,3},{2,0},{3,1},{4,6},{5,7},{6,4},{7,5},{8,10},{9,11},{10,... | collective-permute-start | bytes 589832 | tf_op jit(solution)/shard_map/ppermute | solution.py:546
  62.9 5.0 %collective-permute-start.17 = (bf16[4,192,128]{2,1,0:T(8,128)(2,1)S(1)}, bf16[4,192,128]{2,1,0:T(8,128)(2,1)S(1)}, u32[]{:S(2)}, u32[]{:S(2)}) collective-permute-start(bf16[4,192,128]{2,1,0:T(8,128)(2,1)S(1)} %pad_maximum_fusion.5.a_ref), channel_id=1, source_target_pairs={{0,1},{1,0},{2,3},{3,2},{4,5},{5,4},{6,7},{7,6},{8,9},{9,8},{10,11... | collective-permute-start | bytes 589832 | tf_op jit(solution)/shard_map/ppermute | solution.py:546
  71.5 9.9 %collective-permute-start.21 = (bf16[32,1060]{1,0:T(8,128)(2,1)S(1)}, bf16[32,1060]{1,0:T(8,128)(2,1)S(1)}, u32[]{:S(2)}, u32[]{:S(2)}) collective-permute-start(bf16[32,1060]{1,0:T(8,128)(2,1)S(1)} %get-tuple-element.40), channel_id=1, source_target_pairs={{0,4},{1,5},{2,6},{3,7},{4,0},{5,1},{6,2},{7,3},{8,12},{9,13},{10,... | collective-permute-start | bytes 203528 | tf_op jit(solution)/shard_map/ppermute | solution.py:546
  73.7 8.6 %collective-permute-start.22 = (bf16[32,1060]{1,0:T(8,128)(2,1)S(1)}, bf16[32,1060]{1,0:T(8,128)(2,1)S(1)}, u32[]{:S(2)}, u32[]{:S(2)}) collective-permute-start(bf16[32,1060]{1,0:T(8,128)(2,1)S(1)} %get-tuple-element.41), channel_id=1, source_target_pairs={{0,8},{1,9},{2,10},{3,11},{4,12},{5,13},{6,14},{7,15},{8,0},{9,1},... | collective-permute-start | bytes 203528 | tf_op jit(solution)/shard_map/ppermute | solution.py:546
  75.9 6.7 %collective-permute-start.23 = (bf16[32,1060]{1,0:T(8,128)(2,1)S(1)}, bf16[32,1060]{1,0:T(8,128)(2,1)S(1)}, u32[]{:S(2)}, u32[]{:S(2)}) collective-permute-start(bf16[32,1060]{1,0:T(8,128)(2,1)S(1)} %get-tuple-element.42), channel_id=1, source_target_pairs={{0,12},{1,13},{2,14},{3,15},{4,8},{5,9},{6,10},{7,11},{8,4},{9,5},... | collective-permute-start | bytes 203528 | tf_op jit(solution)/shard_map/ppermute | solution.py:546
  83.0 5.2 %collective-permute-start.24 = (bf16[64,1042]{1,0:T(8,128)(2,1)S(1)}, bf16[64,1042]{1,0:T(8,128)(2,1)S(1)}, u32[]{:S(2)}, u32[]{:S(2)}) collective-permute-start(bf16[64,1042]{1,0:T(8,128)(2,1)S(1)} %pad_maximum_fusion.6.refs_2_), channel_id=1, source_target_pairs={{0,2},{1,3},{2,0},{3,1},{4,6},{5,7},{6,4},{7,5},{8,10},{9,11},{10,... | collective-permute-start | bytes 400136 | tf_op jit(solution)/shard_map/ppermute | solution.py:546
  88.5 4.2 %collective-permute-start.25 = (bf16[24,1048]{1,0:T(8,128)(2,1)S(1)}, bf16[24,1048]{1,0:T(8,128)(2,1)S(1)}, u32[]{:S(2)}, u32[]{:S(2)}) collective-permute-start(bf16[24,1048]{1,0:T(8,128)(2,1)S(1)} %concatenate.51), channel_id=1, source_target_pairs={{0,16},{1,17},{2,18},{3,19},{4,20},{5,21},{6,22},{7,23},{8,24},{9,... | collective-permute-start | bytes 150920 | tf_op jit(solution)/shard_map/ppermute | solution.py:546
  (18 other events, 166.8 us)

commit v3 on v2

--- a/solution.py
+++ b/solution.py
@@ -169,31 +169,61 @@
 SCALARS = pl.BlockSpec(memory_space=pltpu.SMEM)
 
 
-def prepare(place, hidden_input, gain, owned, swapped, adapters, owners, cols):
+def code_two(ref, at, v):
+    width = v.shape[1]
+    groups = v.shape[0] // 16
+    down = ref.shape[0] // 16
+    for g in range(groups):
+        rows = slice(g % down * 16, (g % down + 1) * 16)
+        left = v[g * 16 : (g + 1) * 16]
+        for t in range(2):
+            lane = at + (g // down * 2 + t) * width
+            top = left.astype(jnp.bfloat16)
+            ref[rows, lane : lane + width] = top
+            left = left - top.astype(jnp.float32)
+
+
+def read_two(ref, at, width, groups):
+    down = ref.shape[0] // 16
+    out = []
+    for g in range(groups):
+        rows = slice(g % down * 16, (g % down + 1) * 16)
+        lane = at + g // down * 2 * width
+        part = ref[rows, lane : lane + 2 * width].astype(jnp.float32)
+        out.append(part[:, :width] + part[:, width:])
+    return jnp.concatenate(out, axis=0)
+
+
+def prepare(hidden_input, gain, down, query_up, key_value_up, adapters, owners):
     count, width = hidden_input.shape
-    entries = owned[0].shape[0]
-    rank, heads_width = owned[1].shape
+    entries = down.shape[0]
+    rank, heads_width = query_up.shape
     head_dim = 128
-    lanes = 128
-    heads = owned[2].shape[2] // head_dim
+    heads = key_value_up.shape[2] // head_dim
     group_width = heads_width // heads
-    each = count // 3
+    span = group_width + 2 * head_dim
     chunk = 1024
-    held = (hidden_input, gain, *owned, *swapped)
-
-    def kernel(place_ref, owner_ref, index_ref, *refs):
-        inputs, outputs = refs[: len(held)], refs[len(held) : len(held) + 5]
-        buffers, sem = refs[len(held) + 5 : -1], refs[-1]
-        same_ref, flip_ref, small_ref, slot_ref, mine_ref = outputs
+    quarter = width // 4
+    held = (hidden_input, gain, down, query_up, key_value_up)
+
+    def kernel(
+        owner_ref, index_ref, x_in, gain_in, down_in, q_in, kv_in,
+        same_ref, flip_ref, small_ref, slot_ref, mine_ref,
+        x_ref, gain_ref, down_ref, q_ref, kv_ref, sem,
+    ):
+        def x_copy(i):
+            part = (slice(None), pl.ds(i * quarter, quarter))
+            return pltpu.make_async_copy(x_in.at[part], x_ref.at[part], sem.at[i])
+
+        pairs = ((gain_in, gain_ref), (down_in, down_ref), (q_in, q_ref), (kv_in, kv_ref))
         copies = [
-            pltpu.make_async_copy(src, dst, sem.at[i])
-            for i, (src, dst) in enumerate(zip(inputs, buffers))
+            pltpu.make_async_copy(src, dst, sem.at[4 + i]) for i, (src, dst) in enumerate(pairs)
         ]
-        for copy in copies:
+        x_copies = [x_copy(i) for i in range(4)]
+        for copy in copies[:2] + x_copies + copies[2:]:
             copy.start()
-        x_ref, gain_ref = buffers[:2]
-        down_refs, q_refs, kv_refs = buffers[2::3], buffers[3::3], buffers[4::3]
-
+
+        wide_pos = lax.axis_index("wide")
         row = lax.broadcasted_iota(jnp.int32, (count, count), 0)
         column = lax.broadcasted_iota(jnp.int32, (count, count), 1)
         across = jnp.where(row == column, index_ref[...].astype(jnp.float32), 0.0)
@@ -202,74 +232,62 @@
         for a in range(owners.shape[0]):
             slot = jnp.where(index == a, owner_ref[a], slot)
         slot_ref[...] = slot
-        mine = [(slot == (place_ref[1] ^ dcore)).astype(jnp.float32) for dcore in range(2)]
-        for dcore in range(2):
-            mine_ref[:, dcore : dcore + 1] = mine[dcore]
-
-        for copy in copies:
+        mine = (slot == wide_pos).astype(jnp.float32)
+        mine_ref[...] = mine
+
+        for copy in copies[:2]:
             copy.wait()
         total = jnp.zeros((count, 1), jnp.float32)
-        reduced = [jnp.zeros((count, entries), jnp.float32) for _ in range(2)]
+        reduced = jnp.zeros((count, entries), jnp.float32)
         for at in range(0, width, chunk):
             part = slice(at, at + chunk)
+            if at % quarter == 0:
+                x_copies[at // quarter].wait()
             x = x_ref[:, part].astype(jnp.float32)
             total = total + jnp.sum(x * x, axis=1, keepdims=True)
             gained = (x * gain_ref[:, part]).astype(jnp.bfloat16)
-            for dcore in range(2):
-                reduced[dcore] = reduced[dcore] + lax.dot_general(
-                    gained, down_refs[dcore][:, part], (((1,), (1,)), ((), ())),
-                    preferred_element_type=jnp.float32,
+            reduced = reduced + lax.dot_general(
+                gained, down_ref[:, part], (((1,), (1,)), ((), ())),
+                preferred_element_type=jnp.float32,
+            )
+        small_ref[...] = jnp.zeros_like(small_ref)
+        small_ref[:, :entries] = reduced * mine
+        small_ref[:, entries : entries + 1] = total * mine
+        small = small_ref[...]
+        for copy in copies[2:]:
+            copy.wait()
+
+        low = (wide_pos >> 2) & 1
+        for ref, zb in ((same_ref, low), (flip_ref, 1 - low)):
+            ref[:, span:] = jnp.zeros((2 * rank, 256), ref.dtype)
+            code_two(ref, span, small)
+            q = q_ref[:, pl.ds(pl.multiple_of(zb * 2 * group_width, 128), 2 * group_width)]
+            ref[:, :group_width] = jnp.concatenate(
+                [q[:, :group_width], q[:, group_width:]], axis=0
+            )
+            for t in range(2):
+                kv = kv_ref[t, :, pl.ds(pl.multiple_of(zb * 2 * head_dim, 128), 2 * head_dim)]
+                lane = group_width + t * head_dim
+                ref[:, lane : lane + head_dim] = jnp.concatenate(
+                    [kv[:, :head_dim], kv[:, head_dim:]], axis=0
                 )
-        small_ref[...] = jnp.zeros_like(small_ref)
-        small_ref[:, :entries] = reduced[0] * mine[0] + reduced[1] * mine[1]
-        small_ref[:, entries : entries + 1] = total * (mine[0] + mine[1])
-        small = small_ref[...]
-
-        for ref in (same_ref, flip_ref):
-            ref[:, cols:] = jnp.zeros((4 * rank, 3 * lanes), ref.dtype)
-            for g in range(3):
-                code_three(ref, slice(0, each), cols + g * lanes, small[g * each : (g + 1) * each])
-
-        def write(core, zb, ref):
-            for yb in range(2):
-                h = zb * 2 + yb
-                rows = slice(yb * 2 * rank, (yb + 1) * 2 * rank)
-                at = h * group_width
-                spans = [(at, at + cols), (at + cols, at + group_width)][core]
-                joined = jnp.concatenate([q[:, spans[0] : spans[1]] for q in q_refs], axis=0)
-                rest = spans[1] - spans[0]
-                ref[rows, :rest] = joined
-                if core == 1:
-                    for t in range(2):
-                        part = slice(h * head_dim, (h + 1) * head_dim)
-                        ref[rows, rest + t * head_dim : rest + (t + 1) * head_dim] = (
-                            jnp.concatenate([kv[t, :, part] for kv in kv_refs], axis=0)
-                        )
-
-        for core in range(2):
-            for low in range(2):
-
-                @pl.when((place_ref[0] == core) & ((place_ref[2] & 1) == low))
-                def _():
-                    write(core, low, same_ref)
-                    write(core, 1 - low, flip_ref)
-
-    message = jax.ShapeDtypeStruct((4 * rank, cols + 3 * lanes), owned[1].dtype)
+
+    message = jax.ShapeDtypeStruct((2 * rank, span + 256), query_up.dtype)
     return pl.pallas_call(
         kernel,
-        in_specs=[SCALARS, SCALARS, WHOLE] + [pl.BlockSpec(memory_space=pl.ANY)] * len(held),
+        in_specs=[SCALARS, WHOLE] + [pl.BlockSpec(memory_space=pl.ANY)] * len(held),
         out_specs=[WHOLE] * 5,
         out_shape=[
             message,
             message,
             jax.ShapeDtypeStruct((count, 32), jnp.float32),
             jax.ShapeDtypeStruct((count, 1), jnp.int32),
-            jax.ShapeDtypeStruct((count, 2), jnp.float32),
+            jax.ShapeDtypeStruct((count, 1), jnp.float32),
         ],
         scratch_shapes=[pltpu.VMEM(v.shape, v.dtype) for v in held]
-        + [pltpu.SemaphoreType.DMA((len(held),))],
+        + [pltpu.SemaphoreType.DMA((8,))],
         compiler_params=pltpu.CompilerParams(vmem_limit_bytes=60 * 2**20),
-    )(place, owners, adapters, *held)
+    )(owners, adapters, *held)
 
 
 def stream_product(rows_in, gain, weight, start, stop, before, marker):
@@ -328,69 +346,60 @@
     )(*operands)
 
 
-def code_three(ref, rows, at, v):
-    width = v.shape[1]
-    for t in range(3):
-        top = v.astype(jnp.bfloat16)
-        ref[rows, at + t * width : at + (t + 1) * width] = top
-        v = v - top.astype(jnp.float32)
-
-
-def pack_y(place, parts, small, cols):
-    tall, wide_cols = parts[0].shape
+def pack_y(parts, small, cols):
+    tall = parts[0].shape[0]
     count, entries = small.shape
-    lanes = 128
-    each = count // 3
-    rows = tall // 2
-
-    def kernel(place_ref, a_ref, b_ref, c_ref, d_ref, small_ref, away_ref, keep_ref, sum_ref):
+    rank = tall // 2
+    rows = 4 * rank
+
+    def kernel(a_ref, b_ref, c_ref, d_ref, small_ref, away_ref, near_ref, far_ref, sum_ref):
+        refs = (a_ref, b_ref, c_ref, d_ref)
         total = small_ref[...]
-        for ref in (b_ref, c_ref, d_ref):
-            coded = jnp.concatenate(
-                [
-                    ref[:each, cols + g * lanes : cols + g * lanes + 3 * entries]
-                    for g in range(3)
-                ],
-                axis=0,
-            ).astype(jnp.float32)
-            total = total + (
-                (coded[:, :entries] + coded[:, entries : 2 * entries]) + coded[:, 2 * entries :]
+        for ref in refs[1:]:
+            total = total + read_two(ref, 2 * cols, entries, count // 16)
+        sum_ref[...] = total
+        away_ref[:, 2 * cols :] = jnp.zeros((rows, 128), away_ref.dtype)
+        code_two(away_ref, 2 * cols, total)
+
+        wide_pos = lax.axis_index("wide")
+        core, y = wide_pos & 1, (wide_pos >> 1) & 1
+
+        def write(yb, cb):
+            for out, half in ((near_ref, cb), (far_ref, 1 - cb)):
+                out[...] = jnp.concatenate(
+                    [
+                        ref[yb * rank : (yb + 1) * rank, half * cols : (half + 1) * cols]
+                        for ref in refs
+                    ],
+                    axis=0,
+                )
+            away_ref[:, : 2 * cols] = jnp.concatenate(
+                [ref[(1 - yb) * rank : (2 - yb) * rank, : 2 * cols] for ref in refs], axis=0
             )
-        sum_ref[...] = total
-
-        def write(yb):
-            for dz, ref in enumerate((a_ref, b_ref, c_ref, d_ref)):
-                keep_ref[dz] = ref[yb * rows : (yb + 1) * rows, :cols]
-                away_ref[dz * rows : (dz + 1) * rows, :cols] = ref[
-                    (1 - yb) * rows : (2 - yb) * rows, :cols
-                ]
-
-        @pl.when(place_ref[3] == 0)
-        def _():
-            write(0)
-
-        @pl.when(place_ref[3] == 1)
-        def _():
-            write(1)
-
-        away_ref[:, cols:] = jnp.zeros_like(away_ref[:, cols:])
-        code_three(away_ref, slice(0, count), cols, total)
+
+        for yb in range(2):
+            for cb in range(2):
+
+                @pl.when((y == yb) & (core == cb))
+                def _():
+                    write(yb, cb)
 
     dtype = parts[0].dtype
     return pl.pallas_call(
         kernel,
-        in_specs=[SCALARS] + [WHOLE] * 5,
-        out_specs=[WHOLE] * 3,
+        in_specs=[WHOLE] * 5,
+        out_specs=[WHOLE] * 4,
         out_shape=[
-            jax.ShapeDtypeStruct((4 * rows, cols + lanes), dtype),
-            jax.ShapeDtypeStruct((4, rows, cols), dtype),
+            jax.ShapeDtypeStruct((rows, 2 * cols + 128), dtype),
+            jax.ShapeDtypeStruct((rows, cols), dtype),
+            jax.ShapeDtypeStruct((rows, cols), dtype),
             jax.ShapeDtypeStruct(small.shape, jnp.float32),
         ],
         compiler_params=pltpu.CompilerParams(vmem_limit_bytes=8 * 2**20),
-    )(place, *parts, small)
-
-
-def merge(place, partial, small, received, near, far, slot):
+    )(*parts, small)
+
+
+def merge(partial, small, received, ups, slot):
     count, cols = partial.shape
     lanes = 128
     blocks = cols // lanes
@@ -398,13 +407,14 @@
     entries = 24
     rank = entries // 3
 
-    def kernel(place_ref, p_ref, small_ref, r_ref, near_ref, far_ref, slot_ref, out_ref, acc_ref):
-        other = r_ref[:, cols : cols + 96].astype(jnp.float32)
-        small = small_ref[...] + ((other[:, :32] + other[:, 32:64]) + other[:, 64:96])
+    def kernel(p_ref, small_ref, r_ref, a_ref, b_ref, c_ref, d_ref, slot_ref, out_ref, acc_ref):
+        wide_pos = lax.axis_index("wide")
+        other = r_ref[:, cols : cols + 64].astype(jnp.float32)
+        small = small_ref[...] + (other[:, :32] + other[:, 32:64])
         scale = lax.rsqrt(small[:, entries : entries + 1] / MODEL_WIDTH + 1e-05)
         shrink = (small * scale).astype(jnp.bfloat16)
         lane = lax.broadcasted_iota(jnp.int32, (count, lanes), 1)
-        owner = place_ref[1] ^ (((lane >> 4) & 3) * 4 + (lane >> 6) * 2 + ((lane >> 3) & 1))
+        owner = wide_pos ^ (((lane >> 3) & 3) * 4 + ((lane >> 5) & 1) * 2 + (lane >> 6))
         hit = slot_ref[...] == owner
         entry = lax.broadcasted_iota(jnp.int32, (32, lanes), 0)
         to = lax.broadcasted_iota(jnp.int32, (32, lanes), 1) & (rank - 1)
@@ -414,15 +424,13 @@
             value = jnp.dot(shrink, chosen, preferred_element_type=jnp.float32)
             return jnp.where(hit, value, 0.0).astype(jnp.bfloat16)
 
-        last = place_ref[0] == 1
+        last = (wide_pos & 1) == 1
         parts = [spread(t) for t in range(3)]
         cut = cols - 2 * lanes
         spans = ((0, cut, parts[0]), (cut, cut + lanes, parts[1]), (cut + lanes, cols, parts[2]))
         for lo, hi, own in spans:
             left = parts[0] if lo == 0 else jnp.where(last, own, parts[0])
-            up = jnp.concatenate(
-                [near_ref[dz, :, lo:hi] for dz in range(4)] + [far_ref[:, lo:hi]], axis=0
-            )
+            up = jnp.concatenate([ref[:, lo:hi] for ref in (a_ref, b_ref, c_ref, d_ref)], axis=0)
             change = jnp.dot(left, up, preferred_element_type=jnp.float32)
             base = p_ref[:, lo:hi] + r_ref[:, lo:hi].astype(jnp.float32)
             acc_ref[:, lo:hi] = base * scale + adapter_scale * change
@@ -434,70 +442,196 @@
 
     return pl.pallas_call(
         kernel,
-        in_specs=[SCALARS] + [WHOLE] * 6,
+        in_specs=[WHOLE] * 8,
         out_specs=WHOLE,
         out_shape=jax.ShapeDtypeStruct((4, blocks, each, lanes), jnp.bfloat16),
         scratch_shapes=[pltpu.VMEM((count, cols), jnp.float32)],
         compiler_params=pltpu.CompilerParams(vmem_limit_bytes=12 * 2**20),
-    )(place, partial, small, received, near, far, slot)
-
-
-def in_order(groups, order, downs, mine):
+    )(partial, small, received, *ups, slot)
+
+
+def strided_rows(wide_ref, rows_ref, order):
+    pieces, tall, lanes = wide_ref.shape
+    count, depth = rows_ref.shape
+    blocks = depth // lanes
+    for at, piece in order:
+        wide_ref[at] = piece.astype(jnp.float32)
+    flat = wide_ref.reshape(count * blocks, lanes)
+    for j in range(blocks):
+        rows_ref[:, j * lanes : (j + 1) * lanes] = flat[
+            pl.ds(j, count, stride=blocks), :
+        ].astype(rows_ref.dtype)
+
+
+def ordered_product(groups, order, weight, stop, rows):
     pieces, tall, lanes = groups[0].shape
-    entries, depth = downs[0].shape
-    blocks = depth // lanes
-    count = 4 * pieces * (tall // blocks)
-
-    def kernel(
-        order_ref, a_ref, b_ref, c_ref, d_ref, near_ref, far_ref, mine_ref, rows_ref, small_ref,
-        wide_ref,
-    ):
-        for g, ref in enumerate((a_ref, b_ref, c_ref, d_ref)):
-            for p in range(pieces):
-                wide_ref[order_ref[g * pieces + p]] = ref[p].astype(jnp.float32)
-        flat = wide_ref.reshape(count * blocks, lanes)
-        for j in range(blocks):
-            rows_ref[:, j * lanes : (j + 1) * lanes] = flat[
-                pl.ds(j, count, stride=blocks), :
-            ].astype(rows_ref.dtype)
-        near, far = [
-            lax.dot_general(
+    depth, cols = weight.shape
+    count = 4 * pieces * rows
+    chunk = 512
+    steps = stop // chunk
+
+    def kernel(order_ref, a_ref, b_ref, c_ref, d_ref, w_ref, rows_ref, out_ref, wide_ref, buf, sem):
+        copies = [
+            pltpu.make_async_copy(w_ref.at[pl.ds(i * chunk, chunk)], buf.at[i], sem.at[i])
+            for i in range(steps)
+        ]
+        for copy in copies:
+            copy.start()
+        placed = [
+            (order_ref[g * pieces + p], ref[p])
+            for g, ref in enumerate((a_ref, b_ref, c_ref, d_ref))
+            for p in range(pieces)
+        ]
+        strided_rows(wide_ref, rows_ref, placed)
+        total = jnp.zeros((count, cols), jnp.float32)
+        out_ref[...] = total
+
+        def body(i, carry):
+            pltpu.make_async_copy(
+                w_ref.at[pl.ds(i * chunk, chunk)], buf.at[i], sem.at[i]
+            ).wait()
+            at = pl.multiple_of(i * chunk, chunk)
+            out_ref[...] += jnp.dot(
+                rows_ref[:, pl.ds(at, chunk)], buf[i], preferred_element_type=jnp.float32
+            )
+            return carry
+
+        lax.fori_loop(0, steps, body, 0)
+
+    return pl.pallas_call(
+        kernel,
+        in_specs=[SCALARS] + [WHOLE] * 4 + [pl.BlockSpec(memory_space=pl.ANY)],
+        out_specs=[WHOLE, WHOLE],
+        out_shape=[
+            jax.ShapeDtypeStruct((count, depth), groups[0].dtype),
+            jax.ShapeDtypeStruct((count, cols), jnp.float32),
+        ],
+        scratch_shapes=[
+            pltpu.VMEM((4 * pieces, tall, lanes), jnp.float32),
+            pltpu.VMEM((steps, chunk, cols), weight.dtype),
+            pltpu.SemaphoreType.DMA((steps,)),
+        ],
+        cost_estimate=pl.CostEstimate(
+            flops=2 * count * cols * stop, bytes_accessed=2 * cols * stop, transcendentals=0
+        ),
+        compiler_params=pltpu.CompilerParams(vmem_limit_bytes=48 * 2**20),
+    )(order, *groups, weight)
+
+
+def pack_o_z(place, slot, pieces, downs, up, rows):
+    count, tall, lanes = pieces.shape
+    rank, depth = downs[0].shape
+    span = up.shape[1] // count
+    total = count * rows
+
+    def kernel(place_ref, slot_ref, p_ref, *refs):
+        down_refs, up_ref = refs[:4], refs[4]
+        out_refs, (wide_ref, rows_ref) = refs[5:9], refs[9:]
+        placed = [(place_ref[2] ^ dz, p_ref[dz]) for dz in range(count)]
+        strided_rows(wide_ref, rows_ref, placed)
+        at = lax.broadcasted_iota(jnp.int32, (total, 1), 0)
+        slots = jnp.zeros((total, 1), jnp.int32)
+        for r in range(total):
+            row = (r // rows * 4 + place_ref[3] * 2 + place_ref[0]) * rows + r % rows
+            slots = jnp.where(at == r, slot_ref[row], slots)
+        out = jnp.zeros((total, rank), jnp.float32)
+        for offset, ref in enumerate(down_refs):
+            part = lax.dot_general(
                 rows_ref[...], ref[...], (((1,), (1,)), ((), ())),
                 preferred_element_type=jnp.float32,
             )
-            for ref in (near_ref, far_ref)
-        ]
-        small_ref[...] = near * mine_ref[:, :1] + far * mine_ref[:, 1:]
+            out = out + jnp.where(slots == (place_ref[1] ^ offset), part, 0.0)
+        for dz, ref in enumerate(out_refs):
+            at = pl.multiple_of((place_ref[2] ^ dz) * span, lanes)
+            ref[:, :span] = up_ref[:, pl.ds(at, span)]
+            ref[:, span:] = jnp.zeros((rank, lanes), ref.dtype)
+            for rows_at, at in ((0, span), (rank, span + lanes // 2)):
+                left = out[rows_at : min(rows_at + rank, total)]
+                for t in range(2):
+                    top = left.astype(jnp.bfloat16)
+                    ref[: left.shape[0], at + t * rank : at + (t + 1) * rank] = top
+                    left = left - top.astype(jnp.float32)
 
     return pl.pallas_call(
         kernel,
-        in_specs=[SCALARS] + [WHOLE] * 7,
-        out_specs=[WHOLE, WHOLE],
-        out_shape=[
-            jax.ShapeDtypeStruct((count, depth), groups[0].dtype),
-            jax.ShapeDtypeStruct((count, entries), jnp.float32),
+        in_specs=[SCALARS, SCALARS] + [WHOLE] * 6,
+        out_specs=[WHOLE] * 4,
+        out_shape=[jax.ShapeDtypeStruct((rank, span + lanes), up.dtype)] * 4,
+        scratch_shapes=[
+            pltpu.VMEM((count, tall, lanes), jnp.float32),
+            pltpu.VMEM((total, depth), pieces.dtype),
         ],
-        scratch_shapes=[pltpu.VMEM((4 * pieces, tall, lanes), jnp.float32)],
         cost_estimate=pl.CostEstimate(
-            flops=0, bytes_accessed=4 * count * depth, transcendentals=0
+            flops=0, bytes_accessed=4 * total * depth, transcendentals=0
         ),
         compiler_params=pltpu.CompilerParams(vmem_limit_bytes=10 * 2**20),
-    )(order, *groups, *downs, mine)
-
-
-def in_three(v):
-    out = []
-    for _ in range(3):
-        top = lax.reduce_precision(v, 8, 7)
-        out.append(top.astype(jnp.bfloat16))
-        v = v - top
-    return jnp.concatenate(out, axis=1)
-
-
-def from_three(v):
-    n = v.shape[1] // 3
+    )(place, slot, pieces, *downs, up)
+
+
+def pack_o_y(place, parts, total):
+    rank = parts[0].shape[0]
+    lanes = 128
+    span = (parts[0].shape[1] - lanes) // 2
+
+    def kernel(place_ref, a_ref, b_ref, c_ref, d_ref, away_ref, keep_ref, sum_ref):
+        refs = (a_ref, b_ref, c_ref, d_ref)
+
+        def decoded(ref, rows, at):
+            high, low = [
+                ref[rows, at + t * rank : at + (t + 1) * rank].astype(jnp.float32)
+                for t in range(2)
+            ]
+            return high + low
+
+        for at, rows in (
+            (0, slice(0, rank)),
+            (lanes // 2, slice(0, total - rank)),
+        ):
+            parts_of = [decoded(ref, rows, 2 * span + at) for ref in refs]
+            value = (parts_of[0] + parts_of[1]) + (parts_of[2] + parts_of[3])
+            sum_ref[pl.ds(0 if at == 0 else rank, value.shape[0]), :] = value
+        away_ref[:, span:] = jnp.zeros((4 * rank, lanes), away_ref.dtype)
+        left = sum_ref[...]
+        for t in range(2):
+            top = left.astype(jnp.bfloat16)
+            away_ref[:total, span + t * rank : span + (t + 1) * rank] = top
+            left = left - top.astype(jnp.float32)
+
+        def write(yb):
+            for dz, ref in enumerate(refs):
+                rows = slice(dz * rank, (dz + 1) * rank)
+                keep_ref[rows, :] = ref[:, yb * span : (yb + 1) * span]
+                away_ref[rows, :span] = ref[:, (1 - yb) * span : (2 - yb) * span]
+
+        for yb in range(2):
+
+            @pl.when(place_ref[3] == yb)
+            def _():
+                write(yb)
+
+    dtype = parts[0].dtype
+    return pl.pallas_call(
+        kernel,
+        in_specs=[SCALARS] + [WHOLE] * 4,
+        out_specs=[WHOLE] * 3,
+        out_shape=[
+            jax.ShapeDtypeStruct((4 * rank, span + lanes), dtype),
+            jax.ShapeDtypeStruct((4 * rank, span), dtype),
+            jax.ShapeDtypeStruct((total, rank), jnp.float32),
+        ],
+        compiler_params=pltpu.CompilerParams(vmem_limit_bytes=8 * 2**20),
+    )(place, *parts)
+
+
+def in_two(v):
+    top = lax.reduce_precision(v, 8, 7)
+    return jnp.concatenate([top, v - top], axis=1).astype(jnp.bfloat16)
+
+
+def from_two(v):
+    n = v.shape[1] // 2
     v = v.astype(jnp.float32)
-    return (v[:, :n] + v[:, n : 2 * n]) + v[:, 2 * n :]
+    return v[:, :n] + v[:, n:]
 
 
 def staged_path(
@@ -551,31 +685,42 @@
     half = batch // 2
     place = jnp.stack([core, wide_pos, z, y])
 
-    owned = (joint_down_weight[0].T, query_up_weight[0], key_value_up_weight[0])
     gain = input_norm_gain[None]
     same, flip, small, slot, mine = prepare(
-        place,
         hidden_input,
         gain,
-        owned,
-        tuple(swap(v, 1) for v in owned),
+        joint_down_weight[0].T,
+        query_up_weight[0],
+        key_value_up_weight[0],
         row_adapter_index[None],
         adapter_owner_slot,
-        cols,
     )
     parts = [same, swap(flip, 4), swap(same, 8), swap(flip, 12)]
     depth = hidden_input.shape[1]
     cut = depth * 5 // 8
     weight = joint_projection_weight
     partial = stream_product(hidden_input, gain, weight, 0, cut, None, same)
-    away, ups, small = pack_y(place, parts, small, cols)
+    away, ups_near, ups_far, small = pack_y(parts, small, cols)
     away, partial = lax.optimization_barrier((away, partial))
     from_y = swap(away, 2)
     partial = stream_product(hidden_input, gain, weight, cut, depth, partial, away)
-    small = small + from_three(from_y[:batch, cols : cols + 96])
-    message = jnp.concatenate([partial.astype(bf16), in_three(small)], axis=1)
+    partial, from_y = lax.optimization_barrier((partial, from_y))
+    coded = from_y[:, 2 * cols :].reshape(2, 16, 2, 64).transpose(2, 0, 1, 3).reshape(-1, 64)
+    small = small + from_two(coded[:batch])
+    small = small + swap(small, 1)
+    ups_y = from_y[:, : 2 * cols].reshape(-1, 2, cols)
+    ups = (
+        ups_near,
+        pick(ups_y, core, 1),
+        swap(ups_far, 1),
+        swap(pick(ups_y, 1 - core, 1), 1),
+    )
+    message = jnp.concatenate([partial.astype(bf16), in_two(small)], axis=1)
+    o_down = output_down_weight[0].T
+    message, o_down = lax.optimization_barrier((message, o_down))
     from_x = swap(message, 16, target=True)
-    merged = merge(place, partial, small, from_x, ups, from_y, slot)
+    o_down_y = swap(o_down, 2)
+    merged = merge(partial, small, from_x, ups, slot)
 
     to = [pick(merged, z ^ d) for d in range(4)]
     from_1 = swap(to[1], 4, source=True)
@@ -621,49 +766,44 @@
 
     near = jnp.stack([attended, swap(attended, 4), swap(attended, 8), swap(attended, 12)])
     near_y = swap(near, 2)
+    o_downs = (o_down, swap(o_down, 1), o_down_y, swap(o_down_y, 1))
+    o_z = pack_o_z(place, slot[:, 0], near, o_downs, output_up_weight[0], rows)
+    near_y, o_z = lax.optimization_barrier((near_y, o_z))
+    from_z = [swap(o_z[1], 4), swap(o_z[2], 8), swap(o_z[3], 12)]
     far, far_y = swap(near, 1), swap(near_y, 1)
     offsets = [
         dz * 4 + dy * 2 + dcore for dcore in range(2) for dy in range(2) for dz in range(4)
     ]
     order = wide_pos ^ jnp.array(offsets, jnp.int32)
-    o_down = output_down_weight[0].T
-    everyone, o_reduced = in_order(
-        (near, near_y, far, far_y), order, (o_down, swap(o_down, 1)), mine
-    )
-
-    o_sheet = output_up_weight[0].reshape(rank, 4, 2, 2, out_cols).transpose(3, 1, 2, 0, 4)
-    o_pair = jnp.concatenate([pick(o_sheet, core), swap(pick(o_sheet, 1 - core), 1)], axis=2)
-    o_pair = o_pair.reshape(4, 4 * rank, out_cols)
-    o_extra = 3 * batch // 4
-    coded = jnp.broadcast_to(
-        in_three(o_reduced).reshape(4 * rank, o_extra)[None], (4, 4 * rank, o_extra)
-    )
-    o_pair = jnp.concatenate([o_pair, coded], axis=2)
-    from_z = [swap(pick(o_pair, z ^ d), 4 * d) for d in range(1, 4)]
-    mixed = stream_product(everyone, None, output_weight, 0, cut, None, o_pair)
-    sums = [from_three(v[:, out_cols:].reshape(batch, 3 * rank)) for v in from_z]
-    o_reduced = (o_reduced + sums[0]) + (sums[1] + sums[2])
-    o_ups = jnp.stack([pick(o_pair, z)] + from_z)[:, :, :out_cols]
-    o_ups = o_ups.reshape(4, 2, 2 * rank, out_cols)
-    coded = in_three(o_reduced).reshape(8 * rank, -1)
-    away = pick(o_ups, 1 - y, 1).reshape(8 * rank, out_cols)
-    away = jnp.concatenate([away, coded], axis=1)
-    away, mixed = lax.optimization_barrier((away, mixed))
-    from_y = swap(away, 2)
-    mixed = stream_product(everyone, None, output_weight, cut, depth, mixed, away)
-    o_reduced = o_reduced + from_three(from_y[:, out_cols:].reshape(batch, 3 * rank))
+    first, second = depth * 3 // 8, depth * 3 // 4
+    everyone, mixed = ordered_product(
+        (near, near_y, far, far_y), order, output_weight, first, rows
+    )
+    mixed, from_z = lax.optimization_barrier((mixed, from_z))
+    o_away, o_keep, o_rows = pack_o_y(place, [o_z[0]] + from_z, 4 * rows)
+    o_far = swap(o_away, 2)
+    mixed = stream_product(everyone, None, output_weight, first, second, mixed, o_away)
+    mixed, o_far = lax.optimization_barrier((mixed, o_far))
+    o_rows = jnp.stack([o_rows, from_two(o_far[: 4 * rows, 2 * out_cols :][:, : 2 * rank])])
+    o_up = jnp.concatenate([o_keep, o_far[:, : 2 * out_cols]], axis=0)
+    o_up = o_up.reshape(8 * rank, 2, out_cols)
+    o_up_c = swap(pick(o_up, 1 - core, 1), 1)
+    o_rows_c = swap(o_rows, 1)
+    mixed = stream_product(everyone, None, output_weight, second, depth, mixed, o_rows)
+    o_up = jnp.concatenate([pick(o_up, core, 1), o_up_c], axis=0)
+    o_rows = jnp.stack([o_rows, o_rows_c], axis=1)
+    o_rows = jnp.where(y == 0, o_rows, o_rows[::-1])
+    o_rows = jnp.where(core == 0, o_rows, o_rows[:, ::-1])
+    o_rows = o_rows.reshape(2, 2, 4, rows, rank).transpose(2, 0, 1, 3, 4).reshape(batch, rank)
 
     keep_out = lax.dynamic_slice_in_dim(mixed, kv_pos * half, half)
     give_out = lax.dynamic_slice_in_dim(mixed, (1 - kv_pos) * half, half).astype(bf16)
-    o_keep = lax.dynamic_slice_in_dim(o_reduced, kv_pos * half, half)
-    o_give = in_three(lax.dynamic_slice_in_dim(o_reduced, (1 - kv_pos) * half, half))
+    o_keep = lax.dynamic_slice_in_dim(o_rows, kv_pos * half, half)
+    o_give = in_two(lax.dynamic_slice_in_dim(o_rows, (1 - kv_pos) * half, half))
     from_x = swap(jnp.concatenate([give_out, o_give], axis=1), 16)
-    o_far = from_y[:, :out_cols]
-    o_near = pick(o_ups, y, 1).reshape(8 * rank, out_cols)
-    o_up = jnp.concatenate([o_near, o_far], axis=0)
-    o_keep = o_keep + from_three(from_x[:, out_cols:])
+    o_keep = o_keep + from_two(from_x[:, out_cols:])
     lane = jnp.arange(wide, dtype=jnp.int32)
-    owner = wide_pos ^ (((lane >> 1) & 3) * 4 + (lane >> 3) * 2 + (lane & 1))
+    owner = wide_pos ^ ((lane & 3) * 4 + ((lane >> 2) & 1) * 2 + (lane >> 3))
     slot_o = lax.dynamic_slice_in_dim(slot, kv_pos * half, half)
     hit = slot_o == owner[None, :]
     shrink = jnp.where(hit[:, :, None], o_keep.astype(bf16)[:, None, :], 0).reshape(half, -1)

time: 94 us -> 88.6 us (0.943)
  waiting for transfers between devices: 25.8 us -> 19.7 us
  other arithmetic: 4.99 us -> 2.7 us
  Pallas kernels: 22.9 us -> 24.8 us
  local copies, waits for them, and re-layouts: 2.77 us -> 4.21 us
    ppermute x26 -> x29, waiting for transfers between devices: 25.8 us -> 19.7 us  [swap(): return lax.ppermute(x, ('kv', 'wide'), pairs)]
    pallas_call x4 -> x6, Pallas kernels: 7.12 us -> 10.9 us  [the longest x1 3.69 us: ordered_product(): pl.pallas_call(kernel, in_specs=[SCALARS] + [WHOLE] * 4 + [pl.BlockSpec(m...]
    concatenate x6 -> x1, other arithmetic: 2.83 us -> 0.02 us  [staged_path(): o_up = jnp.concatenate([o_keep, o_far[:, :2 * out_cols]], axis=0)]
    pallas_call x4, Pallas kernels: 15.8 us -> 13.9 us  [stream_product(): pl.pallas_call(kernel, in_specs=specs, out_specs=WHOLE, out_shape=jax.Sha...]
    unnamed x32 -> x30, local copies, waits for them, and re-layouts: 1.73 us -> 2.49 us
    ppermute x26 -> x29, starting transfers between devices: 34.6 us -> 34.1 us  [swap(): return lax.ppermute(x, ('kv', 'wide'), pairs)]
  transfers between devices with their start and end apart: 26 -> 29, of which waited for: 15 -> 16; matrix products, arithmetic and copies ran while one was open for 5% -> 4% of each run, Pallas kernels for 18% -> 22%
where the time goes in v3:
time: 88.6 us; the launch traced here: 88.2 us
  starting transfers between devices  34.1 us (38%)
  Pallas kernels  24.8 us (28%)
  waiting for transfers between devices  19.7 us (22%)
  local copies, waits for them, and re-layouts  4.21 us (5%)
  other arithmetic  2.7 us (3%)
  matrix products  2.04 us (2%)
    ppermute x29, starting transfers between devices, swap(): return lax.ppermute(x, ('kv', 'wide'), pairs)  34.1 us
    ppermute x29, waiting for transfers between devices, swap(): return lax.ppermute(x, ('kv', 'wide'), pairs)  19.7 us
    pallas_call x4, Pallas kernels, stream_product(): pl.pallas_call(kernel, in_specs=specs, out_specs=WHOLE, out_shape=jax.Sha...  13.9 us
    pallas_call x1, Pallas kernels, ordered_product(): pl.pallas_call(kernel, in_specs=[SCALARS] + [WHOLE] * 4 + [pl.BlockSpec(m...  3.69 us
    pallas_call x1, Pallas kernels, prepare(): pl.pallas_call(kernel, in_specs=[SCALARS, WHOLE] + [pl.BlockSpec(memory_s...  3.4 us
    unnamed x30, local copies, waits for them, and re-layouts  2.49 us
    pallas_call x1, Pallas kernels, pack_o_z(): pl.pallas_call(kernel, in_specs=[SCALARS, SCALARS] + [WHOLE] * 6, out_spe...  1.99 us
  transfers between devices with their start and end apart: 29, of which 16 were waited for; matrix products, arithmetic and copies ran while one was open for 4% of the time, Pallas kernels for 22%

profile of v3, /device:TPU:0, one launch (start us, length us, event | category | flops | bytes accessed | tf_op | source)
XLA Modules:
  0.0 88.2 jit_solution(10174839862126963170)
XLA Ops:
  0.0 3.4 %shard_map.145 = (bf16[16,2560]{1,0:T(8,128)(2,1)}, bf16[16,2560]{1,0:T(8,128)(2,1)}, f32[48,32]{1,0:T(8,128)}, s32[48,1]{1,0:T(8,128)}, f32[48,1]{1,0:T(8,128)}) custom-call(s32[16]{0:T(128)} %owner_ref.1, s32[1,48]{1,0:T(1,128)} %bitcast.109, bf16[48,8192]{1,0:T(8,128)(2,1)} %refs_0_.3, f32[1,8192]{1,0:T(1,128)} %bitcast.78, bf16[24,8192]{1,0:T(8,128)(2,1)} %bitcast.87, ...), custom_call_target="tpu_custom_call" | custom-call | tf_op jit(solution)/shard_map/pallas_call | solution.py:276
  3.4 5.1 %collective-permute-start.2 = (bf16[16,2560]{1,0:T(8,128)(2,1)}, bf16[16,2560]{1,0:T(8,128)(2,1)S(1)}, u32[]{:S(2)}, u32[]{:S(2)}) collective-permute-start(bf16[16,2560]{1,0:T(8,128)(2,1)} %get-tuple-element.40), channel_id=1, source_target_pairs={{0,12},{1,13},{2,14},{3,15},{4,8},{5,9},{6,10},{7,11},{8,4},{9,5},... | collective-permute-start | bytes 245768 | tf_op jit(solution)/shard_map/ppermute | solution.py:680
  10.9 4.8 %shard_map.147.refs_4_ = f32[48,1152]{1,0:T(8,128)S(1)} custom-call(bf16[48,8192]{1,0:T(8,128)(2,1)S(1)} %copy-done.1, bf16[8192,1152]{1,0:T(8,128)(2,1)} %refs_1_.5, bf16[16,2560]{1,0:T(8,128)(2,1)S(1)} %copy-done.2, f32[1,8192]{1,0:T(1,128)S(1)} %bitcast.79), custom_call_target="tpu_custom_call" | custom-call | flops 566231040 | bytes 11796480 | tf_op jit(solution)/shard_map/pallas_call | solution.py:331
  16.0 1.7 %collective-permute-start.3 = (bf16[32,2432]{1,0:T(8,128)(2,1)S(1)}, bf16[32,2432]{1,0:T(8,128)(2,1)S(1)}, u32[]{:S(2)}, u32[]{:S(2)}) collective-permute-start(bf16[32,2432]{1,0:T(8,128)(2,1)S(1)} %get-tuple-element.43.refs_2_), channel_id=1, source_target_pairs={{0,2},{1,3},{2,0},{3,1},{4,6},{5,7},{6,4},{7,5},{8,10},{9,11},{10,... | collective-permute-start | bytes 466952 | tf_op jit(solution)/shard_map/ppermute | solution.py:680
  17.7 3.4 %shard_map.148.p_ref = f32[48,1152]{1,0:T(8,128)S(1)} custom-call(bf16[48,8192]{1,0:T(8,128)(2,1)S(1)} %copy-done.1, bf16[8192,1152]{1,0:T(8,128)(2,1)} %refs_1_.5, bf16[32,2432]{1,0:T(8,128)(2,1)S(1)} %get-tuple-element.43.refs_2_, f32[1,8192]{1,0:T(1,128)S(1)} %bitcast.80, f32[48,1152]{1,0:T(8,128)S(1)} %shard_map.147.refs_4_), custom_call_target="tpu_custom_call" | custom-call | flops 339738624 | bytes 7077888 | tf_op jit(solution)/shard_map/pallas_call | solution.py:331
  22.8 1.3 %collective-permute-start.5 = (bf16[48,1216]{1,0:T(8,128)(2,1)S(1)}, bf16[48,1216]{1,0:T(8,128)(2,1)S(1)}, u32[]{:S(2)}, u32[]{:S(2)}) collective-permute-start(bf16[48,1216]{1,0:T(8,128)(2,1)S(1)} %concatenate.34), channel_id=1, source_target_pairs={{8,24},{9,25},{10,26},{11,27},{12,28},{13,29},{14,30},{15,31},{16,... | collective-permute-start | bytes 350216 | tf_op jit(solution)/shard_map/ppermute | solution.py:680
  25.7 4.3 %collective-permute-done.5.r_ref = bf16[48,1216]{1,0:T(8,128)(2,1)S(1)} collective-permute-done((bf16[48,1216]{1,0:T(8,128)(2,1)S(1)}, bf16[48,1216]{1,0:T(8,128)(2,1)S(1)}, u32[]{:S(2)}, u32[]{:S(2)}) %collective-permute-start.5) | collective-permute-done | bytes 116768 | tf_op jit(solution)/shard_map/ppermute | solution.py:680
  30.5 4.7 %collective-permute-start.10 = (bf16[9,12,128]{2,1,0:T(8,128)(2,1)S(1)}, bf16[9,12,128]{2,1,0:T(8,128)(2,1)S(1)}, u32[]{:S(2)}, u32[]{:S(2)}) collective-permute-start(bf16[9,12,128]{2,1,0:T(8,128)(2,1)S(1)} %get-tuple-element.83), channel_id=1, source_target_pairs={{0,12},{1,13},{2,14},{3,15},{4,8},{5,9},{6,10},{7,11},{24,20},{25,... | collective-permute-start | bytes 82952 | tf_op jit(solution)/shard_map/ppermute | solution.py:680
  35.2 1.9 %collective-permute-start.9 = (bf16[9,12,128]{2,1,0:T(8,128)(2,1)S(1)}, bf16[9,12,128]{2,1,0:T(8,128)(2,1)S(1)}, u32[]{:S(2)}, u32[]{:S(2)}) collective-permute-start(bf16[9,12,128]{2,1,0:T(8,128)(2,1)S(1)} %get-tuple-element.84), channel_id=1, source_target_pairs={{0,4},{1,5},{2,6},{3,7},{4,0},{5,1},{6,2},{7,3},{24,28},{25,29},{2... | collective-permute-start | bytes 82952 | tf_op jit(solution)/shard_map/ppermute | solution.py:680
  37.2 1.3 %collective-permute-start.8 = (bf16[9,12,128]{2,1,0:T(8,128)(2,1)S(1)}, bf16[9,12,128]{2,1,0:T(8,128)(2,1)S(1)}, u32[]{:S(2)}, u32[]{:S(2)}) collective-permute-start(bf16[9,12,128]{2,1,0:T(8,128)(2,1)S(1)} %get-tuple-element.85), channel_id=1, source_target_pairs={{0,8},{1,9},{2,10},{3,11},{4,12},{5,13},{6,14},{7,15},{24,16},{25,... | collective-permute-start | bytes 82952 | tf_op jit(solution)/shard_map/ppermute | solution.py:680
  38.5 2.6 %collective-permute-done.9 = bf16[9,12,128]{2,1,0:T(8,128)(2,1)S(1)} collective-permute-done((bf16[9,12,128]{2,1,0:T(8,128)(2,1)S(1)}, bf16[9,12,128]{2,1,0:T(8,128)(2,1)S(1)}, u32[]{:S(2)}, u32[]{:S(2)}) %collective-permute-start.9) | collective-permute-done | bytes 27680 | tf_op jit(solution)/shard_map/ppermute | solution.py:680
  41.1 1.6 %collective-permute-start.11 = (bf16[2,9,6,128]{3,2,1,0:T(8,128)(2,1)S(1)}, bf16[2,9,6,128]{3,2,1,0:T(8,128)(2,1)S(1)}, u32[]{:S(2)}, u32[]{:S(2)}) collective-permute-start(bf16[2,9,6,128]{3,2,1,0:T(8,128)(2,1)S(1)} %fusion.10), channel_id=1, source_target_pairs={{0,2},{1,3},{2,0},{3,1},{4,6},{5,7},{6,4},{7,5},{8,10},{9,11},{10,... | collective-permute-start | bytes 82952 | tf_op jit(solution)/shard_map/ppermute | solution.py:680
  42.8 2.3 %collective-permute-done.11 = bf16[2,9,6,128]{3,2,1,0:T(8,128)(2,1)S(1)} collective-permute-done((bf16[2,9,6,128]{3,2,1,0:T(8,128)(2,1)S(1)}, bf16[2,9,6,128]{3,2,1,0:T(8,128)(2,1)S(1)}, u32[]{:S(2)}, u32[]{:S(2)}) %collective-permute-start.11) | collective-permute-done | bytes 27680 | tf_op jit(solution)/shard_map/ppermute | solution.py:680
  48.7 3.7 %collective-permute-start.15 = (bf16[192,128]{1,0:T(8,128)(2,1)S(1)}, bf16[192,128]{1,0:T(8,128)(2,1)S(1)}, u32[]{:S(2)}, u32[]{:S(2)}) collective-permute-start(bf16[192,128]{1,0:T(8,128)(2,1)S(1)} %bitcast.97), channel_id=1, source_target_pairs={{0,12},{1,13},{2,14},{3,15},{4,8},{5,9},{6,10},{7,11},{8,4},{9,5},... | collective-permute-start | bytes 147464 | tf_op jit(solution)/shard_map/ppermute | solution.py:680
  53.1 1.5 %collective-permute-start.18 = (bf16[8,8192]{1,0:T(8,128)(2,1)S(1)}, bf16[8,8192]{1,0:T(8,128)(2,1)S(1)}, u32[]{:S(2)}, u32[]{:S(2)}) collective-permute-start(bf16[8,8192]{1,0:T(8,128)(2,1)S(1)} %bitcast.83), channel_id=1, source_target_pairs={{0,2},{1,3},{2,0},{3,1},{4,6},{5,7},{6,4},{7,5},{8,10},{9,11},{10,... | collective-permute-start | bytes 393224 | tf_op jit(solution)/shard_map/ppermute | solution.py:680
  54.9 2.6 %collective-permute-done.14 = bf16[192,128]{1,0:T(8,128)(2,1)S(1)} collective-permute-done((bf16[192,128]{1,0:T(8,128)(2,1)S(1)}, bf16[192,128]{1,0:T(8,128)(2,1)S(1)}, u32[]{:S(2)}, u32[]{:S(2)}) %collective-permute-start.14) | collective-permute-done | bytes 49184 | tf_op jit(solution)/shard_map/ppermute | solution.py:680
  57.6 1.6 %collective-permute-start.16 = (bf16[4,192,128]{2,1,0:T(8,128)(2,1)S(1)}, bf16[4,192,128]{2,1,0:T(8,128)(2,1)S(1)}, u32[]{:S(2)}, u32[]{:S(2)}) collective-permute-start(bf16[4,192,128]{2,1,0:T(8,128)(2,1)S(1)} %pad_maximum_fusion.1.p_ref.a_ref), channel_id=1, source_target_pairs={{0,2},{1,3},{2,0},{3,1},{4,6},{5,7},{6,4},{7,5},{8,10},{9,11},{10,... | collective-permute-start | bytes 589832 | tf_op jit(solution)/shard_map/ppermute | solution.py:680
  60.7 2.0 %shard_map.150 = (bf16[8,4224]{1,0:T(8,128)(2,1)S(1)}, bf16[8,4224]{1,0:T(8,128)(2,1)}, bf16[8,4224]{1,0:T(8,128)(2,1)}, bf16[8,4224]{1,0:T(8,128)(2,1)}) custom-call(s32[4]{0:T(128)S(1)} %pad_add_fusion.place_ref, s32[48]{0:T(128)S(1)} %reduce.slot_ref, bf16[4,192,128]{2,1,0:T(8,128)(2,1)S(1)} %pad_maximum_fusion.1.p_ref.a_ref, ...), custom_call_target="tpu_custom_call" | custom-call | bytes 393216 | tf_op jit(solution)/shard_map/pallas_call | solution.py:555
  64.8 2.3 %collective-permute-start.23 = (bf16[8,4224]{1,0:T(8,128)(2,1)}, bf16[8,4224]{1,0:T(8,128)(2,1)S(1)}, u32[]{:S(2)}, u32[]{:S(2)}) collective-permute-start(bf16[8,4224]{1,0:T(8,128)(2,1)} %get-tuple-element.62), channel_id=1, source_target_pairs={{0,8},{1,9},{2,10},{3,11},{4,12},{5,13},{6,14},{7,15},{8,0},{9,1},... | collective-permute-start | bytes 202760 | tf_op jit(solution)/shard_map/ppermute | solution.py:680
  69.6 3.7 %shard_map.151 = (bf16[48,8192]{1,0:T(8,128)(2,1)S(1)}, f32[48,1024]{1,0:T(8,128)S(1)}) custom-call(s32[16]{0:T(128)S(1)} %copy-done.8, bf16[4,192,128]{2,1,0:T(8,128)(2,1)S(1)} %pad_maximum_fusion.1.p_ref.a_ref, bf16[4,192,128]{2,1,0:T(8,128)(2,1)S(1)} %collective-permute-done.16.b_ref, bf16[4,192,128]{2,1,0:T(8,128)(2,1)S(1)} %collective-permute-done.20.c_ref, ...), custom_call_target="tpu_custom_call" | custom-call | flops 301989888 | bytes 6291456 | tf_op jit(solution)/shard_map/pallas_call | solution.py:501
  74.7 1.6 %collective-permute-start.25 = (bf16[32,2176]{1,0:T(8,128)(2,1)S(1)}, bf16[32,2176]{1,0:T(8,128)(2,1)S(1)}, u32[]{:S(2)}, u32[]{:S(2)}) collective-permute-start(bf16[32,2176]{1,0:T(8,128)(2,1)S(1)} %get-tuple-element.68.refs_2_), channel_id=1, source_target_pairs={{0,2},{1,3},{2,0},{3,1},{4,6},{5,7},{6,4},{7,5},{8,10},{9,11},{10,... | collective-permute-start | bytes 417800 | tf_op jit(solution)/shard_map/ppermute | solution.py:680
  76.4 3.2 %shard_map.153.refs_3_ = f32[48,1024]{1,0:T(8,128)S(1)} custom-call(bf16[48,8192]{1,0:T(8,128)(2,1)S(1)} %get-tuple-element.58.refs_0_, bf16[8192,1024]{1,0:T(8,128)(2,1)} %refs_1_.7, bf16[32,2176]{1,0:T(8,128)(2,1)S(1)} %get-tuple-element.68.refs_2_, f32[48,1024]{1,0:T(8,128)S(1)} %get-tuple-element.69.refs_3_), custom_call_target="tpu_custom_call" | custom-call | flops 301989888 | bytes 6291456 | tf_op jit(solution)/shard_map/pallas_call | solution.py:331
  79.9 2.5 %shard_map.154 = f32[48,1024]{1,0:T(8,128)S(1)} custom-call(bf16[48,8192]{1,0:T(8,128)(2,1)S(1)} %get-tuple-element.58.refs_0_, bf16[8192,1024]{1,0:T(8,128)(2,1)} %refs_1_.7, f32[2,12,8]{2,1,0:T(8,128)S(1)} %get-tuple-element.95.refs_2_, f32[48,1024]{1,0:T(8,128)S(1)} %shard_map.153.refs_3_), custom_call_target="tpu_custom_call" | custom-call | flops 201326592 | bytes 4194304 | tf_op jit(solution)/shard_map/pallas_call | solution.py:331
  84.5 2.7 %collective-permute-done.27 = bf16[24,1040]{1,0:T(8,128)(2,1)S(1)} collective-permute-done((bf16[24,1040]{1,0:T(8,128)(2,1)S(1)}, bf16[24,1040]{1,0:T(8,128)(2,1)S(1)}, u32[]{:S(2)}, u32[]{:S(2)}) %collective-permute-start.27) | collective-permute-done | bytes 49952 | tf_op jit(solution)/shard_map/ppermute | solution.py:680
  (141 shorter events, 21.8 us)
Async XLA Ops:
  3.4 12.2 %collective-permute-start.2 = (bf16[16,2560]{1,0:T(8,128)(2,1)}, bf16[16,2560]{1,0:T(8,128)(2,1)S(1)}, u32[]{:S(2)}, u32[]{:S(2)}) collective-permute-start(bf16[16,2560]{1,0:T(8,128)(2,1)} %get-tuple-element.40), channel_id=1, source_target_pairs={{0,12},{1,13},{2,14},{3,15},{4,8},{5,9},{6,10},{7,11},{8,4},{9,5},... | collective-permute-start | bytes 245768 | tf_op jit(solution)/shard_map/ppermute | solution.py:680
  8.5 7.1 %collective-permute-start = (bf16[16,2560]{1,0:T(8,128)(2,1)}, bf16[16,2560]{1,0:T(8,128)(2,1)S(1)}, u32[]{:S(2)}, u32[]{:S(2)}) collective-permute-start(bf16[16,2560]{1,0:T(8,128)(2,1)} %get-tuple-element.40), channel_id=1, source_target_pairs={{0,4},{1,5},{2,6},{3,7},{4,0},{5,1},{6,2},{7,3},{8,12},{9,13},{10,... | collective-permute-start | bytes 245768 | tf_op jit(solution)/shard_map/ppermute | solution.py:680
  8.5 7.2 %collective-permute-start.1 = (bf16[16,2560]{1,0:T(8,128)(2,1)}, bf16[16,2560]{1,0:T(8,128)(2,1)S(1)}, u32[]{:S(2)}, u32[]{:S(2)}) collective-permute-start(bf16[16,2560]{1,0:T(8,128)(2,1)} %get-tuple-element.39.a_ref.refs_2_), channel_id=1, source_target_pairs={{0,8},{1,9},{2,10},{3,11},{4,12},{5,13},{6,14},{7,15},{8,0},{9,1},... | collective-permute-start | bytes 245768 | tf_op jit(solution)/shard_map/ppermute | solution.py:680
  16.0 5.3 %collective-permute-start.3 = (bf16[32,2432]{1,0:T(8,128)(2,1)S(1)}, bf16[32,2432]{1,0:T(8,128)(2,1)S(1)}, u32[]{:S(2)}, u32[]{:S(2)}) collective-permute-start(bf16[32,2432]{1,0:T(8,128)(2,1)S(1)} %get-tuple-element.43.refs_2_), channel_id=1, source_target_pairs={{0,2},{1,3},{2,0},{3,1},{4,6},{5,7},{6,4},{7,5},{8,10},{9,11},{10,... | collective-permute-start | bytes 466952 | tf_op jit(solution)/shard_map/ppermute | solution.py:680
  21.5 3.2 %collective-permute-start.6 = (bf16[32,1152]{1,0:T(8,128)(2,1)S(1)}, bf16[32,1152]{1,0:T(8,128)(2,1)S(1)}, u32[]{:S(2)}, u32[]{:S(2)}) collective-permute-start(bf16[32,1152]{1,0:T(8,128)(2,1)S(1)} %get-tuple-element.50), channel_id=1, source_target_pairs={{0,1},{1,0},{2,3},{3,2},{4,5},{5,4},{6,7},{7,6},{8,9},{9,8},{10,11... | collective-permute-start | bytes 221192 | tf_op jit(solution)/shard_map/ppermute | solution.py:680
  22.8 7.3 %collective-permute-start.5 = (bf16[48,1216]{1,0:T(8,128)(2,1)S(1)}, bf16[48,1216]{1,0:T(8,128)(2,1)S(1)}, u32[]{:S(2)}, u32[]{:S(2)}) collective-permute-start(bf16[48,1216]{1,0:T(8,128)(2,1)S(1)} %concatenate.34), channel_id=1, source_target_pairs={{8,24},{9,25},{10,26},{11,27},{12,28},{13,29},{14,30},{15,31},{16,... | collective-permute-start | bytes 350216 | tf_op jit(solution)/shard_map/ppermute | solution.py:680
  30.5 8.0 %collective-permute-start.10 = (bf16[9,12,128]{2,1,0:T(8,128)(2,1)S(1)}, bf16[9,12,128]{2,1,0:T(8,128)(2,1)S(1)}, u32[]{:S(2)}, u32[]{:S(2)}) collective-permute-start(bf16[9,12,128]{2,1,0:T(8,128)(2,1)S(1)} %get-tuple-element.83), channel_id=1, source_target_pairs={{0,12},{1,13},{2,14},{3,15},{4,8},{5,9},{6,10},{7,11},{24,20},{25,... | collective-permute-start | bytes 82952 | tf_op jit(solution)/shard_map/ppermute | solution.py:680
  35.2 5.9 %collective-permute-start.9 = (bf16[9,12,128]{2,1,0:T(8,128)(2,1)S(1)}, bf16[9,12,128]{2,1,0:T(8,128)(2,1)S(1)}, u32[]{:S(2)}, u32[]{:S(2)}) collective-permute-start(bf16[9,12,128]{2,1,0:T(8,128)(2,1)S(1)} %get-tuple-element.84), channel_id=1, source_target_pairs={{0,4},{1,5},{2,6},{3,7},{4,0},{5,1},{6,2},{7,3},{24,28},{25,29},{2... | collective-permute-start | bytes 82952 | tf_op jit(solution)/shard_map/ppermute | solution.py:680
  37.2 3.9 %collective-permute-start.8 = (bf16[9,12,128]{2,1,0:T(8,128)(2,1)S(1)}, bf16[9,12,128]{2,1,0:T(8,128)(2,1)S(1)}, u32[]{:S(2)}, u32[]{:S(2)}) collective-permute-start(bf16[9,12,128]{2,1,0:T(8,128)(2,1)S(1)} %get-tuple-element.85), channel_id=1, source_target_pairs={{0,8},{1,9},{2,10},{3,11},{4,12},{5,13},{6,14},{7,15},{24,16},{25,... | collective-permute-start | bytes 82952 | tf_op jit(solution)/shard_map/ppermute | solution.py:680
  41.1 4.0 %collective-permute-start.11 = (bf16[2,9,6,128]{3,2,1,0:T(8,128)(2,1)S(1)}, bf16[2,9,6,128]{3,2,1,0:T(8,128)(2,1)S(1)}, u32[]{:S(2)}, u32[]{:S(2)}) collective-permute-start(bf16[2,9,6,128]{3,2,1,0:T(8,128)(2,1)S(1)} %fusion.10), channel_id=1, source_target_pairs={{0,2},{1,3},{2,0},{3,1},{4,6},{5,7},{6,4},{7,5},{8,10},{9,11},{10,... | collective-permute-start | bytes 82952 | tf_op jit(solution)/shard_map/ppermute | solution.py:680
  48.7 6.2 %collective-permute-start.15 = (bf16[192,128]{1,0:T(8,128)(2,1)S(1)}, bf16[192,128]{1,0:T(8,128)(2,1)S(1)}, u32[]{:S(2)}, u32[]{:S(2)}) collective-permute-start(bf16[192,128]{1,0:T(8,128)(2,1)S(1)} %bitcast.97), channel_id=1, source_target_pairs={{0,12},{1,13},{2,14},{3,15},{4,8},{5,9},{6,10},{7,11},{8,4},{9,5},... | collective-permute-start | bytes 147464 | tf_op jit(solution)/shard_map/ppermute | solution.py:680
  52.4 5.0 %collective-permute-start.14 = (bf16[192,128]{1,0:T(8,128)(2,1)S(1)}, bf16[192,128]{1,0:T(8,128)(2,1)S(1)}, u32[]{:S(2)}, u32[]{:S(2)}) collective-permute-start(bf16[192,128]{1,0:T(8,128)(2,1)S(1)} %bitcast.98), channel_id=1, source_target_pairs={{0,8},{1,9},{2,10},{3,11},{4,12},{5,13},{6,14},{7,15},{8,0},{9,1},... | collective-permute-start | bytes 147464 | tf_op jit(solution)/shard_map/ppermute | solution.py:680
  52.4 5.1 %collective-permute-start.13 = (bf16[192,128]{1,0:T(8,128)(2,1)S(1)}, bf16[192,128]{1,0:T(8,128)(2,1)S(1)}, u32[]{:S(2)}, u32[]{:S(2)}) collective-permute-start(bf16[192,128]{1,0:T(8,128)(2,1)S(1)} %bitcast.99), channel_id=1, source_target_pairs={{0,4},{1,5},{2,6},{3,7},{4,0},{5,1},{6,2},{7,3},{8,12},{9,13},{10,... | collective-permute-start | bytes 147464 | tf_op jit(solution)/shard_map/ppermute | solution.py:680
  53.1 6.0 %collective-permute-start.18 = (bf16[8,8192]{1,0:T(8,128)(2,1)S(1)}, bf16[8,8192]{1,0:T(8,128)(2,1)S(1)}, u32[]{:S(2)}, u32[]{:S(2)}) collective-permute-start(bf16[8,8192]{1,0:T(8,128)(2,1)S(1)} %bitcast.83), channel_id=1, source_target_pairs={{0,2},{1,3},{2,0},{3,1},{4,6},{5,7},{6,4},{7,5},{8,10},{9,11},{10,... | collective-permute-start | bytes 393224 | tf_op jit(solution)/shard_map/ppermute | solution.py:680
  57.6 5.7 %collective-permute-start.16 = (bf16[4,192,128]{2,1,0:T(8,128)(2,1)S(1)}, bf16[4,192,128]{2,1,0:T(8,128)(2,1)S(1)}, u32[]{:S(2)}, u32[]{:S(2)}) collective-permute-start(bf16[4,192,128]{2,1,0:T(8,128)(2,1)S(1)} %pad_maximum_fusion.1.p_ref.a_ref), channel_id=1, source_target_pairs={{0,2},{1,3},{2,0},{3,1},{4,6},{5,7},{6,4},{7,5},{8,10},{9,11},{10,... | collective-permute-start | bytes 589832 | tf_op jit(solution)/shard_map/ppermute | solution.py:680
  59.9 9.1 %collective-permute-start.20 = (bf16[4,192,128]{2,1,0:T(8,128)(2,1)S(1)}, bf16[4,192,128]{2,1,0:T(8,128)(2,1)S(1)}, u32[]{:S(2)}, u32[]{:S(2)}) collective-permute-start(bf16[4,192,128]{2,1,0:T(8,128)(2,1)S(1)} %pad_maximum_fusion.1.p_ref.a_ref), channel_id=1, source_target_pairs={{0,1},{1,0},{2,3},{3,2},{4,5},{5,4},{6,7},{7,6},{8,9},{9,8},{10,11... | collective-permute-start | bytes 589832 | tf_op jit(solution)/shard_map/ppermute | solution.py:680
  63.3 5.6 %collective-permute-start.21 = (bf16[4,192,128]{2,1,0:T(8,128)(2,1)S(1)}, bf16[4,192,128]{2,1,0:T(8,128)(2,1)S(1)}, u32[]{:S(2)}, u32[]{:S(2)}) collective-permute-start(bf16[4,192,128]{2,1,0:T(8,128)(2,1)S(1)} %collective-permute-done.16.b_ref), channel_id=1, source_target_pairs={{0,1},{1,0},{2,3},{3,2},{4,5},{5,4},{6,7},{7,6},{8,9},{9,8},{10,11... | collective-permute-start | bytes 589832 | tf_op jit(solution)/shard_map/ppermute | solution.py:680
  63.9 9.4 %collective-permute-start.22 = (bf16[8,4224]{1,0:T(8,128)(2,1)}, bf16[8,4224]{1,0:T(8,128)(2,1)S(1)}, u32[]{:S(2)}, u32[]{:S(2)}) collective-permute-start(bf16[8,4224]{1,0:T(8,128)(2,1)} %get-tuple-element.61), channel_id=1, source_target_pairs={{0,4},{1,5},{2,6},{3,7},{4,0},{5,1},{6,2},{7,3},{8,12},{9,13},{10,... | collective-permute-start | bytes 202760 | tf_op jit(solution)/shard_map/ppermute | solution.py:680
  64.8 8.7 %collective-permute-start.23 = (bf16[8,4224]{1,0:T(8,128)(2,1)}, bf16[8,4224]{1,0:T(8,128)(2,1)S(1)}, u32[]{:S(2)}, u32[]{:S(2)}) collective-permute-start(bf16[8,4224]{1,0:T(8,128)(2,1)} %get-tuple-element.62), channel_id=1, source_target_pairs={{0,8},{1,9},{2,10},{3,11},{4,12},{5,13},{6,14},{7,15},{8,0},{9,1},... | collective-permute-start | bytes 202760 | tf_op jit(solution)/shard_map/ppermute | solution.py:680
  67.1 6.4 %collective-permute-start.24 = (bf16[8,4224]{1,0:T(8,128)(2,1)}, bf16[8,4224]{1,0:T(8,128)(2,1)}, u32[]{:S(2)}, u32[]{:S(2)}) collective-permute-start(bf16[8,4224]{1,0:T(8,128)(2,1)} %get-tuple-element.63), channel_id=1, source_target_pairs={{0,12},{1,13},{2,14},{3,15},{4,8},{5,9},{6,10},{7,11},{8,4},{9,5},... | collective-permute-start | bytes 202760 | tf_op jit(solution)/shard_map/ppermute | solution.py:680
  74.7 5.1 %collective-permute-start.25 = (bf16[32,2176]{1,0:T(8,128)(2,1)S(1)}, bf16[32,2176]{1,0:T(8,128)(2,1)S(1)}, u32[]{:S(2)}, u32[]{:S(2)}) collective-permute-start(bf16[32,2176]{1,0:T(8,128)(2,1)S(1)} %get-tuple-element.68.refs_2_), channel_id=1, source_target_pairs={{0,2},{1,3},{2,0},{3,1},{4,6},{5,7},{6,4},{7,5},{8,10},{9,11},{10,... | collective-permute-start | bytes 417800 | tf_op jit(solution)/shard_map/ppermute | solution.py:680
  79.9 2.8 %collective-permute-start.26 = (f32[2,12,8]{2,1,0:T(8,128)S(1)}, f32[2,12,8]{2,1,0:T(8,128)S(1)}, u32[]{:S(2)}, u32[]{:S(2)}) collective-permute-start(f32[2,12,8]{2,1,0:T(8,128)S(1)} %get-tuple-element.95.refs_2_), channel_id=1, source_target_pairs={{0,1},{1,0},{2,3},{3,2},{4,5},{5,4},{6,7},{7,6},{8,9},{9,8},{10,11... | collective-permute-start | bytes 2312 | tf_op jit(solution)/shard_map/ppermute | solution.py:680
  82.9 4.3 %collective-permute-start.27 = (bf16[24,1040]{1,0:T(8,128)(2,1)S(1)}, bf16[24,1040]{1,0:T(8,128)(2,1)S(1)}, u32[]{:S(2)}, u32[]{:S(2)}) collective-permute-start(bf16[24,1040]{1,0:T(8,128)(2,1)S(1)} %concatenate.40), channel_id=1, source_target_pairs={{0,16},{1,17},{2,18},{3,19},{4,20},{5,21},{6,22},{7,23},{8,24},{9,... | collective-permute-start | bytes 149768 | tf_op jit(solution)/shard_map/ppermute | solution.py:680
  84.3 3.1 %collective-permute-start.28 = (bf16[64,1024]{1,0:T(8,128)(2,1)S(1)}, bf16[64,1024]{1,0:T(8,128)(2,1)S(1)}, u32[]{:S(2)}, u32[]{:S(2)}) collective-permute-start(bf16[64,1024]{1,0:T(8,128)(2,1)S(1)} %bitcast.92), channel_id=1, source_target_pairs={{0,1},{1,0},{2,3},{3,2},{4,5},{5,4},{6,7},{7,6},{8,9},{9,8},{10,11... | collective-permute-start | bytes 393224 | tf_op jit(solution)/shard_map/ppermute | solution.py:680
  (18 other events, 136.1 us)

commit v4 on v3

--- a/solution.py
+++ b/solution.py
@@ -238,18 +238,17 @@
         for copy in copies[:2]:
             copy.wait()
         total = jnp.zeros((count, 1), jnp.float32)
-        reduced = jnp.zeros((count, entries), jnp.float32)
         for at in range(0, width, chunk):
             part = slice(at, at + chunk)
             if at % quarter == 0:
                 x_copies[at // quarter].wait()
             x = x_ref[:, part].astype(jnp.float32)
             total = total + jnp.sum(x * x, axis=1, keepdims=True)
-            gained = (x * gain_ref[:, part]).astype(jnp.bfloat16)
-            reduced = reduced + lax.dot_general(
-                gained, down_ref[:, part], (((1,), (1,)), ((), ())),
-                preferred_element_type=jnp.float32,
-            )
+            x_ref[:, part] = (x * gain_ref[:, part]).astype(jnp.bfloat16)
+        reduced = lax.dot_general(
+            x_ref[...], down_ref[...], (((1,), (1,)), ((), ())),
+            preferred_element_type=jnp.float32,
+        )
         small_ref[...] = jnp.zeros_like(small_ref)
         small_ref[:, :entries] = reduced * mine
         small_ref[:, entries : entries + 1] = total * mine
@@ -295,11 +294,11 @@
     chunk = 512
     steps = (stop - start) // chunk
     held = pl.BlockSpec(memory_space=pl.ANY)
-    operands, specs = [rows_in, weight, marker], [WHOLE, held, held]
-    for more in (gain, before):
+    operands, specs = [rows_in, weight], [WHOLE, held]
+    for more, spec in ((gain, WHOLE), (marker, held), (before, WHOLE)):
         if more is not None:
             operands += [more]
-            specs += [WHOLE]
+            specs += [spec]
 
     def kernel(*refs):
         x_ref, w_ref = refs[:2]
@@ -321,7 +320,7 @@
             at = pl.multiple_of(start + i * chunk, chunk)
             x = x_ref[:, pl.ds(at, chunk)]
             if gain is not None:
-                x = (x.astype(jnp.float32) * refs[3][:, pl.ds(at, chunk)]).astype(jnp.bfloat16)
+                x = (x.astype(jnp.float32) * refs[2][:, pl.ds(at, chunk)]).astype(jnp.bfloat16)
             fetch(i).wait()
             out_ref[...] += jnp.dot(x, buf[i], preferred_element_type=jnp.float32)
             return carry
@@ -407,7 +406,7 @@
     entries = 24
     rank = entries // 3
 
-    def kernel(p_ref, small_ref, r_ref, a_ref, b_ref, c_ref, d_ref, slot_ref, out_ref, acc_ref):
+    def kernel(p_ref, small_ref, r_ref, a_ref, b_ref, c_ref, d_ref, slot_ref, out_ref, acc_ref, tall_ref):
         wide_pos = lax.axis_index("wide")
         other = r_ref[:, cols : cols + 64].astype(jnp.float32)
         small = small_ref[...] + (other[:, :32] + other[:, 32:64])
@@ -434,18 +433,21 @@
             change = jnp.dot(left, up, preferred_element_type=jnp.float32)
             base = p_ref[:, lo:hi] + r_ref[:, lo:hi].astype(jnp.float32)
             acc_ref[:, lo:hi] = base * scale + adapter_scale * change
+        for b in range(blocks):
+            tall_ref[pl.ds(b, count, stride=blocks), :] = acc_ref[:, b * lanes : (b + 1) * lanes]
         for a in range(4):
-            for b in range(blocks):
-                out_ref[a, b] = acc_ref[
-                    a * each : (a + 1) * each, b * lanes : (b + 1) * lanes
-                ].astype(out_ref.dtype)
+            part = slice(a * each * blocks, (a + 1) * each * blocks)
+            out_ref[a // 2, a % 2] = tall_ref[part, :].astype(out_ref.dtype)
 
     return pl.pallas_call(
         kernel,
         in_specs=[WHOLE] * 8,
         out_specs=WHOLE,
-        out_shape=jax.ShapeDtypeStruct((4, blocks, each, lanes), jnp.bfloat16),
-        scratch_shapes=[pltpu.VMEM((count, cols), jnp.float32)],
+        out_shape=jax.ShapeDtypeStruct((2, 2, each * blocks, lanes), jnp.bfloat16),
+        scratch_shapes=[
+            pltpu.VMEM((count, cols), jnp.float32),
+            pltpu.VMEM((count * blocks, lanes), jnp.float32),
+        ],
         compiler_params=pltpu.CompilerParams(vmem_limit_bytes=12 * 2**20),
     )(partial, small, received, *ups, slot)
 
@@ -463,14 +465,18 @@
         ].astype(rows_ref.dtype)
 
 
-def ordered_product(groups, order, weight, stop, rows):
-    pieces, tall, lanes = groups[0].shape
+def ordered_product(groups, offsets, weight, stop, rows):
+    tall, lanes = groups[0].shape[1:]
     depth, cols = weight.shape
-    count = 4 * pieces * rows
+    pieces = sum(len(at) for at in offsets)
+    count = pieces * rows
     chunk = 512
     steps = stop // chunk
 
-    def kernel(order_ref, a_ref, b_ref, c_ref, d_ref, w_ref, rows_ref, out_ref, wide_ref, buf, sem):
+    def kernel(*refs):
+        group_refs, w_ref = refs[: len(groups)], refs[len(groups)]
+        rows_ref, out_ref, wide_ref, buf, sem = refs[len(groups) + 1 :]
+        wide_pos = lax.axis_index("wide")
         copies = [
             pltpu.make_async_copy(w_ref.at[pl.ds(i * chunk, chunk)], buf.at[i], sem.at[i])
             for i in range(steps)
@@ -478,9 +484,9 @@
         for copy in copies:
             copy.start()
         placed = [
-            (order_ref[g * pieces + p], ref[p])
-            for g, ref in enumerate((a_ref, b_ref, c_ref, d_ref))
-            for p in range(pieces)
+            (wide_pos ^ offset, ref[p])
+            for ref, at in zip(group_refs, offsets)
+            for p, offset in enumerate(at)
         ]
         strided_rows(wide_ref, rows_ref, placed)
         total = jnp.zeros((count, cols), jnp.float32)
@@ -500,14 +506,14 @@
 
     return pl.pallas_call(
         kernel,
-        in_specs=[SCALARS] + [WHOLE] * 4 + [pl.BlockSpec(memory_space=pl.ANY)],
+        in_specs=[WHOLE] * len(groups) + [pl.BlockSpec(memory_space=pl.ANY)],
         out_specs=[WHOLE, WHOLE],
         out_shape=[
             jax.ShapeDtypeStruct((count, depth), groups[0].dtype),
             jax.ShapeDtypeStruct((count, cols), jnp.float32),
         ],
         scratch_shapes=[
-            pltpu.VMEM((4 * pieces, tall, lanes), jnp.float32),
+            pltpu.VMEM((pieces, tall, lanes), jnp.float32),
             pltpu.VMEM((steps, chunk, cols), weight.dtype),
             pltpu.SemaphoreType.DMA((steps,)),
         ],
@@ -515,24 +521,26 @@
             flops=2 * count * cols * stop, bytes_accessed=2 * cols * stop, transcendentals=0
         ),
         compiler_params=pltpu.CompilerParams(vmem_limit_bytes=48 * 2**20),
-    )(order, *groups, weight)
-
-
-def pack_o_z(place, slot, pieces, downs, up, rows):
+    )(*groups, weight)
+
+
+def pack_o_z(slot, pieces, downs, up, rows):
     count, tall, lanes = pieces.shape
     rank, depth = downs[0].shape
     span = up.shape[1] // count
     total = count * rows
 
-    def kernel(place_ref, slot_ref, p_ref, *refs):
+    def kernel(slot_ref, p_ref, *refs):
+        wide_pos = lax.axis_index("wide")
+        core, y, z = wide_pos & 1, (wide_pos >> 1) & 1, wide_pos >> 2
         down_refs, up_ref = refs[:4], refs[4]
         out_refs, (wide_ref, rows_ref) = refs[5:9], refs[9:]
-        placed = [(place_ref[2] ^ dz, p_ref[dz]) for dz in range(count)]
+        placed = [(z ^ dz, p_ref[dz]) for dz in range(count)]
         strided_rows(wide_ref, rows_ref, placed)
         at = lax.broadcasted_iota(jnp.int32, (total, 1), 0)
         slots = jnp.zeros((total, 1), jnp.int32)
         for r in range(total):
-            row = (r // rows * 4 + place_ref[3] * 2 + place_ref[0]) * rows + r % rows
+            row = (r // rows * 4 + y * 2 + core) * rows + r % rows
             slots = jnp.where(at == r, slot_ref[row], slots)
         out = jnp.zeros((total, rank), jnp.float32)
         for offset, ref in enumerate(down_refs):
@@ -540,9 +548,9 @@
                 rows_ref[...], ref[...], (((1,), (1,)), ((), ())),
                 preferred_element_type=jnp.float32,
             )
-            out = out + jnp.where(slots == (place_ref[1] ^ offset), part, 0.0)
+            out = out + jnp.where(slots == (wide_pos ^ offset), part, 0.0)
         for dz, ref in enumerate(out_refs):
-            at = pl.multiple_of((place_ref[2] ^ dz) * span, lanes)
+            at = pl.multiple_of((z ^ dz) * span, lanes)
             ref[:, :span] = up_ref[:, pl.ds(at, span)]
             ref[:, span:] = jnp.zeros((rank, lanes), ref.dtype)
             for rows_at, at in ((0, span), (rank, span + lanes // 2)):
@@ -554,7 +562,7 @@
 
     return pl.pallas_call(
         kernel,
-        in_specs=[SCALARS, SCALARS] + [WHOLE] * 6,
+        in_specs=[SCALARS] + [WHOLE] * 6,
         out_specs=[WHOLE] * 4,
         out_shape=[jax.ShapeDtypeStruct((rank, span + lanes), up.dtype)] * 4,
         scratch_shapes=[
@@ -565,15 +573,17 @@
             flops=0, bytes_accessed=4 * total * depth, transcendentals=0
         ),
         compiler_params=pltpu.CompilerParams(vmem_limit_bytes=10 * 2**20),
-    )(place, slot, pieces, *downs, up)
-
-
-def pack_o_y(place, parts, total):
+    )(slot, pieces, *downs, up)
+
+
+def pack_o_y(parts, total):
     rank = parts[0].shape[0]
     lanes = 128
     span = (parts[0].shape[1] - lanes) // 2
 
-    def kernel(place_ref, a_ref, b_ref, c_ref, d_ref, away_ref, keep_ref, sum_ref):
+    def kernel(a_ref, b_ref, c_ref, d_ref, away_ref, near_ref, far_ref, sum_ref):
+        wide_pos = lax.axis_index("wide")
+        core, y = wide_pos & 1, (wide_pos >> 1) & 1
         refs = (a_ref, b_ref, c_ref, d_ref)
 
         def decoded(ref, rows, at):
@@ -597,30 +607,69 @@
             away_ref[:total, span + t * rank : span + (t + 1) * rank] = top
             left = left - top.astype(jnp.float32)
 
-        def write(yb):
+        def write(yb, cb):
             for dz, ref in enumerate(refs):
                 rows = slice(dz * rank, (dz + 1) * rank)
-                keep_ref[rows, :] = ref[:, yb * span : (yb + 1) * span]
+                for out, half in ((near_ref, cb), (far_ref, 1 - cb)):
+                    lane = yb * span + half * span // 2
+                    out[rows, :] = ref[:, lane : lane + span // 2]
                 away_ref[rows, :span] = ref[:, (1 - yb) * span : (2 - yb) * span]
 
         for yb in range(2):
-
-            @pl.when(place_ref[3] == yb)
-            def _():
-                write(yb)
+            for cb in range(2):
+
+                @pl.when((y == yb) & (core == cb))
+                def _():
+                    write(yb, cb)
 
     dtype = parts[0].dtype
     return pl.pallas_call(
         kernel,
-        in_specs=[SCALARS] + [WHOLE] * 4,
-        out_specs=[WHOLE] * 3,
+        in_specs=[WHOLE] * 4,
+        out_specs=[WHOLE] * 4,
         out_shape=[
             jax.ShapeDtypeStruct((4 * rank, span + lanes), dtype),
-            jax.ShapeDtypeStruct((4 * rank, span), dtype),
+            jax.ShapeDtypeStruct((4 * rank, span // 2), dtype),
+            jax.ShapeDtypeStruct((4 * rank, span // 2), dtype),
             jax.ShapeDtypeStruct((total, rank), jnp.float32),
         ],
         compiler_params=pltpu.CompilerParams(vmem_limit_bytes=8 * 2**20),
-    )(place, *parts)
+    )(*parts)
+
+
+def finish(mixed, received, o_rows, slot, ups):
+    count, cols = mixed.shape
+    half = count // 2
+    rank = o_rows.shape[1]
+    lanes = 4 * ups[0].shape[0]
+
+    def kernel(m_ref, r_ref, rows_ref, slot_ref, *refs):
+        out_ref = refs[-1]
+        wide_pos = lax.axis_index("wide")
+        at = pl.ds(pl.multiple_of(lax.axis_index("kv") * half, 8), half)
+        two = r_ref[:, cols:].astype(jnp.float32)
+        total = rows_ref[at, :] + (two[:, :rank] + two[:, rank:])
+        lane = lax.broadcasted_iota(jnp.int32, (half, lanes), 1)
+        owner = wide_pos ^ (((lane >> 3) & 3) * 4 + ((lane >> 5) & 1) * 2 + (lane >> 6))
+        entry = lax.broadcasted_iota(jnp.int32, (rank, lanes), 0)
+        to = lax.broadcasted_iota(jnp.int32, (rank, lanes), 1) & (rank - 1)
+        chosen = (entry == to).astype(jnp.bfloat16)
+        value = jnp.dot(
+            total.astype(jnp.bfloat16), chosen, preferred_element_type=jnp.float32
+        )
+        left = jnp.where(slot_ref[at, :] == owner, value, 0.0).astype(jnp.bfloat16)
+        up = jnp.concatenate([ref[...] for ref in refs[:-1]], axis=0)
+        change = jnp.dot(left, up, preferred_element_type=jnp.float32)
+        base = m_ref[at, :] + r_ref[:, :cols].astype(jnp.float32)
+        out_ref[...] = (base + adapter_scale * change).astype(out_ref.dtype)
+
+    return pl.pallas_call(
+        kernel,
+        in_specs=[WHOLE] * 8,
+        out_specs=WHOLE,
+        out_shape=jax.ShapeDtypeStruct((half, cols), jnp.bfloat16),
+        compiler_params=pltpu.CompilerParams(vmem_limit_bytes=8 * 2**20),
+    )(mixed, received, o_rows, slot, *ups)
 
 
 def in_two(v):
@@ -683,7 +732,6 @@
         return lax.dynamic_index_in_dim(x, i, axis, keepdims=False)
 
     half = batch // 2
-    place = jnp.stack([core, wide_pos, z, y])
 
     gain = input_norm_gain[None]
     same, flip, small, slot, mine = prepare(
@@ -699,7 +747,7 @@
     depth = hidden_input.shape[1]
     cut = depth * 5 // 8
     weight = joint_projection_weight
-    partial = stream_product(hidden_input, gain, weight, 0, cut, None, same)
+    partial = stream_product(hidden_input, gain, weight, 0, cut, None, None)
     away, ups_near, ups_far, small = pack_y(parts, small, cols)
     away, partial = lax.optimization_barrier((away, partial))
     from_y = swap(away, 2)
@@ -722,23 +770,25 @@
     o_down_y = swap(o_down, 2)
     merged = merge(partial, small, from_x, ups, slot)
 
-    to = [pick(merged, z ^ d) for d in range(4)]
-    from_1 = swap(to[1], 4, source=True)
-    from_2 = swap(to[2], 8, source=True)
-    from_3 = swap(to[3], 12, source=True)
-    near = jnp.stack([jnp.where(right, to[0], from_2), jnp.where(right, from_1, from_3)])
-    keep = lax.dynamic_slice_in_dim(near, y * 2 * rows, 2 * rows, 2)
-    give = lax.dynamic_slice_in_dim(near, (1 - y) * 2 * rows, 2 * rows, 2)
-    from_y = swap(give, 2)
-    near = jnp.stack([jnp.where(y == 0, keep, from_y), jnp.where(y == 0, from_y, keep)], axis=1)
+    across = swap(pick(merged, 1 - (z >> 1)), 8, source=True)
+    half_rows = jnp.where(right, pick(merged, z >> 1), across)
+    beside = swap(pick(half_rows, 1 - (z & 1)), 4)
+    near = jnp.stack([pick(half_rows, z & 1), beside])
+    span = rows * blocks
+    keep = lax.dynamic_slice_in_dim(near, y * 2 * span, 2 * span, 1)
+    from_y = swap(lax.dynamic_slice_in_dim(near, (1 - y) * 2 * span, 2 * span, 1), 2)
+    near = jnp.stack([keep, from_y])
     far = swap(near, 1)
-    parts = [jnp.where(core == 0, near, far), jnp.where(core == 0, far, near)]
-    parts = [
-        lax.dynamic_slice_in_dim(jnp.where((z & 1) == 0, p, p[::-1]), core * rows, rows, 3)
-        for p in parts
-    ]
-    joined = jnp.concatenate(parts, axis=2).astype(f32)
-    joined = joined.reshape(heads, 2 * blocks, rows, head_dim).transpose(2, 0, 1, 3)
+    near = lax.dynamic_slice_in_dim(near, core * span, span, 2)
+    far = lax.dynamic_slice_in_dim(far, core * span, span, 2)
+    parts = []
+    for first in (jnp.where(core == 0, near, far), jnp.where(core == 0, far, near)):
+        at = [pick(first, b ^ y) for b in range(2)]
+        parts.append(jnp.stack([pick(v, b ^ (z & 1)) for b in range(2) for v in at]))
+    joined = jnp.concatenate(
+        [p.reshape(heads, rows, blocks, head_dim) for p in parts], axis=2
+    ).astype(f32)
+    joined = joined.transpose(1, 0, 2, 3)
     query_vector = rotate(joined[:, :, :group], lengths).astype(bf16)
     fresh_key = rotate(joined[:, :, group], lengths).astype(bf16)
     value_new = joined[:, :, group + 1].astype(bf16)
@@ -767,49 +817,35 @@
     near = jnp.stack([attended, swap(attended, 4), swap(attended, 8), swap(attended, 12)])
     near_y = swap(near, 2)
     o_downs = (o_down, swap(o_down, 1), o_down_y, swap(o_down_y, 1))
-    o_z = pack_o_z(place, slot[:, 0], near, o_downs, output_up_weight[0], rows)
+    o_z = pack_o_z(slot[:, 0], near, o_downs, output_up_weight[0], rows)
     near_y, o_z = lax.optimization_barrier((near_y, o_z))
     from_z = [swap(o_z[1], 4), swap(o_z[2], 8), swap(o_z[3], 12)]
-    far, far_y = swap(near, 1), swap(near_y, 1)
-    offsets = [
-        dz * 4 + dy * 2 + dcore for dcore in range(2) for dy in range(2) for dz in range(4)
-    ]
-    order = wide_pos ^ jnp.array(offsets, jnp.int32)
+    gathered = (near, near_y)
+    gathered += tuple(swap(v, 1) for v in gathered)
     first, second = depth * 3 // 8, depth * 3 // 4
-    everyone, mixed = ordered_product(
-        (near, near_y, far, far_y), order, output_weight, first, rows
-    )
+    offsets = [(0, 4, 8, 12), (2, 6, 10, 14)]
+    offsets += [tuple(v + 1 for v in at) for at in offsets]
+    everyone, mixed = ordered_product(gathered, offsets, output_weight, first, rows)
     mixed, from_z = lax.optimization_barrier((mixed, from_z))
-    o_away, o_keep, o_rows = pack_o_y(place, [o_z[0]] + from_z, 4 * rows)
+    o_away, o_near, o_near_c, o_rows = pack_o_y([o_z[0]] + from_z, 4 * rows)
     o_far = swap(o_away, 2)
     mixed = stream_product(everyone, None, output_weight, first, second, mixed, o_away)
     mixed, o_far = lax.optimization_barrier((mixed, o_far))
     o_rows = jnp.stack([o_rows, from_two(o_far[: 4 * rows, 2 * out_cols :][:, : 2 * rank])])
-    o_up = jnp.concatenate([o_keep, o_far[:, : 2 * out_cols]], axis=0)
-    o_up = o_up.reshape(8 * rank, 2, out_cols)
-    o_up_c = swap(pick(o_up, 1 - core, 1), 1)
+    o_far_c = lax.dynamic_slice_in_dim(o_far, (1 - core) * out_cols, out_cols, 1)
+    o_far_n = lax.dynamic_slice_in_dim(o_far, core * out_cols, out_cols, 1)
+    o_ups = (o_near, o_far_n, swap(o_near_c, 1), swap(o_far_c, 1))
     o_rows_c = swap(o_rows, 1)
     mixed = stream_product(everyone, None, output_weight, second, depth, mixed, o_rows)
-    o_up = jnp.concatenate([pick(o_up, core, 1), o_up_c], axis=0)
     o_rows = jnp.stack([o_rows, o_rows_c], axis=1)
     o_rows = jnp.where(y == 0, o_rows, o_rows[::-1])
     o_rows = jnp.where(core == 0, o_rows, o_rows[:, ::-1])
     o_rows = o_rows.reshape(2, 2, 4, rows, rank).transpose(2, 0, 1, 3, 4).reshape(batch, rank)
 
-    keep_out = lax.dynamic_slice_in_dim(mixed, kv_pos * half, half)
     give_out = lax.dynamic_slice_in_dim(mixed, (1 - kv_pos) * half, half).astype(bf16)
-    o_keep = lax.dynamic_slice_in_dim(o_rows, kv_pos * half, half)
     o_give = in_two(lax.dynamic_slice_in_dim(o_rows, (1 - kv_pos) * half, half))
     from_x = swap(jnp.concatenate([give_out, o_give], axis=1), 16)
-    o_keep = o_keep + from_two(from_x[:, out_cols:])
-    lane = jnp.arange(wide, dtype=jnp.int32)
-    owner = wide_pos ^ ((lane & 3) * 4 + ((lane >> 2) & 1) * 2 + (lane >> 3))
-    slot_o = lax.dynamic_slice_in_dim(slot, kv_pos * half, half)
-    hit = slot_o == owner[None, :]
-    shrink = jnp.where(hit[:, :, None], o_keep.astype(bf16)[:, None, :], 0).reshape(half, -1)
-    change = jnp.dot(shrink, o_up, preferred_element_type=f32)
-    base = keep_out + from_x[:, :out_cols].astype(f32)
-    return (base + adapter_scale * change).astype(bf16)
+    return finish(mixed, from_x, o_rows, slot, o_ups)
 
 
 def on_device(*arrays):

time: 88.6 us -> 85.8 us (0.968)
  waiting for transfers between devices: 19.7 us -> 24.7 us
  local copies, waits for them, and re-layouts: 4.21 us -> 1.68 us
  starting transfers between devices: 34.1 us -> 32.5 us
  other arithmetic: 2.7 us -> 1.2 us
  Pallas kernels: 24.8 us -> 23.7 us
    ppermute x29, waiting for transfers between devices: 19.7 us -> 24.7 us  [swap(): return lax.ppermute(x, ('kv', 'wide'), pairs)]
    unnamed x30 -> x22, local copies, waits for them, and re-layouts: 2.49 us -> 0.82 us
    ppermute x29, starting transfers between devices: 34.1 us -> 32.5 us  [swap(): return lax.ppermute(x, ('kv', 'wide'), pairs)]
    pallas_call x3 -> x4, Pallas kernels: 6.8 us -> 5.62 us  [the longest x1 3.15 us: ordered_product(): pl.pallas_call(kernel, in_specs=[WHOLE] * len(groups) + [pl.BlockSpec(mem...]
    xor x2 -> x0, other arithmetic: 1.11 us -> none  [the longest x1 0.57 us: staged_path(): order = wide_pos ^ jnp.array(offsets, jnp.int32)]
  transfers between devices with their start and end apart: 29 -> 29, of which waited for: 16 -> 16; matrix products, arithmetic and copies ran while one was open for 4% -> 1% of each run, Pallas kernels for 22% -> 21%
where the time goes in v4:
time: 85.8 us; the launch traced here: 85.5 us
  starting transfers between devices  32.5 us (38%)
  waiting for transfers between devices  24.7 us (29%)
  Pallas kernels  23.7 us (28%)
  local copies, waits for them, and re-layouts  1.68 us (2%)
  matrix products  1.22 us (1%)
  other arithmetic  1.2 us (1%)
    ppermute x29, starting transfers between devices, swap(): return lax.ppermute(x, ('kv', 'wide'), pairs)  32.5 us
    ppermute x29, waiting for transfers between devices, swap(): return lax.ppermute(x, ('kv', 'wide'), pairs)  24.7 us
    pallas_call x4, Pallas kernels, stream_product(): pl.pallas_call(kernel, in_specs=specs, out_specs=WHOLE, out_shape=jax.Sha...  13.9 us
    pallas_call x1, Pallas kernels, prepare(): pl.pallas_call(kernel, in_specs=[SCALARS, WHOLE] + [pl.BlockSpec(memory_s...  3.46 us
    pallas_call x1, Pallas kernels, ordered_product(): pl.pallas_call(kernel, in_specs=[WHOLE] * len(groups) + [pl.BlockSpec(mem...  3.15 us
  transfers between devices with their start and end apart: 29, of which 16 were waited for; matrix products, arithmetic and copies ran while one was open for 1% of the time, Pallas kernels for 21%

profile of v4, /device:TPU:0, one launch (start us, length us, event | category | flops | bytes accessed | tf_op | source)
XLA Modules:
  0.0 85.5 jit_solution(14144152830227534459)
XLA Ops:
  0.0 3.5 %shard_map.136 = (bf16[16,2560]{1,0:T(8,128)(2,1)}, bf16[16,2560]{1,0:T(8,128)(2,1)}, f32[48,32]{1,0:T(8,128)}, s32[48,1]{1,0:T(8,128)}, f32[48,1]{1,0:T(8,128)}) custom-call(s32[16]{0:T(128)} %owner_ref.1, s32[1,48]{1,0:T(1,128)} %bitcast.101, bf16[48,8192]{1,0:T(8,128)(2,1)} %refs_0_.3, f32[1,8192]{1,0:T(1,128)} %bitcast.63, bf16[24,8192]{1,0:T(8,128)(2,1)} %bitcast.72, ...), custom_call_target="tpu_custom_call" | custom-call | tf_op jit(solution)/shard_map/pallas_call | solution.py:275
  3.5 4.1 %collective-permute-start.1 = (bf16[16,2560]{1,0:T(8,128)(2,1)}, bf16[16,2560]{1,0:T(8,128)(2,1)S(1)}, u32[]{:S(2)}, u32[]{:S(2)}) collective-permute-start(bf16[16,2560]{1,0:T(8,128)(2,1)} %get-tuple-element.40.a_ref), channel_id=1, source_target_pairs={{0,8},{1,9},{2,10},{3,11},{4,12},{5,13},{6,14},{7,15},{8,0},{9,1},... | collective-permute-start | bytes 245768 | tf_op jit(solution)/shard_map/ppermute | solution.py:729
  9.9 4.8 %shard_map.138.refs_4_ = f32[48,1152]{1,0:T(8,128)S(1)} custom-call(bf16[48,8192]{1,0:T(8,128)(2,1)S(1)} %copy-done.1, bf16[8192,1152]{1,0:T(8,128)(2,1)} %refs_1_.5, f32[1,8192]{1,0:T(1,128)S(1)} %bitcast.64), custom_call_target="tpu_custom_call" | custom-call | flops 566231040 | bytes 11796480 | tf_op jit(solution)/shard_map/pallas_call | solution.py:330
  15.2 1.8 %collective-permute-start.3 = (bf16[32,2432]{1,0:T(8,128)(2,1)S(1)}, bf16[32,2432]{1,0:T(8,128)(2,1)S(1)}, u32[]{:S(2)}, u32[]{:S(2)}) collective-permute-start(bf16[32,2432]{1,0:T(8,128)(2,1)S(1)} %get-tuple-element.44.refs_3_), channel_id=1, source_target_pairs={{0,2},{1,3},{2,0},{3,1},{4,6},{5,7},{6,4},{7,5},{8,10},{9,11},{10,... | collective-permute-start | bytes 466952 | tf_op jit(solution)/shard_map/ppermute | solution.py:729
  17.0 3.4 %shard_map.139.p_ref = f32[48,1152]{1,0:T(8,128)S(1)} custom-call(bf16[48,8192]{1,0:T(8,128)(2,1)S(1)} %copy-done.1, bf16[8192,1152]{1,0:T(8,128)(2,1)} %refs_1_.5, f32[1,8192]{1,0:T(1,128)S(1)} %bitcast.65, bf16[32,2432]{1,0:T(8,128)(2,1)S(1)} %get-tuple-element.44.refs_3_, f32[48,1152]{1,0:T(8,128)S(1)} %shard_map.138.refs_4_), custom_call_target="tpu_custom_call" | custom-call | flops 339738624 | bytes 7077888 | tf_op jit(solution)/shard_map/pallas_call | solution.py:330
  25.0 4.3 %collective-permute-done.5.r_ref = bf16[48,1216]{1,0:T(8,128)(2,1)S(1)} collective-permute-done((bf16[48,1216]{1,0:T(8,128)(2,1)S(1)}, bf16[48,1216]{1,0:T(8,128)(2,1)S(1)}, u32[]{:S(2)}, u32[]{:S(2)}) %collective-permute-start.5) | collective-permute-done | bytes 116768 | tf_op jit(solution)/shard_map/ppermute | solution.py:729
  29.8 4.7 %collective-permute-start.8 = (bf16[2,108,128]{2,1,0:T(8,128)(2,1)S(1)}, bf16[2,108,128]{2,1,0:T(8,128)(2,1)S(1)}, u32[]{:S(2)}, u32[]{:S(2)}) collective-permute-start(bf16[2,108,128]{2,1,0:T(8,128)(2,1)S(1)} %dynamic-slice_bitcast_fusion), channel_id=1, source_target_pairs={{0,8},{1,9},{2,10},{3,11},{4,12},{5,13},{6,14},{7,15},{24,16},{25,... | collective-permute-start | bytes 165896 | tf_op jit(solution)/shard_map/ppermute | solution.py:729
  34.6 1.8 %collective-permute-done.8 = bf16[2,108,128]{2,1,0:T(8,128)(2,1)S(1)} collective-permute-done((bf16[2,108,128]{2,1,0:T(8,128)(2,1)S(1)}, bf16[2,108,128]{2,1,0:T(8,128)(2,1)S(1)}, u32[]{:S(2)}, u32[]{:S(2)}) %collective-permute-start.8) | collective-permute-done | bytes 55328 | tf_op jit(solution)/shard_map/ppermute | solution.py:729
  36.8 3.5 %collective-permute-done.9 = bf16[108,128]{1,0:T(8,128)(2,1)S(1)} collective-permute-done((bf16[108,128]{1,0:T(8,128)(2,1)S(1)}, bf16[108,128]{1,0:T(8,128)(2,1)S(1)}, u32[]{:S(2)}, u32[]{:S(2)}) %collective-permute-start.9) | collective-permute-done | bytes 27680 | tf_op jit(solution)/shard_map/ppermute | solution.py:729
  40.4 1.6 %collective-permute-start.10 = (bf16[2,54,128]{2,1,0:T(8,128)(2,1)S(1)}, bf16[2,54,128]{2,1,0:T(8,128)(2,1)S(1)}, u32[]{:S(2)}, u32[]{:S(2)}) collective-permute-start(bf16[2,54,128]{2,1,0:T(8,128)(2,1)S(1)} %get-tuple-element.88), channel_id=1, source_target_pairs={{0,2},{1,3},{2,0},{3,1},{4,6},{5,7},{6,4},{7,5},{8,10},{9,11},{10,... | collective-permute-start | bytes 82952 | tf_op jit(solution)/shard_map/ppermute | solution.py:729
  42.1 2.3 %collective-permute-done.10 = bf16[2,54,128]{2,1,0:T(8,128)(2,1)S(1)} collective-permute-done((bf16[2,54,128]{2,1,0:T(8,128)(2,1)S(1)}, bf16[2,54,128]{2,1,0:T(8,128)(2,1)S(1)}, u32[]{:S(2)}, u32[]{:S(2)}) %collective-permute-start.10) | collective-permute-done | bytes 27680 | tf_op jit(solution)/shard_map/ppermute | solution.py:729
  47.7 3.2 %collective-permute-start.14 = (bf16[192,128]{1,0:T(8,128)(2,1)S(1)}, bf16[192,128]{1,0:T(8,128)(2,1)S(1)}, u32[]{:S(2)}, u32[]{:S(2)}) collective-permute-start(bf16[192,128]{1,0:T(8,128)(2,1)S(1)} %bitcast.88), channel_id=1, source_target_pairs={{0,12},{1,13},{2,14},{3,15},{4,8},{5,9},{6,10},{7,11},{8,4},{9,5},... | collective-permute-start | bytes 147464 | tf_op jit(solution)/shard_map/ppermute | solution.py:729
  52.2 1.5 %collective-permute-start.17 = (bf16[8,8192]{1,0:T(8,128)(2,1)S(1)}, bf16[8,8192]{1,0:T(8,128)(2,1)S(1)}, u32[]{:S(2)}, u32[]{:S(2)}) collective-permute-start(bf16[8,8192]{1,0:T(8,128)(2,1)S(1)} %bitcast.68), channel_id=1, source_target_pairs={{0,2},{1,3},{2,0},{3,1},{4,6},{5,7},{6,4},{7,5},{8,10},{9,11},{10,... | collective-permute-start | bytes 393224 | tf_op jit(solution)/shard_map/ppermute | solution.py:729
  53.7 2.5 %collective-permute-done.13 = bf16[192,128]{1,0:T(8,128)(2,1)S(1)} collective-permute-done((bf16[192,128]{1,0:T(8,128)(2,1)S(1)}, bf16[192,128]{1,0:T(8,128)(2,1)S(1)}, u32[]{:S(2)}, u32[]{:S(2)}) %collective-permute-start.13) | collective-permute-done | bytes 49184 | tf_op jit(solution)/shard_map/ppermute | solution.py:729
  56.3 1.6 %collective-permute-start.15 = (bf16[4,192,128]{2,1,0:T(8,128)(2,1)S(1)}, bf16[4,192,128]{2,1,0:T(8,128)(2,1)S(1)}, u32[]{:S(2)}, u32[]{:S(2)}) collective-permute-start(bf16[4,192,128]{2,1,0:T(8,128)(2,1)S(1)} %pad_maximum_fusion.p_ref.refs_0_), channel_id=1, source_target_pairs={{0,2},{1,3},{2,0},{3,1},{4,6},{5,7},{6,4},{7,5},{8,10},{9,11},{10,... | collective-permute-start | bytes 589832 | tf_op jit(solution)/shard_map/ppermute | solution.py:729
  60.7 1.5 %collective-permute-done.15.refs_1_ = bf16[4,192,128]{2,1,0:T(8,128)(2,1)S(1)} collective-permute-done((bf16[4,192,128]{2,1,0:T(8,128)(2,1)S(1)}, bf16[4,192,128]{2,1,0:T(8,128)(2,1)S(1)}, u32[]{:S(2)}, u32[]{:S(2)}) %collective-permute-start.15) | collective-permute-done | bytes 196640 | tf_op jit(solution)/shard_map/ppermute | solution.py:729
  62.9 2.6 %collective-permute-start.22 = (bf16[8,4224]{1,0:T(8,128)(2,1)S(1)}, bf16[8,4224]{1,0:T(8,128)(2,1)S(1)}, u32[]{:S(2)}, u32[]{:S(2)}) collective-permute-start(bf16[8,4224]{1,0:T(8,128)(2,1)S(1)} %get-tuple-element.63), channel_id=1, source_target_pairs={{0,8},{1,9},{2,10},{3,11},{4,12},{5,13},{6,14},{7,15},{8,0},{9,1},... | collective-permute-start | bytes 202760 | tf_op jit(solution)/shard_map/ppermute | solution.py:729
  66.6 3.2 %shard_map.142 = (bf16[48,8192]{1,0:T(8,128)(2,1)S(1)}, f32[48,1024]{1,0:T(8,128)S(1)}) custom-call(bf16[4,192,128]{2,1,0:T(8,128)(2,1)S(1)} %pad_maximum_fusion.p_ref.refs_0_, bf16[4,192,128]{2,1,0:T(8,128)(2,1)S(1)} %collective-permute-done.15.refs_1_, bf16[4,192,128]{2,1,0:T(8,128)(2,1)S(1)} %collective-permute-done.19.refs_2_, ...), custom_call_target="tpu_custom_call" | custom-call | flops 301989888 | bytes 6291456 | tf_op jit(solution)/shard_map/pallas_call | solution.py:507
  69.8 1.8 %collective-permute-done.23.d_ref = bf16[8,4224]{1,0:T(8,128)(2,1)S(1)} collective-permute-done((bf16[8,4224]{1,0:T(8,128)(2,1)S(1)}, bf16[8,4224]{1,0:T(8,128)(2,1)S(1)}, u32[]{:S(2)}, u32[]{:S(2)}) %collective-permute-start.23) | collective-permute-done | bytes 67616 | tf_op jit(solution)/shard_map/ppermute | solution.py:729
  71.8 1.6 %collective-permute-start.24 = (bf16[32,2176]{1,0:T(8,128)(2,1)S(1)}, bf16[32,2176]{1,0:T(8,128)(2,1)S(1)}, u32[]{:S(2)}, u32[]{:S(2)}) collective-permute-start(bf16[32,2176]{1,0:T(8,128)(2,1)S(1)} %get-tuple-element.69.refs_2_), channel_id=1, source_target_pairs={{0,2},{1,3},{2,0},{3,1},{4,6},{5,7},{6,4},{7,5},{8,10},{9,11},{10,... | collective-permute-start | bytes 417800 | tf_op jit(solution)/shard_map/ppermute | solution.py:729
  73.4 3.2 %shard_map.144.refs_3_ = f32[48,1024]{1,0:T(8,128)S(1)} custom-call(bf16[48,8192]{1,0:T(8,128)(2,1)S(1)} %get-tuple-element.59.refs_0_, bf16[8192,1024]{1,0:T(8,128)(2,1)} %refs_1_.7, bf16[32,2176]{1,0:T(8,128)(2,1)S(1)} %get-tuple-element.69.refs_2_, f32[48,1024]{1,0:T(8,128)S(1)} %get-tuple-element.70.refs_3_), custom_call_target="tpu_custom_call" | custom-call | flops 301989888 | bytes 6291456 | tf_op jit(solution)/shard_map/pallas_call | solution.py:330
  77.3 2.5 %shard_map.145.m_ref = f32[48,1024]{1,0:T(8,128)S(1)} custom-call(bf16[48,8192]{1,0:T(8,128)(2,1)S(1)} %get-tuple-element.59.refs_0_, bf16[8192,1024]{1,0:T(8,128)(2,1)} %refs_1_.7, f32[2,12,8]{2,1,0:T(8,128)S(1)} %get-tuple-element.104.refs_2_, f32[48,1024]{1,0:T(8,128)S(1)} %shard_map.144.refs_3_), custom_call_target="tpu_custom_call" | custom-call | flops 201326592 | bytes 4194304 | tf_op jit(solution)/shard_map/pallas_call | solution.py:330
  80.4 1.5 %collective-permute-start.26 = (bf16[24,1040]{1,0:T(8,128)(2,1)S(1)}, bf16[24,1040]{1,0:T(8,128)(2,1)S(1)}, u32[]{:S(2)}, u32[]{:S(2)}) collective-permute-start(bf16[24,1040]{1,0:T(8,128)(2,1)S(1)} %concatenate.29), channel_id=1, source_target_pairs={{0,16},{1,17},{2,18},{3,19},{4,20},{5,21},{6,22},{7,23},{8,24},{9,... | collective-permute-start | bytes 149768 | tf_op jit(solution)/shard_map/ppermute | solution.py:729
  82.0 2.6 %collective-permute-done.26.r_ref = bf16[24,1040]{1,0:T(8,128)(2,1)S(1)} collective-permute-done((bf16[24,1040]{1,0:T(8,128)(2,1)S(1)}, bf16[24,1040]{1,0:T(8,128)(2,1)S(1)}, u32[]{:S(2)}, u32[]{:S(2)}) %collective-permute-start.26) | collective-permute-done | bytes 49952 | tf_op jit(solution)/shard_map/ppermute | solution.py:729
  (125 shorter events, 20.0 us)
Async XLA Ops:
  3.5 11.3 %collective-permute-start.1 = (bf16[16,2560]{1,0:T(8,128)(2,1)}, bf16[16,2560]{1,0:T(8,128)(2,1)S(1)}, u32[]{:S(2)}, u32[]{:S(2)}) collective-permute-start(bf16[16,2560]{1,0:T(8,128)(2,1)} %get-tuple-element.40.a_ref), channel_id=1, source_target_pairs={{0,8},{1,9},{2,10},{3,11},{4,12},{5,13},{6,14},{7,15},{8,0},{9,1},... | collective-permute-start | bytes 245768 | tf_op jit(solution)/shard_map/ppermute | solution.py:729
  7.6 7.2 %collective-permute-start.2 = (bf16[16,2560]{1,0:T(8,128)(2,1)}, bf16[16,2560]{1,0:T(8,128)(2,1)S(1)}, u32[]{:S(2)}, u32[]{:S(2)}) collective-permute-start(bf16[16,2560]{1,0:T(8,128)(2,1)} %get-tuple-element.41), channel_id=1, source_target_pairs={{0,12},{1,13},{2,14},{3,15},{4,8},{5,9},{6,10},{7,11},{8,4},{9,5},... | collective-permute-start | bytes 245768 | tf_op jit(solution)/shard_map/ppermute | solution.py:729
  8.9 6.0 %collective-permute-start = (bf16[16,2560]{1,0:T(8,128)(2,1)}, bf16[16,2560]{1,0:T(8,128)(2,1)S(1)}, u32[]{:S(2)}, u32[]{:S(2)}) collective-permute-start(bf16[16,2560]{1,0:T(8,128)(2,1)} %get-tuple-element.41), channel_id=1, source_target_pairs={{0,4},{1,5},{2,6},{3,7},{4,0},{5,1},{6,2},{7,3},{8,12},{9,13},{10,... | collective-permute-start | bytes 245768 | tf_op jit(solution)/shard_map/ppermute | solution.py:729
  15.2 5.3 %collective-permute-start.3 = (bf16[32,2432]{1,0:T(8,128)(2,1)S(1)}, bf16[32,2432]{1,0:T(8,128)(2,1)S(1)}, u32[]{:S(2)}, u32[]{:S(2)}) collective-permute-start(bf16[32,2432]{1,0:T(8,128)(2,1)S(1)} %get-tuple-element.44.refs_3_), channel_id=1, source_target_pairs={{0,2},{1,3},{2,0},{3,1},{4,6},{5,7},{6,4},{7,5},{8,10},{9,11},{10,... | collective-permute-start | bytes 466952 | tf_op jit(solution)/shard_map/ppermute | solution.py:729
  20.8 3.2 %collective-permute-start.6 = (bf16[32,1152]{1,0:T(8,128)(2,1)S(1)}, bf16[32,1152]{1,0:T(8,128)(2,1)S(1)}, u32[]{:S(2)}, u32[]{:S(2)}) collective-permute-start(bf16[32,1152]{1,0:T(8,128)(2,1)S(1)} %get-tuple-element.51), channel_id=1, source_target_pairs={{0,1},{1,0},{2,3},{3,2},{4,5},{5,4},{6,7},{7,6},{8,9},{9,8},{10,11... | collective-permute-start | bytes 221192 | tf_op jit(solution)/shard_map/ppermute | solution.py:729
  22.0 7.3 %collective-permute-start.5 = (bf16[48,1216]{1,0:T(8,128)(2,1)S(1)}, bf16[48,1216]{1,0:T(8,128)(2,1)S(1)}, u32[]{:S(2)}, u32[]{:S(2)}) collective-permute-start(bf16[48,1216]{1,0:T(8,128)(2,1)S(1)} %concatenate.25), channel_id=1, source_target_pairs={{8,24},{9,25},{10,26},{11,27},{12,28},{13,29},{14,30},{15,31},{16,... | collective-permute-start | bytes 350216 | tf_op jit(solution)/shard_map/ppermute | solution.py:729
  29.8 6.6 %collective-permute-start.8 = (bf16[2,108,128]{2,1,0:T(8,128)(2,1)S(1)}, bf16[2,108,128]{2,1,0:T(8,128)(2,1)S(1)}, u32[]{:S(2)}, u32[]{:S(2)}) collective-permute-start(bf16[2,108,128]{2,1,0:T(8,128)(2,1)S(1)} %dynamic-slice_bitcast_fusion), channel_id=1, source_target_pairs={{0,8},{1,9},{2,10},{3,11},{4,12},{5,13},{6,14},{7,15},{24,16},{25,... | collective-permute-start | bytes 165896 | tf_op jit(solution)/shard_map/ppermute | solution.py:729
  36.4 3.9 %collective-permute-start.9 = (bf16[108,128]{1,0:T(8,128)(2,1)S(1)}, bf16[108,128]{1,0:T(8,128)(2,1)S(1)}, u32[]{:S(2)}, u32[]{:S(2)}) collective-permute-start(bf16[108,128]{1,0:T(8,128)(2,1)S(1)} %get-tuple-element.89), channel_id=1, source_target_pairs={{0,4},{1,5},{2,6},{3,7},{4,0},{5,1},{6,2},{7,3},{8,12},{9,13},{10,... | collective-permute-start | bytes 82952 | tf_op jit(solution)/shard_map/ppermute | solution.py:729
  40.4 3.9 %collective-permute-start.10 = (bf16[2,54,128]{2,1,0:T(8,128)(2,1)S(1)}, bf16[2,54,128]{2,1,0:T(8,128)(2,1)S(1)}, u32[]{:S(2)}, u32[]{:S(2)}) collective-permute-start(bf16[2,54,128]{2,1,0:T(8,128)(2,1)S(1)} %get-tuple-element.88), channel_id=1, source_target_pairs={{0,2},{1,3},{2,0},{3,1},{4,6},{5,7},{6,4},{7,5},{8,10},{9,11},{10,... | collective-permute-start | bytes 82952 | tf_op jit(solution)/shard_map/ppermute | solution.py:729
  47.7 6.0 %collective-permute-start.14 = (bf16[192,128]{1,0:T(8,128)(2,1)S(1)}, bf16[192,128]{1,0:T(8,128)(2,1)S(1)}, u32[]{:S(2)}, u32[]{:S(2)}) collective-permute-start(bf16[192,128]{1,0:T(8,128)(2,1)S(1)} %bitcast.88), channel_id=1, source_target_pairs={{0,12},{1,13},{2,14},{3,15},{4,8},{5,9},{6,10},{7,11},{8,4},{9,5},... | collective-permute-start | bytes 147464 | tf_op jit(solution)/shard_map/ppermute | solution.py:729
  50.9 5.4 %collective-permute-start.13 = (bf16[192,128]{1,0:T(8,128)(2,1)S(1)}, bf16[192,128]{1,0:T(8,128)(2,1)S(1)}, u32[]{:S(2)}, u32[]{:S(2)}) collective-permute-start(bf16[192,128]{1,0:T(8,128)(2,1)S(1)} %bitcast.89), channel_id=1, source_target_pairs={{0,8},{1,9},{2,10},{3,11},{4,12},{5,13},{6,14},{7,15},{8,0},{9,1},... | collective-permute-start | bytes 147464 | tf_op jit(solution)/shard_map/ppermute | solution.py:729
  51.2 5.1 %collective-permute-start.12 = (bf16[192,128]{1,0:T(8,128)(2,1)S(1)}, bf16[192,128]{1,0:T(8,128)(2,1)S(1)}, u32[]{:S(2)}, u32[]{:S(2)}) collective-permute-start(bf16[192,128]{1,0:T(8,128)(2,1)S(1)} %bitcast.90), channel_id=1, source_target_pairs={{0,4},{1,5},{2,6},{3,7},{4,0},{5,1},{6,2},{7,3},{8,12},{9,13},{10,... | collective-permute-start | bytes 147464 | tf_op jit(solution)/shard_map/ppermute | solution.py:729
  52.2 5.7 %collective-permute-start.17 = (bf16[8,8192]{1,0:T(8,128)(2,1)S(1)}, bf16[8,8192]{1,0:T(8,128)(2,1)S(1)}, u32[]{:S(2)}, u32[]{:S(2)}) collective-permute-start(bf16[8,8192]{1,0:T(8,128)(2,1)S(1)} %bitcast.68), channel_id=1, source_target_pairs={{0,2},{1,3},{2,0},{3,1},{4,6},{5,7},{6,4},{7,5},{8,10},{9,11},{10,... | collective-permute-start | bytes 393224 | tf_op jit(solution)/shard_map/ppermute | solution.py:729
  56.3 5.9 %collective-permute-start.15 = (bf16[4,192,128]{2,1,0:T(8,128)(2,1)S(1)}, bf16[4,192,128]{2,1,0:T(8,128)(2,1)S(1)}, u32[]{:S(2)}, u32[]{:S(2)}) collective-permute-start(bf16[4,192,128]{2,1,0:T(8,128)(2,1)S(1)} %pad_maximum_fusion.p_ref.refs_0_), channel_id=1, source_target_pairs={{0,2},{1,3},{2,0},{3,1},{4,6},{5,7},{6,4},{7,5},{8,10},{9,11},{10,... | collective-permute-start | bytes 589832 | tf_op jit(solution)/shard_map/ppermute | solution.py:729
  58.5 8.1 %collective-permute-start.19 = (bf16[4,192,128]{2,1,0:T(8,128)(2,1)S(1)}, bf16[4,192,128]{2,1,0:T(8,128)(2,1)S(1)}, u32[]{:S(2)}, u32[]{:S(2)}) collective-permute-start(bf16[4,192,128]{2,1,0:T(8,128)(2,1)S(1)} %pad_maximum_fusion.p_ref.refs_0_), channel_id=1, source_target_pairs={{0,1},{1,0},{2,3},{3,2},{4,5},{5,4},{6,7},{7,6},{8,9},{9,8},{10,11... | collective-permute-start | bytes 589832 | tf_op jit(solution)/shard_map/ppermute | solution.py:729
  62.2 4.4 %collective-permute-start.20 = (bf16[4,192,128]{2,1,0:T(8,128)(2,1)S(1)}, bf16[4,192,128]{2,1,0:T(8,128)(2,1)S(1)}, u32[]{:S(2)}, u32[]{:S(2)}) collective-permute-start(bf16[4,192,128]{2,1,0:T(8,128)(2,1)S(1)} %collective-permute-done.15.refs_1_), channel_id=1, source_target_pairs={{0,1},{1,0},{2,3},{3,2},{4,5},{5,4},{6,7},{7,6},{8,9},{9,8},{10,11... | collective-permute-start | bytes 589832 | tf_op jit(solution)/shard_map/ppermute | solution.py:729
  62.2 7.6 %collective-permute-start.21 = (bf16[8,4224]{1,0:T(8,128)(2,1)S(1)}, bf16[8,4224]{1,0:T(8,128)(2,1)S(1)}, u32[]{:S(2)}, u32[]{:S(2)}) collective-permute-start(bf16[8,4224]{1,0:T(8,128)(2,1)S(1)} %get-tuple-element.62), channel_id=1, source_target_pairs={{0,4},{1,5},{2,6},{3,7},{4,0},{5,1},{6,2},{7,3},{8,12},{9,13},{10,... | collective-permute-start | bytes 202760 | tf_op jit(solution)/shard_map/ppermute | solution.py:729
  62.9 6.9 %collective-permute-start.22 = (bf16[8,4224]{1,0:T(8,128)(2,1)S(1)}, bf16[8,4224]{1,0:T(8,128)(2,1)S(1)}, u32[]{:S(2)}, u32[]{:S(2)}) collective-permute-start(bf16[8,4224]{1,0:T(8,128)(2,1)S(1)} %get-tuple-element.63), channel_id=1, source_target_pairs={{0,8},{1,9},{2,10},{3,11},{4,12},{5,13},{6,14},{7,15},{8,0},{9,1},... | collective-permute-start | bytes 202760 | tf_op jit(solution)/shard_map/ppermute | solution.py:729
  65.5 6.1 %collective-permute-start.23 = (bf16[8,4224]{1,0:T(8,128)(2,1)S(1)}, bf16[8,4224]{1,0:T(8,128)(2,1)S(1)}, u32[]{:S(2)}, u32[]{:S(2)}) collective-permute-start(bf16[8,4224]{1,0:T(8,128)(2,1)S(1)} %get-tuple-element.64), channel_id=1, source_target_pairs={{0,12},{1,13},{2,14},{3,15},{4,8},{5,9},{6,10},{7,11},{8,4},{9,5},... | collective-permute-start | bytes 202760 | tf_op jit(solution)/shard_map/ppermute | solution.py:729
  71.8 5.1 %collective-permute-start.24 = (bf16[32,2176]{1,0:T(8,128)(2,1)S(1)}, bf16[32,2176]{1,0:T(8,128)(2,1)S(1)}, u32[]{:S(2)}, u32[]{:S(2)}) collective-permute-start(bf16[32,2176]{1,0:T(8,128)(2,1)S(1)} %get-tuple-element.69.refs_2_), channel_id=1, source_target_pairs={{0,2},{1,3},{2,0},{3,1},{4,6},{5,7},{6,4},{7,5},{8,10},{9,11},{10,... | collective-permute-start | bytes 417800 | tf_op jit(solution)/shard_map/ppermute | solution.py:729
  73.4 8.5 %collective-permute-start.27 = (bf16[32,1024]{1,0:T(8,128)(2,1)S(1)}, bf16[32,1024]{1,0:T(8,128)(2,1)S(1)}, u32[]{:S(2)}, u32[]{:S(2)}) collective-permute-start(bf16[32,1024]{1,0:T(8,128)(2,1)S(1)} %get-tuple-element.74), channel_id=1, source_target_pairs={{0,1},{1,0},{2,3},{3,2},{4,5},{5,4},{6,7},{7,6},{8,9},{9,8},{10,11... | collective-permute-start | bytes 196616 | tf_op jit(solution)/shard_map/ppermute | solution.py:729
  77.0 3.2 %collective-permute-start.25 = (f32[2,12,8]{2,1,0:T(8,128)S(1)}, f32[2,12,8]{2,1,0:T(8,128)S(1)}, u32[]{:S(2)}, u32[]{:S(2)}) collective-permute-start(f32[2,12,8]{2,1,0:T(8,128)S(1)} %get-tuple-element.104.refs_2_), channel_id=1, source_target_pairs={{0,1},{1,0},{2,3},{3,2},{4,5},{5,4},{6,7},{7,6},{8,9},{9,8},{10,11... | collective-permute-start | bytes 2312 | tf_op jit(solution)/shard_map/ppermute | solution.py:729
  79.8 4.8 %collective-permute-start.28 = (bf16[32,1024]{1,0:T(8,128)(2,1)S(1)}, bf16[32,1024]{1,0:T(8,128)(2,1)S(1)}, u32[]{:S(2)}, u32[]{:S(2)}) collective-permute-start(bf16[32,1024]{1,0:T(8,128)(2,1)S(1)} %get-tuple-element.83), channel_id=1, source_target_pairs={{0,1},{1,0},{2,3},{3,2},{4,5},{5,4},{6,7},{7,6},{8,9},{9,8},{10,11... | collective-permute-start | bytes 196616 | tf_op jit(solution)/shard_map/ppermute | solution.py:729
  80.4 4.2 %collective-permute-start.26 = (bf16[24,1040]{1,0:T(8,128)(2,1)S(1)}, bf16[24,1040]{1,0:T(8,128)(2,1)S(1)}, u32[]{:S(2)}, u32[]{:S(2)}) collective-permute-start(bf16[24,1040]{1,0:T(8,128)(2,1)S(1)} %concatenate.29), channel_id=1, source_target_pairs={{0,16},{1,17},{2,18},{3,19},{4,20},{5,21},{6,22},{7,23},{8,24},{9,... | collective-permute-start | bytes 149768 | tf_op jit(solution)/shard_map/ppermute | solution.py:729
  (15 other events, 116.2 us)

commit v5 on v4

--- a/solution.py
+++ b/solution.py
@@ -402,7 +402,7 @@
     count, cols = partial.shape
     lanes = 128
     blocks = cols // lanes
-    each = count // 4
+    each = count // 2
     entries = 24
     rank = entries // 3
 
@@ -435,15 +435,15 @@
             acc_ref[:, lo:hi] = base * scale + adapter_scale * change
         for b in range(blocks):
             tall_ref[pl.ds(b, count, stride=blocks), :] = acc_ref[:, b * lanes : (b + 1) * lanes]
-        for a in range(4):
+        for a in range(2):
             part = slice(a * each * blocks, (a + 1) * each * blocks)
-            out_ref[a // 2, a % 2] = tall_ref[part, :].astype(out_ref.dtype)
+            out_ref[a] = tall_ref[part, :].astype(out_ref.dtype)
 
     return pl.pallas_call(
         kernel,
         in_specs=[WHOLE] * 8,
         out_specs=WHOLE,
-        out_shape=jax.ShapeDtypeStruct((2, 2, each * blocks, lanes), jnp.bfloat16),
+        out_shape=jax.ShapeDtypeStruct((2, each * blocks, lanes), jnp.bfloat16),
         scratch_shapes=[
             pltpu.VMEM((count, cols), jnp.float32),
             pltpu.VMEM((count * blocks, lanes), jnp.float32),
@@ -717,16 +717,8 @@
     z = wide_pos >> 2
     right = (z >> 1) == kv_pos
 
-    def is_right(i):
-        return ((i % wide) >> 3) == i // wide
-
-    def swap(x, mask, source=None, target=None):
-        pairs = [(i, i ^ mask) for i in range(2 * wide)]
-        if source is not None:
-            pairs = [p for p in pairs if is_right(p[0]) == source]
-        if target is not None:
-            pairs = [p for p in pairs if is_right(p[1]) == target]
-        return lax.ppermute(x, ("kv", "wide"), pairs)
+    def swap(x, mask):
+        return lax.ppermute(x, ("kv", "wide"), [(i, i ^ mask) for i in range(2 * wide)])
 
     def pick(x, i, axis=0):
         return lax.dynamic_index_in_dim(x, i, axis, keepdims=False)
@@ -763,17 +755,24 @@
         swap(ups_far, 1),
         swap(pick(ups_y, 1 - core, 1), 1),
     )
-    message = jnp.concatenate([partial.astype(bf16), in_two(small)], axis=1)
+
+    own = lax.dynamic_slice_in_dim(partial, (z >> 1) * half, half)
+    away = lax.dynamic_slice_in_dim(partial, (1 - (z >> 1)) * half, half).astype(bf16)
+    across = swap(away, 8)
+    small_h = lax.dynamic_slice_in_dim(small, (z >> 1) * half, half)
+    slot_h = lax.dynamic_slice_in_dim(slot, (z >> 1) * half, half)
+    keep = jnp.where(right, own, across.astype(f32))
+    message = jnp.where(right, across, own.astype(bf16))
+    message = jnp.concatenate([message, in_two(small_h)], axis=1)
+
     o_down = output_down_weight[0].T
     message, o_down = lax.optimization_barrier((message, o_down))
-    from_x = swap(message, 16, target=True)
+    from_x = swap(message, 16)
     o_down_y = swap(o_down, 2)
-    merged = merge(partial, small, from_x, ups, slot)
-
-    across = swap(pick(merged, 1 - (z >> 1)), 8, source=True)
-    half_rows = jnp.where(right, pick(merged, z >> 1), across)
-    beside = swap(pick(half_rows, 1 - (z & 1)), 4)
-    near = jnp.stack([pick(half_rows, z & 1), beside])
+    merged = merge(keep, small_h, from_x, ups, slot_h)
+
+    beside = swap(pick(merged, 1 - (z & 1)), 4)
+    near = jnp.stack([pick(merged, z & 1), beside])
     span = rows * blocks
     keep = lax.dynamic_slice_in_dim(near, y * 2 * span, 2 * span, 1)
     from_y = swap(lax.dynamic_slice_in_dim(near, (1 - y) * 2 * span, 2 * span, 1), 2)
@@ -822,7 +821,7 @@
     from_z = [swap(o_z[1], 4), swap(o_z[2], 8), swap(o_z[3], 12)]
     gathered = (near, near_y)
     gathered += tuple(swap(v, 1) for v in gathered)
-    first, second = depth * 3 // 8, depth * 3 // 4
+    first, second = depth // 2, depth * 7 // 8
     offsets = [(0, 4, 8, 12), (2, 6, 10, 14)]
     offsets += [tuple(v + 1 for v in at) for at in offsets]
     everyone, mixed = ordered_product(gathered, offsets, output_weight, first, rows)

time: 85.8 us -> 81.5 us (0.950)
  waiting for transfers between devices: 24.7 us -> 22.2 us
  starting transfers between devices: 32.5 us -> 30.7 us
    ppermute x29, waiting for transfers between devices: 24.7 us -> 22.2 us  [swap(): lax.ppermute(x, ('kv', 'wide'), [(i, i ^ mask) for i in range(2 * wide)])]
    ppermute x29, starting transfers between devices: 32.5 us -> 30.7 us  [swap(): lax.ppermute(x, ('kv', 'wide'), [(i, i ^ mask) for i in range(2 * wide)])]
  transfers between devices with their start and end apart: 29 -> 29, of which waited for: 16 -> 16; matrix products, arithmetic and copies ran while one was open for 1% -> 2% of each run, Pallas kernels for 21% -> 23%
where the time goes in v5:
time: 81.5 us; the launch traced here: 81.2 us
  starting transfers between devices  30.7 us (38%)
  Pallas kernels  23.7 us (29%)
  waiting for transfers between devices  22.2 us (27%)
  local copies, waits for them, and re-layouts  1.67 us (2%)
  matrix products  1.22 us (1%)
  other arithmetic  1.2 us (1%)
    ppermute x29, starting transfers between devices, swap(): lax.ppermute(x, ('kv', 'wide'), [(i, i ^ mask) for i in range(2 * wide)])  30.7 us
    ppermute x29, waiting for transfers between devices, swap(): lax.ppermute(x, ('kv', 'wide'), [(i, i ^ mask) for i in range(2 * wide)])  22.2 us
    pallas_call x4, Pallas kernels, stream_product(): pl.pallas_call(kernel, in_specs=specs, out_specs=WHOLE, out_shape=jax.Sha...  13.3 us
    pallas_call x1, Pallas kernels, ordered_product(): pl.pallas_call(kernel, in_specs=[WHOLE] * len(groups) + [pl.BlockSpec(mem...  3.77 us
    pallas_call x1, Pallas kernels, prepare(): pl.pallas_call(kernel, in_specs=[SCALARS, WHOLE] + [pl.BlockSpec(memory_s...  3.46 us
  transfers between devices with their start and end apart: 29, of which 16 were waited for; matrix products, arithmetic and copies ran while one was open for 2% of the time, Pallas kernels for 23%

profile of v5, /device:TPU:0, one launch (start us, length us, event | category | flops | bytes accessed | tf_op | source)
XLA Modules:
  0.0 81.2 jit_solution(14727798451621548391)
XLA Ops:
  0.0 3.5 %shard_map.136 = (bf16[16,2560]{1,0:T(8,128)(2,1)}, bf16[16,2560]{1,0:T(8,128)(2,1)}, f32[48,32]{1,0:T(8,128)}, s32[48,1]{1,0:T(8,128)}, f32[48,1]{1,0:T(8,128)}) custom-call(s32[16]{0:T(128)} %owner_ref.1, s32[1,48]{1,0:T(1,128)} %bitcast.97, bf16[48,8192]{1,0:T(8,128)(2,1)} %refs_0_.3, f32[1,8192]{1,0:T(1,128)} %bitcast.59, bf16[24,8192]{1,0:T(8,128)(2,1)} %bitcast.68, ...), custom_call_target="tpu_custom_call" | custom-call | tf_op jit(solution)/shard_map/pallas_call | solution.py:275
  3.5 4.1 %collective-permute-start.1 = (bf16[16,2560]{1,0:T(8,128)(2,1)}, bf16[16,2560]{1,0:T(8,128)(2,1)S(1)}, u32[]{:S(2)}, u32[]{:S(2)}) collective-permute-start(bf16[16,2560]{1,0:T(8,128)(2,1)} %get-tuple-element.40.a_ref), channel_id=1, source_target_pairs={{0,8},{1,9},{2,10},{3,11},{4,12},{5,13},{6,14},{7,15},{8,0},{9,1},... | collective-permute-start | bytes 245768 | tf_op jit(solution)/shard_map/ppermute | solution.py:721
  9.9 4.8 %shard_map.138.refs_4_ = f32[48,1152]{1,0:T(8,128)S(1)} custom-call(bf16[48,8192]{1,0:T(8,128)(2,1)S(1)} %copy-done.1, bf16[8192,1152]{1,0:T(8,128)(2,1)} %refs_1_.5, f32[1,8192]{1,0:T(1,128)S(1)} %bitcast.60), custom_call_target="tpu_custom_call" | custom-call | flops 566231040 | bytes 11796480 | tf_op jit(solution)/shard_map/pallas_call | solution.py:330
  15.2 1.8 %collective-permute-start.3 = (bf16[32,2432]{1,0:T(8,128)(2,1)S(1)}, bf16[32,2432]{1,0:T(8,128)(2,1)S(1)}, u32[]{:S(2)}, u32[]{:S(2)}) collective-permute-start(bf16[32,2432]{1,0:T(8,128)(2,1)S(1)} %get-tuple-element.44.refs_3_), channel_id=1, source_target_pairs={{0,2},{1,3},{2,0},{3,1},{4,6},{5,7},{6,4},{7,5},{8,10},{9,11},{10,... | collective-permute-start | bytes 466952 | tf_op jit(solution)/shard_map/ppermute | solution.py:721
  17.0 3.4 %shard_map.139 = f32[48,1152]{1,0:T(8,128)S(1)} custom-call(bf16[48,8192]{1,0:T(8,128)(2,1)S(1)} %copy-done.1, bf16[8192,1152]{1,0:T(8,128)(2,1)} %refs_1_.5, f32[1,8192]{1,0:T(1,128)S(1)} %bitcast.61, bf16[32,2432]{1,0:T(8,128)(2,1)S(1)} %get-tuple-element.44.refs_3_, f32[48,1152]{1,0:T(8,128)S(1)} %shard_map.138.refs_4_), custom_call_target="tpu_custom_call" | custom-call | flops 339738624 | bytes 7077888 | tf_op jit(solution)/shard_map/pallas_call | solution.py:330
  21.3 3.5 %collective-permute-start.4 = (bf16[24,1152]{1,0:T(8,128)(2,1)S(1)}, bf16[24,1152]{1,0:T(8,128)(2,1)S(1)}, u32[]{:S(2)}, u32[]{:S(2)}) collective-permute-start(bf16[24,1152]{1,0:T(8,128)(2,1)S(1)} %dynamic-slice_convert_fusion), channel_id=1, source_target_pairs={{0,8},{1,9},{2,10},{3,11},{4,12},{5,13},{6,14},{7,15},{8,0},{9,1},... | collective-permute-start | bytes 165896 | tf_op jit(solution)/shard_map/ppermute | solution.py:721
  25.4 3.1 %collective-permute-done.4 = bf16[24,1152]{1,0:T(8,128)(2,1)S(1)} collective-permute-done((bf16[24,1152]{1,0:T(8,128)(2,1)S(1)}, bf16[24,1152]{1,0:T(8,128)(2,1)S(1)}, u32[]{:S(2)}, u32[]{:S(2)}) %collective-permute-start.4) | collective-permute-done | bytes 55328 | tf_op jit(solution)/shard_map/ppermute | solution.py:721
  28.5 1.5 %collective-permute-start.6 = (bf16[24,1216]{1,0:T(8,128)(2,1)S(1)}, bf16[24,1216]{1,0:T(8,128)(2,1)S(1)}, u32[]{:S(2)}, u32[]{:S(2)}) collective-permute-start(bf16[24,1216]{1,0:T(8,128)(2,1)S(1)} %concatenate.25), channel_id=1, source_target_pairs={{0,16},{1,17},{2,18},{3,19},{4,20},{5,21},{6,22},{7,23},{8,24},{9,... | collective-permute-start | bytes 175112 | tf_op jit(solution)/shard_map/ppermute | solution.py:721
  30.1 2.7 %collective-permute-done.6.r_ref = bf16[24,1216]{1,0:T(8,128)(2,1)S(1)} collective-permute-done((bf16[24,1216]{1,0:T(8,128)(2,1)S(1)}, bf16[24,1216]{1,0:T(8,128)(2,1)S(1)}, u32[]{:S(2)}, u32[]{:S(2)}) %collective-permute-start.6) | collective-permute-done | bytes 58400 | tf_op jit(solution)/shard_map/ppermute | solution.py:721
  33.4 3.8 %collective-permute-done.9 = bf16[108,128]{1,0:T(8,128)(2,1)S(1)} collective-permute-done((bf16[108,128]{1,0:T(8,128)(2,1)S(1)}, bf16[108,128]{1,0:T(8,128)(2,1)S(1)}, u32[]{:S(2)}, u32[]{:S(2)}) %collective-permute-start.9) | collective-permute-done | bytes 27680 | tf_op jit(solution)/shard_map/ppermute | solution.py:721
  37.2 1.6 %collective-permute-start.10 = (bf16[2,54,128]{2,1,0:T(8,128)(2,1)S(1)}, bf16[2,54,128]{2,1,0:T(8,128)(2,1)S(1)}, u32[]{:S(2)}, u32[]{:S(2)}) collective-permute-start(bf16[2,54,128]{2,1,0:T(8,128)(2,1)S(1)} %get-tuple-element.88), channel_id=1, source_target_pairs={{0,2},{1,3},{2,0},{3,1},{4,6},{5,7},{6,4},{7,5},{8,10},{9,11},{10,... | collective-permute-start | bytes 82952 | tf_op jit(solution)/shard_map/ppermute | solution.py:721
  38.9 2.3 %collective-permute-done.10 = bf16[2,54,128]{2,1,0:T(8,128)(2,1)S(1)} collective-permute-done((bf16[2,54,128]{2,1,0:T(8,128)(2,1)S(1)}, bf16[2,54,128]{2,1,0:T(8,128)(2,1)S(1)}, u32[]{:S(2)}, u32[]{:S(2)}) %collective-permute-start.10) | collective-permute-done | bytes 27680 | tf_op jit(solution)/shard_map/ppermute | solution.py:721
  46.2 2.9 %collective-permute-start.12 = (bf16[192,128]{1,0:T(8,128)(2,1)S(1)}, bf16[192,128]{1,0:T(8,128)(2,1)S(1)}, u32[]{:S(2)}, u32[]{:S(2)}) collective-permute-start(bf16[192,128]{1,0:T(8,128)(2,1)S(1)} %bitcast.86), channel_id=1, source_target_pairs={{0,4},{1,5},{2,6},{3,7},{4,0},{5,1},{6,2},{7,3},{8,12},{9,13},{10,... | collective-permute-start | bytes 147464 | tf_op jit(solution)/shard_map/ppermute | solution.py:721
  49.0 1.5 %collective-permute-start.17 = (bf16[8,8192]{1,0:T(8,128)(2,1)S(1)}, bf16[8,8192]{1,0:T(8,128)(2,1)S(1)}, u32[]{:S(2)}, u32[]{:S(2)}) collective-permute-start(bf16[8,8192]{1,0:T(8,128)(2,1)S(1)} %bitcast.64), channel_id=1, source_target_pairs={{0,2},{1,3},{2,0},{3,1},{4,6},{5,7},{6,4},{7,5},{8,10},{9,11},{10,... | collective-permute-start | bytes 393224 | tf_op jit(solution)/shard_map/ppermute | solution.py:721
  52.3 1.5 %collective-permute-start.15 = (bf16[4,192,128]{2,1,0:T(8,128)(2,1)S(1)}, bf16[4,192,128]{2,1,0:T(8,128)(2,1)S(1)}, u32[]{:S(2)}, u32[]{:S(2)}) collective-permute-start(bf16[4,192,128]{2,1,0:T(8,128)(2,1)S(1)} %pad_maximum_fusion.p_ref.refs_0_), channel_id=1, source_target_pairs={{0,2},{1,3},{2,0},{3,1},{4,6},{5,7},{6,4},{7,5},{8,10},{9,11},{10,... | collective-permute-start | bytes 589832 | tf_op jit(solution)/shard_map/ppermute | solution.py:721
  56.6 2.5 %collective-permute-done.15.refs_1_ = bf16[4,192,128]{2,1,0:T(8,128)(2,1)S(1)} collective-permute-done((bf16[4,192,128]{2,1,0:T(8,128)(2,1)S(1)}, bf16[4,192,128]{2,1,0:T(8,128)(2,1)S(1)}, u32[]{:S(2)}, u32[]{:S(2)}) %collective-permute-start.15) | collective-permute-done | bytes 196640 | tf_op jit(solution)/shard_map/ppermute | solution.py:721
  59.1 2.0 %collective-permute-start.22 = (bf16[8,4224]{1,0:T(8,128)(2,1)S(1)}, bf16[8,4224]{1,0:T(8,128)(2,1)S(1)}, u32[]{:S(2)}, u32[]{:S(2)}) collective-permute-start(bf16[8,4224]{1,0:T(8,128)(2,1)S(1)} %get-tuple-element.63), channel_id=1, source_target_pairs={{0,8},{1,9},{2,10},{3,11},{4,12},{5,13},{6,14},{7,15},{8,0},{9,1},... | collective-permute-start | bytes 202760 | tf_op jit(solution)/shard_map/ppermute | solution.py:721
  61.1 2.4 %collective-permute-start.23 = (bf16[8,4224]{1,0:T(8,128)(2,1)S(1)}, bf16[8,4224]{1,0:T(8,128)(2,1)S(1)}, u32[]{:S(2)}, u32[]{:S(2)}) collective-permute-start(bf16[8,4224]{1,0:T(8,128)(2,1)S(1)} %get-tuple-element.64), channel_id=1, source_target_pairs={{0,12},{1,13},{2,14},{3,15},{4,8},{5,9},{6,10},{7,11},{8,4},{9,5},... | collective-permute-start | bytes 202760 | tf_op jit(solution)/shard_map/ppermute | solution.py:721
  63.5 3.8 %shard_map.142 = (bf16[48,8192]{1,0:T(8,128)(2,1)S(1)}, f32[48,1024]{1,0:T(8,128)S(1)}) custom-call(bf16[4,192,128]{2,1,0:T(8,128)(2,1)S(1)} %pad_maximum_fusion.p_ref.refs_0_, bf16[4,192,128]{2,1,0:T(8,128)(2,1)S(1)} %collective-permute-done.15.refs_1_, bf16[4,192,128]{2,1,0:T(8,128)(2,1)S(1)} %collective-permute-done.19.refs_2_, ...), custom_call_target="tpu_custom_call" | custom-call | flops 402653184 | bytes 8388608 | tf_op jit(solution)/shard_map/pallas_call | solution.py:507
  68.1 1.4 %collective-permute-start.24 = (bf16[32,2176]{1,0:T(8,128)(2,1)S(1)}, bf16[32,2176]{1,0:T(8,128)(2,1)S(1)}, u32[]{:S(2)}, u32[]{:S(2)}) collective-permute-start(bf16[32,2176]{1,0:T(8,128)(2,1)S(1)} %get-tuple-element.69.refs_2_), channel_id=1, source_target_pairs={{0,2},{1,3},{2,0},{3,1},{4,6},{5,7},{6,4},{7,5},{8,10},{9,11},{10,... | collective-permute-start | bytes 417800 | tf_op jit(solution)/shard_map/ppermute | solution.py:721
  69.5 3.2 %shard_map.144.refs_3_ = f32[48,1024]{1,0:T(8,128)S(1)} custom-call(bf16[48,8192]{1,0:T(8,128)(2,1)S(1)} %get-tuple-element.59.refs_0_, bf16[8192,1024]{1,0:T(8,128)(2,1)} %refs_1_.7, bf16[32,2176]{1,0:T(8,128)(2,1)S(1)} %get-tuple-element.69.refs_2_, f32[48,1024]{1,0:T(8,128)S(1)} %get-tuple-element.70.refs_3_), custom_call_target="tpu_custom_call" | custom-call | flops 301989888 | bytes 6291456 | tf_op jit(solution)/shard_map/pallas_call | solution.py:330
  73.4 1.9 %shard_map.145.m_ref = f32[48,1024]{1,0:T(8,128)S(1)} custom-call(bf16[48,8192]{1,0:T(8,128)(2,1)S(1)} %get-tuple-element.59.refs_0_, bf16[8192,1024]{1,0:T(8,128)(2,1)} %refs_1_.7, f32[2,12,8]{2,1,0:T(8,128)S(1)} %get-tuple-element.104.refs_2_, f32[48,1024]{1,0:T(8,128)S(1)} %shard_map.144.refs_3_), custom_call_target="tpu_custom_call" | custom-call | flops 100663296 | bytes 2097152 | tf_op jit(solution)/shard_map/pallas_call | solution.py:330
  76.1 1.5 %collective-permute-start.26 = (bf16[24,1040]{1,0:T(8,128)(2,1)S(1)}, bf16[24,1040]{1,0:T(8,128)(2,1)S(1)}, u32[]{:S(2)}, u32[]{:S(2)}) collective-permute-start(bf16[24,1040]{1,0:T(8,128)(2,1)S(1)} %concatenate.29), channel_id=1, source_target_pairs={{0,16},{1,17},{2,18},{3,19},{4,20},{5,21},{6,22},{7,23},{8,24},{9,... | collective-permute-start | bytes 149768 | tf_op jit(solution)/shard_map/ppermute | solution.py:721
  77.6 2.7 %collective-permute-done.26.r_ref = bf16[24,1040]{1,0:T(8,128)(2,1)S(1)} collective-permute-done((bf16[24,1040]{1,0:T(8,128)(2,1)S(1)}, bf16[24,1040]{1,0:T(8,128)(2,1)S(1)}, u32[]{:S(2)}, u32[]{:S(2)}) %collective-permute-start.26) | collective-permute-done | bytes 49952 | tf_op jit(solution)/shard_map/ppermute | solution.py:721
  (128 shorter events, 17.8 us)
Async XLA Ops:
  3.5 11.3 %collective-permute-start.1 = (bf16[16,2560]{1,0:T(8,128)(2,1)}, bf16[16,2560]{1,0:T(8,128)(2,1)S(1)}, u32[]{:S(2)}, u32[]{:S(2)}) collective-permute-start(bf16[16,2560]{1,0:T(8,128)(2,1)} %get-tuple-element.40.a_ref), channel_id=1, source_target_pairs={{0,8},{1,9},{2,10},{3,11},{4,12},{5,13},{6,14},{7,15},{8,0},{9,1},... | collective-permute-start | bytes 245768 | tf_op jit(solution)/shard_map/ppermute | solution.py:721
  7.6 7.2 %collective-permute-start.2 = (bf16[16,2560]{1,0:T(8,128)(2,1)}, bf16[16,2560]{1,0:T(8,128)(2,1)S(1)}, u32[]{:S(2)}, u32[]{:S(2)}) collective-permute-start(bf16[16,2560]{1,0:T(8,128)(2,1)} %get-tuple-element.41), channel_id=1, source_target_pairs={{0,12},{1,13},{2,14},{3,15},{4,8},{5,9},{6,10},{7,11},{8,4},{9,5},... | collective-permute-start | bytes 245768 | tf_op jit(solution)/shard_map/ppermute | solution.py:721
  8.9 6.0 %collective-permute-start = (bf16[16,2560]{1,0:T(8,128)(2,1)}, bf16[16,2560]{1,0:T(8,128)(2,1)S(1)}, u32[]{:S(2)}, u32[]{:S(2)}) collective-permute-start(bf16[16,2560]{1,0:T(8,128)(2,1)} %get-tuple-element.41), channel_id=1, source_target_pairs={{0,4},{1,5},{2,6},{3,7},{4,0},{5,1},{6,2},{7,3},{8,12},{9,13},{10,... | collective-permute-start | bytes 245768 | tf_op jit(solution)/shard_map/ppermute | solution.py:721
  15.2 5.3 %collective-permute-start.3 = (bf16[32,2432]{1,0:T(8,128)(2,1)S(1)}, bf16[32,2432]{1,0:T(8,128)(2,1)S(1)}, u32[]{:S(2)}, u32[]{:S(2)}) collective-permute-start(bf16[32,2432]{1,0:T(8,128)(2,1)S(1)} %get-tuple-element.44.refs_3_), channel_id=1, source_target_pairs={{0,2},{1,3},{2,0},{3,1},{4,6},{5,7},{6,4},{7,5},{8,10},{9,11},{10,... | collective-permute-start | bytes 466952 | tf_op jit(solution)/shard_map/ppermute | solution.py:721
  17.0 13.0 %collective-permute-start.7 = (bf16[32,1152]{1,0:T(8,128)(2,1)S(1)}, bf16[32,1152]{1,0:T(8,128)(2,1)S(1)}, u32[]{:S(2)}, u32[]{:S(2)}) collective-permute-start(bf16[32,1152]{1,0:T(8,128)(2,1)S(1)} %get-tuple-element.51), channel_id=1, source_target_pairs={{0,1},{1,0},{2,3},{3,2},{4,5},{5,4},{6,7},{7,6},{8,9},{9,8},{10,11... | collective-permute-start | bytes 221192 | tf_op jit(solution)/shard_map/ppermute | solution.py:721
  20.8 4.6 %collective-permute-start.5 = (f32[48,32]{1,0:T(8,128)S(1)}, f32[48,32]{1,0:T(8,128)S(1)}, u32[]{:S(2)}, u32[]{:S(2)}) collective-permute-start(f32[48,32]{1,0:T(8,128)S(1)} %fusion.10), channel_id=1, source_target_pairs={{0,1},{1,0},{2,3},{3,2},{4,5},{5,4},{6,7},{7,6},{8,9},{9,8},{10,11... | collective-permute-start | bytes 18440 | tf_op jit(solution)/shard_map/ppermute | solution.py:721
  21.3 7.2 %collective-permute-start.4 = (bf16[24,1152]{1,0:T(8,128)(2,1)S(1)}, bf16[24,1152]{1,0:T(8,128)(2,1)S(1)}, u32[]{:S(2)}, u32[]{:S(2)}) collective-permute-start(bf16[24,1152]{1,0:T(8,128)(2,1)S(1)} %dynamic-slice_convert_fusion), channel_id=1, source_target_pairs={{0,8},{1,9},{2,10},{3,11},{4,12},{5,13},{6,14},{7,15},{8,0},{9,1},... | collective-permute-start | bytes 165896 | tf_op jit(solution)/shard_map/ppermute | solution.py:721
  25.1 5.0 %collective-permute-start.8 = (bf16[32,1152]{1,0:T(8,128)(2,1)S(1)}, bf16[32,1152]{1,0:T(8,128)(2,1)S(1)}, u32[]{:S(2)}, u32[]{:S(2)}) collective-permute-start(bf16[32,1152]{1,0:T(8,128)(2,1)S(1)} %bitcast.73), channel_id=1, source_target_pairs={{0,1},{1,0},{2,3},{3,2},{4,5},{5,4},{6,7},{7,6},{8,9},{9,8},{10,11... | collective-permute-start | bytes 221192 | tf_op jit(solution)/shard_map/ppermute | solution.py:721
  28.5 4.2 %collective-permute-start.6 = (bf16[24,1216]{1,0:T(8,128)(2,1)S(1)}, bf16[24,1216]{1,0:T(8,128)(2,1)S(1)}, u32[]{:S(2)}, u32[]{:S(2)}) collective-permute-start(bf16[24,1216]{1,0:T(8,128)(2,1)S(1)} %concatenate.25), channel_id=1, source_target_pairs={{0,16},{1,17},{2,18},{3,19},{4,20},{5,21},{6,22},{7,23},{8,24},{9,... | collective-permute-start | bytes 175112 | tf_op jit(solution)/shard_map/ppermute | solution.py:721
  33.2 3.9 %collective-permute-start.9 = (bf16[108,128]{1,0:T(8,128)(2,1)S(1)}, bf16[108,128]{1,0:T(8,128)(2,1)S(1)}, u32[]{:S(2)}, u32[]{:S(2)}) collective-permute-start(bf16[108,128]{1,0:T(8,128)(2,1)S(1)} %get-tuple-element.89), channel_id=1, source_target_pairs={{0,4},{1,5},{2,6},{3,7},{4,0},{5,1},{6,2},{7,3},{8,12},{9,13},{10,... | collective-permute-start | bytes 82952 | tf_op jit(solution)/shard_map/ppermute | solution.py:721
  44.6 6.5 %collective-permute-start.14 = (bf16[192,128]{1,0:T(8,128)(2,1)S(1)}, bf16[192,128]{1,0:T(8,128)(2,1)S(1)}, u32[]{:S(2)}, u32[]{:S(2)}) collective-permute-start(bf16[192,128]{1,0:T(8,128)(2,1)S(1)} %bitcast.84), channel_id=1, source_target_pairs={{0,12},{1,13},{2,14},{3,15},{4,8},{5,9},{6,10},{7,11},{8,4},{9,5},... | collective-permute-start | bytes 147464 | tf_op jit(solution)/shard_map/ppermute | solution.py:721
  45.7 6.5 %collective-permute-start.13 = (bf16[192,128]{1,0:T(8,128)(2,1)S(1)}, bf16[192,128]{1,0:T(8,128)(2,1)S(1)}, u32[]{:S(2)}, u32[]{:S(2)}) collective-permute-start(bf16[192,128]{1,0:T(8,128)(2,1)S(1)} %bitcast.85), channel_id=1, source_target_pairs={{0,8},{1,9},{2,10},{3,11},{4,12},{5,13},{6,14},{7,15},{8,0},{9,1},... | collective-permute-start | bytes 147464 | tf_op jit(solution)/shard_map/ppermute | solution.py:721
  46.2 6.1 %collective-permute-start.12 = (bf16[192,128]{1,0:T(8,128)(2,1)S(1)}, bf16[192,128]{1,0:T(8,128)(2,1)S(1)}, u32[]{:S(2)}, u32[]{:S(2)}) collective-permute-start(bf16[192,128]{1,0:T(8,128)(2,1)S(1)} %bitcast.86), channel_id=1, source_target_pairs={{0,4},{1,5},{2,6},{3,7},{4,0},{5,1},{6,2},{7,3},{8,12},{9,13},{10,... | collective-permute-start | bytes 147464 | tf_op jit(solution)/shard_map/ppermute | solution.py:721
  49.0 5.0 %collective-permute-start.17 = (bf16[8,8192]{1,0:T(8,128)(2,1)S(1)}, bf16[8,8192]{1,0:T(8,128)(2,1)S(1)}, u32[]{:S(2)}, u32[]{:S(2)}) collective-permute-start(bf16[8,8192]{1,0:T(8,128)(2,1)S(1)} %bitcast.64), channel_id=1, source_target_pairs={{0,2},{1,3},{2,0},{3,1},{4,6},{5,7},{6,4},{7,5},{8,10},{9,11},{10,... | collective-permute-start | bytes 393224 | tf_op jit(solution)/shard_map/ppermute | solution.py:721
  52.3 6.8 %collective-permute-start.15 = (bf16[4,192,128]{2,1,0:T(8,128)(2,1)S(1)}, bf16[4,192,128]{2,1,0:T(8,128)(2,1)S(1)}, u32[]{:S(2)}, u32[]{:S(2)}) collective-permute-start(bf16[4,192,128]{2,1,0:T(8,128)(2,1)S(1)} %pad_maximum_fusion.p_ref.refs_0_), channel_id=1, source_target_pairs={{0,2},{1,3},{2,0},{3,1},{4,6},{5,7},{6,4},{7,5},{8,10},{9,11},{10,... | collective-permute-start | bytes 589832 | tf_op jit(solution)/shard_map/ppermute | solution.py:721
  54.4 9.1 %collective-permute-start.19 = (bf16[4,192,128]{2,1,0:T(8,128)(2,1)S(1)}, bf16[4,192,128]{2,1,0:T(8,128)(2,1)S(1)}, u32[]{:S(2)}, u32[]{:S(2)}) collective-permute-start(bf16[4,192,128]{2,1,0:T(8,128)(2,1)S(1)} %pad_maximum_fusion.p_ref.refs_0_), channel_id=1, source_target_pairs={{0,1},{1,0},{2,3},{3,2},{4,5},{5,4},{6,7},{7,6},{8,9},{9,8},{10,11... | collective-permute-start | bytes 589832 | tf_op jit(solution)/shard_map/ppermute | solution.py:721
  59.1 4.4 %collective-permute-start.20 = (bf16[4,192,128]{2,1,0:T(8,128)(2,1)S(1)}, bf16[4,192,128]{2,1,0:T(8,128)(2,1)S(1)}, u32[]{:S(2)}, u32[]{:S(2)}) collective-permute-start(bf16[4,192,128]{2,1,0:T(8,128)(2,1)S(1)} %collective-permute-done.15.refs_1_), channel_id=1, source_target_pairs={{0,1},{1,0},{2,3},{3,2},{4,5},{5,4},{6,7},{7,6},{8,9},{9,8},{10,11... | collective-permute-start | bytes 589832 | tf_op jit(solution)/shard_map/ppermute | solution.py:721
  59.1 8.2 %collective-permute-start.21 = (bf16[8,4224]{1,0:T(8,128)(2,1)S(1)}, bf16[8,4224]{1,0:T(8,128)(2,1)S(1)}, u32[]{:S(2)}, u32[]{:S(2)}) collective-permute-start(bf16[8,4224]{1,0:T(8,128)(2,1)S(1)} %get-tuple-element.62), channel_id=1, source_target_pairs={{0,4},{1,5},{2,6},{3,7},{4,0},{5,1},{6,2},{7,3},{8,12},{9,13},{10,... | collective-permute-start | bytes 202760 | tf_op jit(solution)/shard_map/ppermute | solution.py:721
  59.1 8.8 %collective-permute-start.22 = (bf16[8,4224]{1,0:T(8,128)(2,1)S(1)}, bf16[8,4224]{1,0:T(8,128)(2,1)S(1)}, u32[]{:S(2)}, u32[]{:S(2)}) collective-permute-start(bf16[8,4224]{1,0:T(8,128)(2,1)S(1)} %get-tuple-element.63), channel_id=1, source_target_pairs={{0,8},{1,9},{2,10},{3,11},{4,12},{5,13},{6,14},{7,15},{8,0},{9,1},... | collective-permute-start | bytes 202760 | tf_op jit(solution)/shard_map/ppermute | solution.py:721
  61.1 6.8 %collective-permute-start.23 = (bf16[8,4224]{1,0:T(8,128)(2,1)S(1)}, bf16[8,4224]{1,0:T(8,128)(2,1)S(1)}, u32[]{:S(2)}, u32[]{:S(2)}) collective-permute-start(bf16[8,4224]{1,0:T(8,128)(2,1)S(1)} %get-tuple-element.64), channel_id=1, source_target_pairs={{0,12},{1,13},{2,14},{3,15},{4,8},{5,9},{6,10},{7,11},{8,4},{9,5},... | collective-permute-start | bytes 202760 | tf_op jit(solution)/shard_map/ppermute | solution.py:721
  68.1 5.1 %collective-permute-start.24 = (bf16[32,2176]{1,0:T(8,128)(2,1)S(1)}, bf16[32,2176]{1,0:T(8,128)(2,1)S(1)}, u32[]{:S(2)}, u32[]{:S(2)}) collective-permute-start(bf16[32,2176]{1,0:T(8,128)(2,1)S(1)} %get-tuple-element.69.refs_2_), channel_id=1, source_target_pairs={{0,2},{1,3},{2,0},{3,1},{4,6},{5,7},{6,4},{7,5},{8,10},{9,11},{10,... | collective-permute-start | bytes 417800 | tf_op jit(solution)/shard_map/ppermute | solution.py:721
  69.5 8.1 %collective-permute-start.27 = (bf16[32,1024]{1,0:T(8,128)(2,1)S(1)}, bf16[32,1024]{1,0:T(8,128)(2,1)S(1)}, u32[]{:S(2)}, u32[]{:S(2)}) collective-permute-start(bf16[32,1024]{1,0:T(8,128)(2,1)S(1)} %get-tuple-element.74), channel_id=1, source_target_pairs={{0,1},{1,0},{2,3},{3,2},{4,5},{5,4},{6,7},{7,6},{8,9},{9,8},{10,11... | collective-permute-start | bytes 196616 | tf_op jit(solution)/shard_map/ppermute | solution.py:721
  75.3 5.0 %collective-permute-start.28 = (bf16[32,1024]{1,0:T(8,128)(2,1)S(1)}, bf16[32,1024]{1,0:T(8,128)(2,1)S(1)}, u32[]{:S(2)}, u32[]{:S(2)}) collective-permute-start(bf16[32,1024]{1,0:T(8,128)(2,1)S(1)} %get-tuple-element.83), channel_id=1, source_target_pairs={{0,1},{1,0},{2,3},{3,2},{4,5},{5,4},{6,7},{7,6},{8,9},{9,8},{10,11... | collective-permute-start | bytes 196616 | tf_op jit(solution)/shard_map/ppermute | solution.py:721
  76.1 4.2 %collective-permute-start.26 = (bf16[24,1040]{1,0:T(8,128)(2,1)S(1)}, bf16[24,1040]{1,0:T(8,128)(2,1)S(1)}, u32[]{:S(2)}, u32[]{:S(2)}) collective-permute-start(bf16[24,1040]{1,0:T(8,128)(2,1)S(1)} %concatenate.29), channel_id=1, source_target_pairs={{0,16},{1,17},{2,18},{3,19},{4,20},{5,21},{6,22},{7,23},{8,24},{9,... | collective-permute-start | bytes 149768 | tf_op jit(solution)/shard_map/ppermute | solution.py:721
  (16 other events, 118.5 us)

commit v6 on v5

--- a/solution.py
+++ b/solution.py
@@ -204,39 +204,41 @@
     span = group_width + 2 * head_dim
     chunk = 1024
     quarter = width // 4
-    held = (hidden_input, gain, down, query_up, key_value_up)
+    held = (hidden_input, gain, down, query_up, key_value_up, adapters, owners)
 
     def kernel(
-        owner_ref, index_ref, x_in, gain_in, down_in, q_in, kv_in,
-        same_ref, flip_ref, small_ref, slot_ref, mine_ref,
-        x_ref, gain_ref, down_ref, q_ref, kv_ref, sem,
+        x_in, gain_in, down_in, q_in, kv_in, index_in, owner_in,
+        same_ref, flip_ref, small_ref, slot_ref,
+        x_ref, gain_ref, down_ref, q_ref, kv_ref, index_ref, owner_ref, sem,
     ):
         def x_copy(i):
             part = (slice(None), pl.ds(i * quarter, quarter))
             return pltpu.make_async_copy(x_in.at[part], x_ref.at[part], sem.at[i])
 
-        pairs = ((gain_in, gain_ref), (down_in, down_ref), (q_in, q_ref), (kv_in, kv_ref))
+        pairs = (
+            (index_in, index_ref), (owner_in, owner_ref), (gain_in, gain_ref),
+            (down_in, down_ref), (q_in, q_ref), (kv_in, kv_ref),
+        )
         copies = [
             pltpu.make_async_copy(src, dst, sem.at[4 + i]) for i, (src, dst) in enumerate(pairs)
         ]
         x_copies = [x_copy(i) for i in range(4)]
-        for copy in copies[:2] + x_copies + copies[2:]:
+        for copy in copies[:3] + x_copies + copies[3:]:
             copy.start()
 
         wide_pos = lax.axis_index("wide")
+        for copy in copies[:3]:
+            copy.wait()
         row = lax.broadcasted_iota(jnp.int32, (count, count), 0)
         column = lax.broadcasted_iota(jnp.int32, (count, count), 1)
         across = jnp.where(row == column, index_ref[...].astype(jnp.float32), 0.0)
         index = jnp.sum(across, axis=1, keepdims=True).astype(jnp.int32)
-        slot = jnp.zeros((count, 1), jnp.int32)
-        for a in range(owners.shape[0]):
-            slot = jnp.where(index == a, owner_ref[a], slot)
+        which = lax.broadcasted_iota(jnp.int32, (count, owners.shape[1]), 1)
+        chosen = jnp.where(index == which, owner_ref[...].astype(jnp.float32), 0.0)
+        slot = jnp.sum(chosen, axis=1, keepdims=True).astype(jnp.int32)
         slot_ref[...] = slot
         mine = (slot == wide_pos).astype(jnp.float32)
-        mine_ref[...] = mine
-
-        for copy in copies[:2]:
-            copy.wait()
+
         total = jnp.zeros((count, 1), jnp.float32)
         for at in range(0, width, chunk):
             part = slice(at, at + chunk)
@@ -245,6 +247,7 @@
             x = x_ref[:, part].astype(jnp.float32)
             total = total + jnp.sum(x * x, axis=1, keepdims=True)
             x_ref[:, part] = (x * gain_ref[:, part]).astype(jnp.bfloat16)
+        copies[3].wait()
         reduced = lax.dot_general(
             x_ref[...], down_ref[...], (((1,), (1,)), ((), ())),
             preferred_element_type=jnp.float32,
@@ -253,7 +256,7 @@
         small_ref[:, :entries] = reduced * mine
         small_ref[:, entries : entries + 1] = total * mine
         small = small_ref[...]
-        for copy in copies[2:]:
+        for copy in copies[4:]:
             copy.wait()
 
         low = (wide_pos >> 2) & 1
@@ -274,19 +277,18 @@
     message = jax.ShapeDtypeStruct((2 * rank, span + 256), query_up.dtype)
     return pl.pallas_call(
         kernel,
-        in_specs=[SCALARS, WHOLE] + [pl.BlockSpec(memory_space=pl.ANY)] * len(held),
-        out_specs=[WHOLE] * 5,
+        in_specs=[pl.BlockSpec(memory_space=pl.ANY)] * len(held),
+        out_specs=[WHOLE] * 4,
         out_shape=[
             message,
             message,
             jax.ShapeDtypeStruct((count, 32), jnp.float32),
             jax.ShapeDtypeStruct((count, 1), jnp.int32),
-            jax.ShapeDtypeStruct((count, 1), jnp.float32),
         ],
         scratch_shapes=[pltpu.VMEM(v.shape, v.dtype) for v in held]
-        + [pltpu.SemaphoreType.DMA((8,))],
+        + [pltpu.SemaphoreType.DMA((10,))],
         compiler_params=pltpu.CompilerParams(vmem_limit_bytes=60 * 2**20),
-    )(owners, adapters, *held)
+    )(*held)
 
 
 def stream_product(rows_in, gain, weight, start, stop, before, marker):
@@ -435,15 +437,16 @@
             acc_ref[:, lo:hi] = base * scale + adapter_scale * change
         for b in range(blocks):
             tall_ref[pl.ds(b, count, stride=blocks), :] = acc_ref[:, b * lanes : (b + 1) * lanes]
-        for a in range(2):
-            part = slice(a * each * blocks, (a + 1) * each * blocks)
-            out_ref[a] = tall_ref[part, :].astype(out_ref.dtype)
+        tall = each * blocks // 2
+        for a in range(4):
+            part = slice(a * tall, (a + 1) * tall)
+            out_ref[a // 2, a % 2] = tall_ref[part, :].astype(out_ref.dtype)
 
     return pl.pallas_call(
         kernel,
         in_specs=[WHOLE] * 8,
         out_specs=WHOLE,
-        out_shape=jax.ShapeDtypeStruct((2, each * blocks, lanes), jnp.bfloat16),
+        out_shape=jax.ShapeDtypeStruct((2, 2, each * blocks // 2, lanes), jnp.bfloat16),
         scratch_shapes=[
             pltpu.VMEM((count, cols), jnp.float32),
             pltpu.VMEM((count * blocks, lanes), jnp.float32),
@@ -726,14 +729,14 @@
     half = batch // 2
 
     gain = input_norm_gain[None]
-    same, flip, small, slot, mine = prepare(
+    same, flip, small, slot = prepare(
         hidden_input,
         gain,
         joint_down_weight[0].T,
         query_up_weight[0],
         key_value_up_weight[0],
         row_adapter_index[None],
-        adapter_owner_slot,
+        adapter_owner_slot[None],
     )
     parts = [same, swap(flip, 4), swap(same, 8), swap(flip, 12)]
     depth = hidden_input.shape[1]
@@ -771,12 +774,14 @@
     o_down_y = swap(o_down, 2)
     merged = merge(keep, small_h, from_x, ups, slot_h)
 
-    beside = swap(pick(merged, 1 - (z & 1)), 4)
-    near = jnp.stack([pick(merged, z & 1), beside])
+    def rows_of(dz, dy):
+        return pick(pick(merged, (z & 1) ^ dz), y ^ dy)
+
     span = rows * blocks
-    keep = lax.dynamic_slice_in_dim(near, y * 2 * span, 2 * span, 1)
-    from_y = swap(lax.dynamic_slice_in_dim(near, (1 - y) * 2 * span, 2 * span, 1), 2)
-    near = jnp.stack([keep, from_y])
+    near = jnp.stack(
+        [rows_of(0, 0), swap(rows_of(1, 0), 4), swap(rows_of(0, 1), 2), swap(rows_of(1, 1), 6)]
+    )
+    near = near.reshape((2, 2) + near.shape[1:])
     far = swap(near, 1)
     near = lax.dynamic_slice_in_dim(near, core * span, span, 2)
     far = lax.dynamic_slice_in_dim(far, core * span, span, 2)

time: 81.5 us -> 78.8 us (0.967)
  waiting for transfers between devices: 22.2 us -> 18.1 us
  starting transfers between devices: 30.7 us -> 32.9 us
    ppermute x29 -> x30, waiting for transfers between devices: 22.2 us -> 18.1 us  [swap(): lax.ppermute(x, ('kv', 'wide'), [(i, i ^ mask) for i in range(2 * wide)])]
    ppermute x29 -> x30, starting transfers between devices: 30.7 us -> 32.9 us  [swap(): lax.ppermute(x, ('kv', 'wide'), [(i, i ^ mask) for i in range(2 * wide)])]
  transfers between devices with their start and end apart: 29 -> 30, of which waited for: 16 -> 15; matrix products, arithmetic and copies ran while one was open for 2% -> 2% of each run, Pallas kernels for 23% -> 23%
where the time goes in v6:
time: 78.8 us; the launch traced here: 78.6 us
  starting transfers between devices  32.9 us (42%)
  Pallas kernels  23 us (29%)
  waiting for transfers between devices  18.1 us (23%)
  local copies, waits for them, and re-layouts  1.68 us (2%)
  matrix products  1.22 us (2%)
  other arithmetic  1.16 us (1%)
    ppermute x30, starting transfers between devices, swap(): lax.ppermute(x, ('kv', 'wide'), [(i, i ^ mask) for i in range(2 * wide)])  32.9 us
    ppermute x30, waiting for transfers between devices, swap(): lax.ppermute(x, ('kv', 'wide'), [(i, i ^ mask) for i in range(2 * wide)])  18.1 us
    pallas_call x4, Pallas kernels, stream_product(): pl.pallas_call(kernel, in_specs=specs, out_specs=WHOLE, out_shape=jax.Sha...  13.2 us
    pallas_call x1, Pallas kernels, ordered_product(): pl.pallas_call(kernel, in_specs=[WHOLE] * len(groups) + [pl.BlockSpec(mem...  3.77 us
    pallas_call x1, Pallas kernels, prepare(): pl.pallas_call(kernel, in_specs=[pl.BlockSpec(memory_space=pl.ANY)] * len...  2.86 us
  transfers between devices with their start and end apart: 30, of which 15 were waited for; matrix products, arithmetic and copies ran while one was open for 2% of the time, Pallas kernels for 23%

profile of v6, /device:TPU:0, one launch (start us, length us, event | category | flops | bytes accessed | tf_op | source)
XLA Modules:
  0.0 78.6 jit_solution(12237412863354949407)
XLA Ops:
  0.0 2.9 %shard_map.136 = (bf16[16,2560]{1,0:T(8,128)(2,1)}, bf16[16,2560]{1,0:T(8,128)(2,1)}, f32[48,32]{1,0:T(8,128)}, s32[48,1]{1,0:T(8,128)}) custom-call(bf16[48,8192]{1,0:T(8,128)(2,1)} %refs_0_.3, f32[1,8192]{1,0:T(1,128)} %bitcast.66, bf16[24,8192]{1,0:T(8,128)(2,1)} %bitcast.75, bf16[8,8192]{1,0:T(8,128)(2,1)} %bitcast.78, bf16[2,8,512]{2,1,0:T(8,128)(2,1)} %bitcast.100, ...), custom_call_target="tpu_custom_call" | custom-call | tf_op jit(solution)/shard_map/pallas_call | solution.py:278
  2.9 4.1 %collective-permute-start.1 = (bf16[16,2560]{1,0:T(8,128)(2,1)}, bf16[16,2560]{1,0:T(8,128)(2,1)S(1)}, u32[]{:S(2)}, u32[]{:S(2)}) collective-permute-start(bf16[16,2560]{1,0:T(8,128)(2,1)} %get-tuple-element.40.a_ref), channel_id=1, source_target_pairs={{0,8},{1,9},{2,10},{3,11},{4,12},{5,13},{6,14},{7,15},{8,0},{9,1},... | collective-permute-start | bytes 245768 | tf_op jit(solution)/shard_map/ppermute | solution.py:724
  7.0 1.4 %collective-permute-start.2 = (bf16[16,2560]{1,0:T(8,128)(2,1)}, bf16[16,2560]{1,0:T(8,128)(2,1)S(1)}, u32[]{:S(2)}, u32[]{:S(2)}) collective-permute-start(bf16[16,2560]{1,0:T(8,128)(2,1)} %get-tuple-element.41), channel_id=1, source_target_pairs={{0,12},{1,13},{2,14},{3,15},{4,8},{5,9},{6,10},{7,11},{8,4},{9,5},... | collective-permute-start | bytes 245768 | tf_op jit(solution)/shard_map/ppermute | solution.py:724
  9.3 4.8 %shard_map.138.refs_4_ = f32[48,1152]{1,0:T(8,128)S(1)} custom-call(bf16[48,8192]{1,0:T(8,128)(2,1)S(1)} %copy-done.1, bf16[8192,1152]{1,0:T(8,128)(2,1)} %refs_1_.5, f32[1,8192]{1,0:T(1,128)S(1)} %bitcast.67), custom_call_target="tpu_custom_call" | custom-call | flops 566231040 | bytes 11796480 | tf_op jit(solution)/shard_map/pallas_call | solution.py:332
  14.7 1.8 %collective-permute-start.3 = (bf16[32,2432]{1,0:T(8,128)(2,1)S(1)}, bf16[32,2432]{1,0:T(8,128)(2,1)S(1)}, u32[]{:S(2)}, u32[]{:S(2)}) collective-permute-start(bf16[32,2432]{1,0:T(8,128)(2,1)S(1)} %get-tuple-element.44.refs_3_), channel_id=1, source_target_pairs={{0,2},{1,3},{2,0},{3,1},{4,6},{5,7},{6,4},{7,5},{8,10},{9,11},{10,... | collective-permute-start | bytes 466952 | tf_op jit(solution)/shard_map/ppermute | solution.py:724
  16.6 3.4 %shard_map.139 = f32[48,1152]{1,0:T(8,128)S(1)} custom-call(bf16[48,8192]{1,0:T(8,128)(2,1)S(1)} %copy-done.1, bf16[8192,1152]{1,0:T(8,128)(2,1)} %refs_1_.5, f32[1,8192]{1,0:T(1,128)S(1)} %bitcast.68, bf16[32,2432]{1,0:T(8,128)(2,1)S(1)} %get-tuple-element.44.refs_3_, f32[48,1152]{1,0:T(8,128)S(1)} %shard_map.138.refs_4_), custom_call_target="tpu_custom_call" | custom-call | flops 339738624 | bytes 7077888 | tf_op jit(solution)/shard_map/pallas_call | solution.py:332
  20.8 3.3 %collective-permute-start.4 = (bf16[24,1152]{1,0:T(8,128)(2,1)S(1)}, bf16[24,1152]{1,0:T(8,128)(2,1)S(1)}, u32[]{:S(2)}, u32[]{:S(2)}) collective-permute-start(bf16[24,1152]{1,0:T(8,128)(2,1)S(1)} %dynamic-slice_convert_fusion), channel_id=1, source_target_pairs={{0,8},{1,9},{2,10},{3,11},{4,12},{5,13},{6,14},{7,15},{8,0},{9,1},... | collective-permute-start | bytes 165896 | tf_op jit(solution)/shard_map/ppermute | solution.py:724
  24.7 3.1 %collective-permute-done.4 = bf16[24,1152]{1,0:T(8,128)(2,1)S(1)} collective-permute-done((bf16[24,1152]{1,0:T(8,128)(2,1)S(1)}, bf16[24,1152]{1,0:T(8,128)(2,1)S(1)}, u32[]{:S(2)}, u32[]{:S(2)}) %collective-permute-start.4) | collective-permute-done | bytes 55328 | tf_op jit(solution)/shard_map/ppermute | solution.py:724
  27.9 1.5 %collective-permute-start.6 = (bf16[24,1216]{1,0:T(8,128)(2,1)S(1)}, bf16[24,1216]{1,0:T(8,128)(2,1)S(1)}, u32[]{:S(2)}, u32[]{:S(2)}) collective-permute-start(bf16[24,1216]{1,0:T(8,128)(2,1)S(1)} %concatenate.25), channel_id=1, source_target_pairs={{0,16},{1,17},{2,18},{3,19},{4,20},{5,21},{6,22},{7,23},{8,24},{9,... | collective-permute-start | bytes 175112 | tf_op jit(solution)/shard_map/ppermute | solution.py:724
  29.4 2.7 %collective-permute-done.6.r_ref = bf16[24,1216]{1,0:T(8,128)(2,1)S(1)} collective-permute-done((bf16[24,1216]{1,0:T(8,128)(2,1)S(1)}, bf16[24,1216]{1,0:T(8,128)(2,1)S(1)}, u32[]{:S(2)}, u32[]{:S(2)}) %collective-permute-start.6) | collective-permute-done | bytes 58400 | tf_op jit(solution)/shard_map/ppermute | solution.py:724
  34.3 1.9 %collective-permute-start.9 = (bf16[54,128]{1,0:T(8,128)(2,1)S(1)}, bf16[54,128]{1,0:T(8,128)(2,1)S(1)}, u32[]{:S(2)}, u32[]{:S(2)}) collective-permute-start(bf16[54,128]{1,0:T(8,128)(2,1)S(1)} %get-tuple-element.90), channel_id=1, source_target_pairs={{0,4},{1,5},{2,6},{3,7},{4,0},{5,1},{6,2},{7,3},{8,12},{9,13},{10,... | collective-permute-start | bytes 41480 | tf_op jit(solution)/shard_map/ppermute | solution.py:724
  41.4 2.9 %collective-permute-start.15 = (bf16[192,128]{1,0:T(8,128)(2,1)S(1)}, bf16[192,128]{1,0:T(8,128)(2,1)S(1)}, u32[]{:S(2)}, u32[]{:S(2)}) collective-permute-start(bf16[192,128]{1,0:T(8,128)(2,1)S(1)} %bitcast.91), channel_id=1, source_target_pairs={{0,12},{1,13},{2,14},{3,15},{4,8},{5,9},{6,10},{7,11},{8,4},{9,5},... | collective-permute-start | bytes 147464 | tf_op jit(solution)/shard_map/ppermute | solution.py:724
  45.9 1.4 %collective-permute-start.18 = (bf16[8,8192]{1,0:T(8,128)(2,1)S(1)}, bf16[8,8192]{1,0:T(8,128)(2,1)S(1)}, u32[]{:S(2)}, u32[]{:S(2)}) collective-permute-start(bf16[8,8192]{1,0:T(8,128)(2,1)S(1)} %bitcast.71), channel_id=1, source_target_pairs={{0,2},{1,3},{2,0},{3,1},{4,6},{5,7},{6,4},{7,5},{8,10},{9,11},{10,... | collective-permute-start | bytes 393224 | tf_op jit(solution)/shard_map/ppermute | solution.py:724
  47.8 2.0 %collective-permute-done.14 = bf16[192,128]{1,0:T(8,128)(2,1)S(1)} collective-permute-done((bf16[192,128]{1,0:T(8,128)(2,1)S(1)}, bf16[192,128]{1,0:T(8,128)(2,1)S(1)}, u32[]{:S(2)}, u32[]{:S(2)}) %collective-permute-start.14) | collective-permute-done | bytes 49184 | tf_op jit(solution)/shard_map/ppermute | solution.py:724
  49.9 1.6 %collective-permute-start.16 = (bf16[4,192,128]{2,1,0:T(8,128)(2,1)S(1)}, bf16[4,192,128]{2,1,0:T(8,128)(2,1)S(1)}, u32[]{:S(2)}, u32[]{:S(2)}) collective-permute-start(bf16[4,192,128]{2,1,0:T(8,128)(2,1)S(1)} %pad_maximum_fusion.p_ref.refs_0_), channel_id=1, source_target_pairs={{0,2},{1,3},{2,0},{3,1},{4,6},{5,7},{6,4},{7,5},{8,10},{9,11},{10,... | collective-permute-start | bytes 589832 | tf_op jit(solution)/shard_map/ppermute | solution.py:724
  54.4 1.9 %collective-permute-done.16.refs_1_ = bf16[4,192,128]{2,1,0:T(8,128)(2,1)S(1)} collective-permute-done((bf16[4,192,128]{2,1,0:T(8,128)(2,1)S(1)}, bf16[4,192,128]{2,1,0:T(8,128)(2,1)S(1)}, u32[]{:S(2)}, u32[]{:S(2)}) %collective-permute-start.16) | collective-permute-done | bytes 196640 | tf_op jit(solution)/shard_map/ppermute | solution.py:724
  56.5 2.3 %collective-permute-start.23 = (bf16[8,4224]{1,0:T(8,128)(2,1)S(1)}, bf16[8,4224]{1,0:T(8,128)(2,1)S(1)}, u32[]{:S(2)}, u32[]{:S(2)}) collective-permute-start(bf16[8,4224]{1,0:T(8,128)(2,1)S(1)} %get-tuple-element.63), channel_id=1, source_target_pairs={{0,8},{1,9},{2,10},{3,11},{4,12},{5,13},{6,14},{7,15},{8,0},{9,1},... | collective-permute-start | bytes 202760 | tf_op jit(solution)/shard_map/ppermute | solution.py:724
  58.8 1.9 %collective-permute-start.24 = (bf16[8,4224]{1,0:T(8,128)(2,1)S(1)}, bf16[8,4224]{1,0:T(8,128)(2,1)S(1)}, u32[]{:S(2)}, u32[]{:S(2)}) collective-permute-start(bf16[8,4224]{1,0:T(8,128)(2,1)S(1)} %get-tuple-element.64), channel_id=1, source_target_pairs={{0,12},{1,13},{2,14},{3,15},{4,8},{5,9},{6,10},{7,11},{8,4},{9,5},... | collective-permute-start | bytes 202760 | tf_op jit(solution)/shard_map/ppermute | solution.py:724
  60.7 3.8 %shard_map.142 = (bf16[48,8192]{1,0:T(8,128)(2,1)S(1)}, f32[48,1024]{1,0:T(8,128)S(1)}) custom-call(bf16[4,192,128]{2,1,0:T(8,128)(2,1)S(1)} %pad_maximum_fusion.p_ref.refs_0_, bf16[4,192,128]{2,1,0:T(8,128)(2,1)S(1)} %collective-permute-done.16.refs_1_, bf16[4,192,128]{2,1,0:T(8,128)(2,1)S(1)} %collective-permute-done.20.refs_2_, ...), custom_call_target="tpu_custom_call" | custom-call | flops 402653184 | bytes 8388608 | tf_op jit(solution)/shard_map/pallas_call | solution.py:510
  65.5 1.6 %collective-permute-start.25 = (bf16[32,2176]{1,0:T(8,128)(2,1)S(1)}, bf16[32,2176]{1,0:T(8,128)(2,1)S(1)}, u32[]{:S(2)}, u32[]{:S(2)}) collective-permute-start(bf16[32,2176]{1,0:T(8,128)(2,1)S(1)} %get-tuple-element.69.refs_2_), channel_id=1, source_target_pairs={{0,2},{1,3},{2,0},{3,1},{4,6},{5,7},{6,4},{7,5},{8,10},{9,11},{10,... | collective-permute-start | bytes 417800 | tf_op jit(solution)/shard_map/ppermute | solution.py:724
  67.1 3.2 %shard_map.144.refs_3_ = f32[48,1024]{1,0:T(8,128)S(1)} custom-call(bf16[48,8192]{1,0:T(8,128)(2,1)S(1)} %get-tuple-element.59.refs_0_, bf16[8192,1024]{1,0:T(8,128)(2,1)} %refs_1_.7, bf16[32,2176]{1,0:T(8,128)(2,1)S(1)} %get-tuple-element.69.refs_2_, f32[48,1024]{1,0:T(8,128)S(1)} %get-tuple-element.70.refs_3_), custom_call_target="tpu_custom_call" | custom-call | flops 301989888 | bytes 6291456 | tf_op jit(solution)/shard_map/pallas_call | solution.py:332
  70.9 1.9 %shard_map.145.m_ref = f32[48,1024]{1,0:T(8,128)S(1)} custom-call(bf16[48,8192]{1,0:T(8,128)(2,1)S(1)} %get-tuple-element.59.refs_0_, bf16[8192,1024]{1,0:T(8,128)(2,1)} %refs_1_.7, f32[2,12,8]{2,1,0:T(8,128)S(1)} %get-tuple-element.104.refs_2_, f32[48,1024]{1,0:T(8,128)S(1)} %shard_map.144.refs_3_), custom_call_target="tpu_custom_call" | custom-call | flops 100663296 | bytes 2097152 | tf_op jit(solution)/shard_map/pallas_call | solution.py:332
  73.4 1.5 %collective-permute-start.27 = (bf16[24,1040]{1,0:T(8,128)(2,1)S(1)}, bf16[24,1040]{1,0:T(8,128)(2,1)S(1)}, u32[]{:S(2)}, u32[]{:S(2)}) collective-permute-start(bf16[24,1040]{1,0:T(8,128)(2,1)S(1)} %concatenate.29), channel_id=1, source_target_pairs={{0,16},{1,17},{2,18},{3,19},{4,20},{5,21},{6,22},{7,23},{8,24},{9,... | collective-permute-start | bytes 149768 | tf_op jit(solution)/shard_map/ppermute | solution.py:724
  74.9 2.7 %collective-permute-done.27.r_ref = bf16[24,1040]{1,0:T(8,128)(2,1)S(1)} collective-permute-done((bf16[24,1040]{1,0:T(8,128)(2,1)S(1)}, bf16[24,1040]{1,0:T(8,128)(2,1)S(1)}, u32[]{:S(2)}, u32[]{:S(2)}) %collective-permute-start.27) | collective-permute-done | bytes 49952 | tf_op jit(solution)/shard_map/ppermute | solution.py:724
  (129 shorter events, 18.7 us)
Async XLA Ops:
  2.9 11.3 %collective-permute-start.1 = (bf16[16,2560]{1,0:T(8,128)(2,1)}, bf16[16,2560]{1,0:T(8,128)(2,1)S(1)}, u32[]{:S(2)}, u32[]{:S(2)}) collective-permute-start(bf16[16,2560]{1,0:T(8,128)(2,1)} %get-tuple-element.40.a_ref), channel_id=1, source_target_pairs={{0,8},{1,9},{2,10},{3,11},{4,12},{5,13},{6,14},{7,15},{8,0},{9,1},... | collective-permute-start | bytes 245768 | tf_op jit(solution)/shard_map/ppermute | solution.py:724
  7.0 7.2 %collective-permute-start.2 = (bf16[16,2560]{1,0:T(8,128)(2,1)}, bf16[16,2560]{1,0:T(8,128)(2,1)S(1)}, u32[]{:S(2)}, u32[]{:S(2)}) collective-permute-start(bf16[16,2560]{1,0:T(8,128)(2,1)} %get-tuple-element.41), channel_id=1, source_target_pairs={{0,12},{1,13},{2,14},{3,15},{4,8},{5,9},{6,10},{7,11},{8,4},{9,5},... | collective-permute-start | bytes 245768 | tf_op jit(solution)/shard_map/ppermute | solution.py:724
  8.3 6.0 %collective-permute-start = (bf16[16,2560]{1,0:T(8,128)(2,1)}, bf16[16,2560]{1,0:T(8,128)(2,1)S(1)}, u32[]{:S(2)}, u32[]{:S(2)}) collective-permute-start(bf16[16,2560]{1,0:T(8,128)(2,1)} %get-tuple-element.41), channel_id=1, source_target_pairs={{0,4},{1,5},{2,6},{3,7},{4,0},{5,1},{6,2},{7,3},{8,12},{9,13},{10,... | collective-permute-start | bytes 245768 | tf_op jit(solution)/shard_map/ppermute | solution.py:724
  14.7 5.3 %collective-permute-start.3 = (bf16[32,2432]{1,0:T(8,128)(2,1)S(1)}, bf16[32,2432]{1,0:T(8,128)(2,1)S(1)}, u32[]{:S(2)}, u32[]{:S(2)}) collective-permute-start(bf16[32,2432]{1,0:T(8,128)(2,1)S(1)} %get-tuple-element.44.refs_3_), channel_id=1, source_target_pairs={{0,2},{1,3},{2,0},{3,1},{4,6},{5,7},{6,4},{7,5},{8,10},{9,11},{10,... | collective-permute-start | bytes 466952 | tf_op jit(solution)/shard_map/ppermute | solution.py:724
  16.5 13.0 %collective-permute-start.7 = (bf16[32,1152]{1,0:T(8,128)(2,1)S(1)}, bf16[32,1152]{1,0:T(8,128)(2,1)S(1)}, u32[]{:S(2)}, u32[]{:S(2)}) collective-permute-start(bf16[32,1152]{1,0:T(8,128)(2,1)S(1)} %get-tuple-element.51), channel_id=1, source_target_pairs={{0,1},{1,0},{2,3},{3,2},{4,5},{5,4},{6,7},{7,6},{8,9},{9,8},{10,11... | collective-permute-start | bytes 221192 | tf_op jit(solution)/shard_map/ppermute | solution.py:724
  20.3 4.5 %collective-permute-start.5 = (f32[48,32]{1,0:T(8,128)S(1)}, f32[48,32]{1,0:T(8,128)S(1)}, u32[]{:S(2)}, u32[]{:S(2)}) collective-permute-start(f32[48,32]{1,0:T(8,128)S(1)} %fusion.6), channel_id=1, source_target_pairs={{0,1},{1,0},{2,3},{3,2},{4,5},{5,4},{6,7},{7,6},{8,9},{9,8},{10,11... | collective-permute-start | bytes 18440 | tf_op jit(solution)/shard_map/ppermute | solution.py:724
  20.8 7.0 %collective-permute-start.4 = (bf16[24,1152]{1,0:T(8,128)(2,1)S(1)}, bf16[24,1152]{1,0:T(8,128)(2,1)S(1)}, u32[]{:S(2)}, u32[]{:S(2)}) collective-permute-start(bf16[24,1152]{1,0:T(8,128)(2,1)S(1)} %dynamic-slice_convert_fusion), channel_id=1, source_target_pairs={{0,8},{1,9},{2,10},{3,11},{4,12},{5,13},{6,14},{7,15},{8,0},{9,1},... | collective-permute-start | bytes 165896 | tf_op jit(solution)/shard_map/ppermute | solution.py:724
  24.5 5.0 %collective-permute-start.8 = (bf16[32,1152]{1,0:T(8,128)(2,1)S(1)}, bf16[32,1152]{1,0:T(8,128)(2,1)S(1)}, u32[]{:S(2)}, u32[]{:S(2)}) collective-permute-start(bf16[32,1152]{1,0:T(8,128)(2,1)S(1)} %bitcast.80), channel_id=1, source_target_pairs={{0,1},{1,0},{2,3},{3,2},{4,5},{5,4},{6,7},{7,6},{8,9},{9,8},{10,11... | collective-permute-start | bytes 221192 | tf_op jit(solution)/shard_map/ppermute | solution.py:724
  27.9 4.2 %collective-permute-start.6 = (bf16[24,1216]{1,0:T(8,128)(2,1)S(1)}, bf16[24,1216]{1,0:T(8,128)(2,1)S(1)}, u32[]{:S(2)}, u32[]{:S(2)}) collective-permute-start(bf16[24,1216]{1,0:T(8,128)(2,1)S(1)} %concatenate.25), channel_id=1, source_target_pairs={{0,16},{1,17},{2,18},{3,19},{4,20},{5,21},{6,22},{7,23},{8,24},{9,... | collective-permute-start | bytes 175112 | tf_op jit(solution)/shard_map/ppermute | solution.py:724
  32.6 4.7 %collective-permute-start.11 = (bf16[54,128]{1,0:T(8,128)(2,1)S(1)}, bf16[54,128]{1,0:T(8,128)(2,1)S(1)}, u32[]{:S(2)}, u32[]{:S(2)}) collective-permute-start(bf16[54,128]{1,0:T(8,128)(2,1)S(1)} %get-tuple-element.88), channel_id=1, source_target_pairs={{0,6},{1,7},{2,4},{3,5},{4,2},{5,3},{6,0},{7,1},{8,14},{9,15},{10,... | collective-permute-start | bytes 41480 | tf_op jit(solution)/shard_map/ppermute | solution.py:724
  41.4 6.4 %collective-permute-start.15 = (bf16[192,128]{1,0:T(8,128)(2,1)S(1)}, bf16[192,128]{1,0:T(8,128)(2,1)S(1)}, u32[]{:S(2)}, u32[]{:S(2)}) collective-permute-start(bf16[192,128]{1,0:T(8,128)(2,1)S(1)} %bitcast.91), channel_id=1, source_target_pairs={{0,12},{1,13},{2,14},{3,15},{4,8},{5,9},{6,10},{7,11},{8,4},{9,5},... | collective-permute-start | bytes 147464 | tf_op jit(solution)/shard_map/ppermute | solution.py:724
  44.3 5.5 %collective-permute-start.14 = (bf16[192,128]{1,0:T(8,128)(2,1)S(1)}, bf16[192,128]{1,0:T(8,128)(2,1)S(1)}, u32[]{:S(2)}, u32[]{:S(2)}) collective-permute-start(bf16[192,128]{1,0:T(8,128)(2,1)S(1)} %bitcast.92), channel_id=1, source_target_pairs={{0,8},{1,9},{2,10},{3,11},{4,12},{5,13},{6,14},{7,15},{8,0},{9,1},... | collective-permute-start | bytes 147464 | tf_op jit(solution)/shard_map/ppermute | solution.py:724
  44.8 5.1 %collective-permute-start.13 = (bf16[192,128]{1,0:T(8,128)(2,1)S(1)}, bf16[192,128]{1,0:T(8,128)(2,1)S(1)}, u32[]{:S(2)}, u32[]{:S(2)}) collective-permute-start(bf16[192,128]{1,0:T(8,128)(2,1)S(1)} %bitcast.93), channel_id=1, source_target_pairs={{0,4},{1,5},{2,6},{3,7},{4,0},{5,1},{6,2},{7,3},{8,12},{9,13},{10,... | collective-permute-start | bytes 147464 | tf_op jit(solution)/shard_map/ppermute | solution.py:724
  45.9 5.7 %collective-permute-start.18 = (bf16[8,8192]{1,0:T(8,128)(2,1)S(1)}, bf16[8,8192]{1,0:T(8,128)(2,1)S(1)}, u32[]{:S(2)}, u32[]{:S(2)}) collective-permute-start(bf16[8,8192]{1,0:T(8,128)(2,1)S(1)} %bitcast.71), channel_id=1, source_target_pairs={{0,2},{1,3},{2,0},{3,1},{4,6},{5,7},{6,4},{7,5},{8,10},{9,11},{10,... | collective-permute-start | bytes 393224 | tf_op jit(solution)/shard_map/ppermute | solution.py:724
  49.9 6.4 %collective-permute-start.16 = (bf16[4,192,128]{2,1,0:T(8,128)(2,1)S(1)}, bf16[4,192,128]{2,1,0:T(8,128)(2,1)S(1)}, u32[]{:S(2)}, u32[]{:S(2)}) collective-permute-start(bf16[4,192,128]{2,1,0:T(8,128)(2,1)S(1)} %pad_maximum_fusion.p_ref.refs_0_), channel_id=1, source_target_pairs={{0,2},{1,3},{2,0},{3,1},{4,6},{5,7},{6,4},{7,5},{8,10},{9,11},{10,... | collective-permute-start | bytes 589832 | tf_op jit(solution)/shard_map/ppermute | solution.py:724
  52.2 8.5 %collective-permute-start.20 = (bf16[4,192,128]{2,1,0:T(8,128)(2,1)S(1)}, bf16[4,192,128]{2,1,0:T(8,128)(2,1)S(1)}, u32[]{:S(2)}, u32[]{:S(2)}) collective-permute-start(bf16[4,192,128]{2,1,0:T(8,128)(2,1)S(1)} %pad_maximum_fusion.p_ref.refs_0_), channel_id=1, source_target_pairs={{0,1},{1,0},{2,3},{3,2},{4,5},{5,4},{6,7},{7,6},{8,9},{9,8},{10,11... | collective-permute-start | bytes 589832 | tf_op jit(solution)/shard_map/ppermute | solution.py:724
  56.3 4.4 %collective-permute-start.21 = (bf16[4,192,128]{2,1,0:T(8,128)(2,1)S(1)}, bf16[4,192,128]{2,1,0:T(8,128)(2,1)S(1)}, u32[]{:S(2)}, u32[]{:S(2)}) collective-permute-start(bf16[4,192,128]{2,1,0:T(8,128)(2,1)S(1)} %collective-permute-done.16.refs_1_), channel_id=1, source_target_pairs={{0,1},{1,0},{2,3},{3,2},{4,5},{5,4},{6,7},{7,6},{8,9},{9,8},{10,11... | collective-permute-start | bytes 589832 | tf_op jit(solution)/shard_map/ppermute | solution.py:724
  56.3 8.2 %collective-permute-start.22 = (bf16[8,4224]{1,0:T(8,128)(2,1)S(1)}, bf16[8,4224]{1,0:T(8,128)(2,1)S(1)}, u32[]{:S(2)}, u32[]{:S(2)}) collective-permute-start(bf16[8,4224]{1,0:T(8,128)(2,1)S(1)} %get-tuple-element.62), channel_id=1, source_target_pairs={{0,4},{1,5},{2,6},{3,7},{4,0},{5,1},{6,2},{7,3},{8,12},{9,13},{10,... | collective-permute-start | bytes 202760 | tf_op jit(solution)/shard_map/ppermute | solution.py:724
  56.5 8.8 %collective-permute-start.23 = (bf16[8,4224]{1,0:T(8,128)(2,1)S(1)}, bf16[8,4224]{1,0:T(8,128)(2,1)S(1)}, u32[]{:S(2)}, u32[]{:S(2)}) collective-permute-start(bf16[8,4224]{1,0:T(8,128)(2,1)S(1)} %get-tuple-element.63), channel_id=1, source_target_pairs={{0,8},{1,9},{2,10},{3,11},{4,12},{5,13},{6,14},{7,15},{8,0},{9,1},... | collective-permute-start | bytes 202760 | tf_op jit(solution)/shard_map/ppermute | solution.py:724
  58.8 6.5 %collective-permute-start.24 = (bf16[8,4224]{1,0:T(8,128)(2,1)S(1)}, bf16[8,4224]{1,0:T(8,128)(2,1)S(1)}, u32[]{:S(2)}, u32[]{:S(2)}) collective-permute-start(bf16[8,4224]{1,0:T(8,128)(2,1)S(1)} %get-tuple-element.64), channel_id=1, source_target_pairs={{0,12},{1,13},{2,14},{3,15},{4,8},{5,9},{6,10},{7,11},{8,4},{9,5},... | collective-permute-start | bytes 202760 | tf_op jit(solution)/shard_map/ppermute | solution.py:724
  65.5 5.1 %collective-permute-start.25 = (bf16[32,2176]{1,0:T(8,128)(2,1)S(1)}, bf16[32,2176]{1,0:T(8,128)(2,1)S(1)}, u32[]{:S(2)}, u32[]{:S(2)}) collective-permute-start(bf16[32,2176]{1,0:T(8,128)(2,1)S(1)} %get-tuple-element.69.refs_2_), channel_id=1, source_target_pairs={{0,2},{1,3},{2,0},{3,1},{4,6},{5,7},{6,4},{7,5},{8,10},{9,11},{10,... | collective-permute-start | bytes 417800 | tf_op jit(solution)/shard_map/ppermute | solution.py:724
  67.1 7.9 %collective-permute-start.28 = (bf16[32,1024]{1,0:T(8,128)(2,1)S(1)}, bf16[32,1024]{1,0:T(8,128)(2,1)S(1)}, u32[]{:S(2)}, u32[]{:S(2)}) collective-permute-start(bf16[32,1024]{1,0:T(8,128)(2,1)S(1)} %get-tuple-element.74), channel_id=1, source_target_pairs={{0,1},{1,0},{2,3},{3,2},{4,5},{5,4},{6,7},{7,6},{8,9},{9,8},{10,11... | collective-permute-start | bytes 196616 | tf_op jit(solution)/shard_map/ppermute | solution.py:724
  72.8 4.8 %collective-permute-start.29 = (bf16[32,1024]{1,0:T(8,128)(2,1)S(1)}, bf16[32,1024]{1,0:T(8,128)(2,1)S(1)}, u32[]{:S(2)}, u32[]{:S(2)}) collective-permute-start(bf16[32,1024]{1,0:T(8,128)(2,1)S(1)} %get-tuple-element.83), channel_id=1, source_target_pairs={{0,1},{1,0},{2,3},{3,2},{4,5},{5,4},{6,7},{7,6},{8,9},{9,8},{10,11... | collective-permute-start | bytes 196616 | tf_op jit(solution)/shard_map/ppermute | solution.py:724
  73.4 4.2 %collective-permute-start.27 = (bf16[24,1040]{1,0:T(8,128)(2,1)S(1)}, bf16[24,1040]{1,0:T(8,128)(2,1)S(1)}, u32[]{:S(2)}, u32[]{:S(2)}) collective-permute-start(bf16[24,1040]{1,0:T(8,128)(2,1)S(1)} %concatenate.29), channel_id=1, source_target_pairs={{0,16},{1,17},{2,18},{3,19},{4,20},{5,21},{6,22},{7,23},{8,24},{9,... | collective-permute-start | bytes 149768 | tf_op jit(solution)/shard_map/ppermute | solution.py:724
  (17 other events, 116.4 us)

commit v7 on v6

--- a/solution.py
+++ b/solution.py
@@ -751,13 +751,6 @@
     coded = from_y[:, 2 * cols :].reshape(2, 16, 2, 64).transpose(2, 0, 1, 3).reshape(-1, 64)
     small = small + from_two(coded[:batch])
     small = small + swap(small, 1)
-    ups_y = from_y[:, : 2 * cols].reshape(-1, 2, cols)
-    ups = (
-        ups_near,
-        pick(ups_y, core, 1),
-        swap(ups_far, 1),
-        swap(pick(ups_y, 1 - core, 1), 1),
-    )
 
     own = lax.dynamic_slice_in_dim(partial, (z >> 1) * half, half)
     away = lax.dynamic_slice_in_dim(partial, (1 - (z >> 1)) * half, half).astype(bf16)
@@ -769,7 +762,15 @@
     message = jnp.concatenate([message, in_two(small_h)], axis=1)
 
     o_down = output_down_weight[0].T
-    message, o_down = lax.optimization_barrier((message, o_down))
+    message, o_down, ups_far, from_y = lax.optimization_barrier(
+        (message, o_down, ups_far, from_y)
+    )
+    ups = (
+        ups_near,
+        lax.dynamic_slice_in_dim(from_y, core * cols, cols, 1),
+        swap(ups_far, 1),
+        swap(lax.dynamic_slice_in_dim(from_y, (1 - core) * cols, cols, 1), 1),
+    )
     from_x = swap(message, 16)
     o_down_y = swap(o_down, 2)
     merged = merge(keep, small_h, from_x, ups, slot_h)
@@ -838,7 +839,7 @@
     o_rows = jnp.stack([o_rows, from_two(o_far[: 4 * rows, 2 * out_cols :][:, : 2 * rank])])
     o_far_c = lax.dynamic_slice_in_dim(o_far, (1 - core) * out_cols, out_cols, 1)
     o_far_n = lax.dynamic_slice_in_dim(o_far, core * out_cols, out_cols, 1)
-    o_ups = (o_near, o_far_n, swap(o_near_c, 1), swap(o_far_c, 1))
+    o_near_c = swap(o_near_c, 1)
     o_rows_c = swap(o_rows, 1)
     mixed = stream_product(everyone, None, output_weight, second, depth, mixed, o_rows)
     o_rows = jnp.stack([o_rows, o_rows_c], axis=1)
@@ -848,7 +849,10 @@
 
     give_out = lax.dynamic_slice_in_dim(mixed, (1 - kv_pos) * half, half).astype(bf16)
     o_give = in_two(lax.dynamic_slice_in_dim(o_rows, (1 - kv_pos) * half, half))
-    from_x = swap(jnp.concatenate([give_out, o_give], axis=1), 16)
+    message = jnp.concatenate([give_out, o_give], axis=1)
+    message, o_far_c = lax.optimization_barrier((message, o_far_c))
+    from_x = swap(message, 16)
+    o_ups = (o_near, o_far_n, o_near_c, swap(o_far_c, 1))
     return finish(mixed, from_x, o_rows, slot, o_ups)
 
 

time: 78.8 us -> 78.7 us (level)
  transfers between devices with their start and end apart: 30 -> 30, of which waited for: 15 -> 15; matrix products, arithmetic and copies ran while one was open for 2% -> 1% of each run, Pallas kernels for 23% -> 23%
where the time goes in v7:
time: 78.7 us; the launch traced here: 78.5 us
  starting transfers between devices  33.1 us (42%)
  Pallas kernels  23 us (29%)
  waiting for transfers between devices  18.2 us (23%)
  local copies, waits for them, and re-layouts  1.33 us (2%)
  matrix products  1.22 us (2%)
  other arithmetic  1.16 us (1%)
    ppermute x30, starting transfers between devices, swap(): lax.ppermute(x, ('kv', 'wide'), [(i, i ^ mask) for i in range(2 * wide)])  33.1 us
    ppermute x30, waiting for transfers between devices, swap(): lax.ppermute(x, ('kv', 'wide'), [(i, i ^ mask) for i in range(2 * wide)])  18.2 us
    pallas_call x4, Pallas kernels, stream_product(): pl.pallas_call(kernel, in_specs=specs, out_specs=WHOLE, out_shape=jax.Sha...  13.2 us
    pallas_call x1, Pallas kernels, ordered_product(): pl.pallas_call(kernel, in_specs=[WHOLE] * len(groups) + [pl.BlockSpec(mem...  3.77 us
    pallas_call x1, Pallas kernels, prepare(): pl.pallas_call(kernel, in_specs=[pl.BlockSpec(memory_space=pl.ANY)] * len...  2.86 us
  transfers between devices with their start and end apart: 30, of which 15 were waited for; matrix products, arithmetic and copies ran while one was open for 1% of the time, Pallas kernels for 23%

profile of v7, /device:TPU:0, one launch (start us, length us, event | category | flops | bytes accessed | tf_op | source)
XLA Modules:
  0.0 78.5 jit_solution(8878682068046325202)
XLA Ops:
  0.0 2.9 %shard_map.136 = (bf16[16,2560]{1,0:T(8,128)(2,1)}, bf16[16,2560]{1,0:T(8,128)(2,1)}, f32[48,32]{1,0:T(8,128)}, s32[48,1]{1,0:T(8,128)}) custom-call(bf16[48,8192]{1,0:T(8,128)(2,1)} %refs_0_.3, f32[1,8192]{1,0:T(1,128)} %bitcast.59, bf16[24,8192]{1,0:T(8,128)(2,1)} %bitcast.67, bf16[8,8192]{1,0:T(8,128)(2,1)} %bitcast.70, bf16[2,8,512]{2,1,0:T(8,128)(2,1)} %bitcast.92, ...), custom_call_target="tpu_custom_call" | custom-call | tf_op jit(solution)/shard_map/pallas_call | solution.py:278
  2.9 4.1 %collective-permute-start.1 = (bf16[16,2560]{1,0:T(8,128)(2,1)}, bf16[16,2560]{1,0:T(8,128)(2,1)S(1)}, u32[]{:S(2)}, u32[]{:S(2)}) collective-permute-start(bf16[16,2560]{1,0:T(8,128)(2,1)} %get-tuple-element.44.a_ref), channel_id=1, source_target_pairs={{0,8},{1,9},{2,10},{3,11},{4,12},{5,13},{6,14},{7,15},{8,0},{9,1},... | collective-permute-start | bytes 245768 | tf_op jit(solution)/shard_map/ppermute | solution.py:724
  7.0 1.4 %collective-permute-start.2 = (bf16[16,2560]{1,0:T(8,128)(2,1)}, bf16[16,2560]{1,0:T(8,128)(2,1)S(1)}, u32[]{:S(2)}, u32[]{:S(2)}) collective-permute-start(bf16[16,2560]{1,0:T(8,128)(2,1)} %get-tuple-element.45), channel_id=1, source_target_pairs={{0,12},{1,13},{2,14},{3,15},{4,8},{5,9},{6,10},{7,11},{8,4},{9,5},... | collective-permute-start | bytes 245768 | tf_op jit(solution)/shard_map/ppermute | solution.py:724
  9.3 4.8 %shard_map.138.refs_4_ = f32[48,1152]{1,0:T(8,128)S(1)} custom-call(bf16[48,8192]{1,0:T(8,128)(2,1)S(1)} %copy-done.1, bf16[8192,1152]{1,0:T(8,128)(2,1)} %refs_1_.5, f32[1,8192]{1,0:T(1,128)S(1)} %bitcast.60), custom_call_target="tpu_custom_call" | custom-call | flops 566231040 | bytes 11796480 | tf_op jit(solution)/shard_map/pallas_call | solution.py:332
  14.7 1.8 %collective-permute-start.3 = (bf16[32,2432]{1,0:T(8,128)(2,1)S(1)}, bf16[32,2432]{1,0:T(8,128)(2,1)S(1)}, u32[]{:S(2)}, u32[]{:S(2)}) collective-permute-start(bf16[32,2432]{1,0:T(8,128)(2,1)S(1)} %get-tuple-element.48.refs_3_), channel_id=1, source_target_pairs={{0,2},{1,3},{2,0},{3,1},{4,6},{5,7},{6,4},{7,5},{8,10},{9,11},{10,... | collective-permute-start | bytes 466952 | tf_op jit(solution)/shard_map/ppermute | solution.py:724
  16.5 3.4 %shard_map.139 = f32[48,1152]{1,0:T(8,128)S(1)} custom-call(bf16[48,8192]{1,0:T(8,128)(2,1)S(1)} %copy-done.1, bf16[8192,1152]{1,0:T(8,128)(2,1)} %refs_1_.5, f32[1,8192]{1,0:T(1,128)S(1)} %bitcast.61, bf16[32,2432]{1,0:T(8,128)(2,1)S(1)} %get-tuple-element.48.refs_3_, f32[48,1152]{1,0:T(8,128)S(1)} %shard_map.138.refs_4_), custom_call_target="tpu_custom_call" | custom-call | flops 339738624 | bytes 7077888 | tf_op jit(solution)/shard_map/pallas_call | solution.py:332
  20.2 3.9 %collective-permute-start.4 = (bf16[24,1152]{1,0:T(8,128)(2,1)S(1)}, bf16[24,1152]{1,0:T(8,128)(2,1)S(1)}, u32[]{:S(2)}, u32[]{:S(2)}) collective-permute-start(bf16[24,1152]{1,0:T(8,128)(2,1)S(1)} %dynamic-slice_convert_fusion), channel_id=1, source_target_pairs={{0,8},{1,9},{2,10},{3,11},{4,12},{5,13},{6,14},{7,15},{8,0},{9,1},... | collective-permute-start | bytes 165896 | tf_op jit(solution)/shard_map/ppermute | solution.py:724
  24.1 3.7 %collective-permute-done.4 = bf16[24,1152]{1,0:T(8,128)(2,1)S(1)} collective-permute-done((bf16[24,1152]{1,0:T(8,128)(2,1)S(1)}, bf16[24,1152]{1,0:T(8,128)(2,1)S(1)}, u32[]{:S(2)}, u32[]{:S(2)}) %collective-permute-start.4) | collective-permute-done | bytes 55328 | tf_op jit(solution)/shard_map/ppermute | solution.py:724
  27.9 1.5 %collective-permute-start.6 = (bf16[24,1216]{1,0:T(8,128)(2,1)S(1)}, bf16[24,1216]{1,0:T(8,128)(2,1)S(1)}, u32[]{:S(2)}, u32[]{:S(2)}) collective-permute-start(bf16[24,1216]{1,0:T(8,128)(2,1)S(1)} %concatenate.25), channel_id=1, source_target_pairs={{0,16},{1,17},{2,18},{3,19},{4,20},{5,21},{6,22},{7,23},{8,24},{9,... | collective-permute-start | bytes 175112 | tf_op jit(solution)/shard_map/ppermute | solution.py:724
  30.0 2.1 %collective-permute-done.6.r_ref = bf16[24,1216]{1,0:T(8,128)(2,1)S(1)} collective-permute-done((bf16[24,1216]{1,0:T(8,128)(2,1)S(1)}, bf16[24,1216]{1,0:T(8,128)(2,1)S(1)}, u32[]{:S(2)}, u32[]{:S(2)}) %collective-permute-start.6) | collective-permute-done | bytes 58400 | tf_op jit(solution)/shard_map/ppermute | solution.py:724
  34.2 1.9 %collective-permute-start.9 = (bf16[54,128]{1,0:T(8,128)(2,1)S(1)}, bf16[54,128]{1,0:T(8,128)(2,1)S(1)}, u32[]{:S(2)}, u32[]{:S(2)}) collective-permute-start(bf16[54,128]{1,0:T(8,128)(2,1)S(1)} %get-tuple-element.98), channel_id=1, source_target_pairs={{0,4},{1,5},{2,6},{3,7},{4,0},{5,1},{6,2},{7,3},{8,12},{9,13},{10,... | collective-permute-start | bytes 41480 | tf_op jit(solution)/shard_map/ppermute | solution.py:724
  41.4 2.9 %collective-permute-start.15 = (bf16[192,128]{1,0:T(8,128)(2,1)S(1)}, bf16[192,128]{1,0:T(8,128)(2,1)S(1)}, u32[]{:S(2)}, u32[]{:S(2)}) collective-permute-start(bf16[192,128]{1,0:T(8,128)(2,1)S(1)} %bitcast.83), channel_id=1, source_target_pairs={{0,12},{1,13},{2,14},{3,15},{4,8},{5,9},{6,10},{7,11},{8,4},{9,5},... | collective-permute-start | bytes 147464 | tf_op jit(solution)/shard_map/ppermute | solution.py:724
  45.8 1.4 %collective-permute-start.18 = (bf16[8,8192]{1,0:T(8,128)(2,1)S(1)}, bf16[8,8192]{1,0:T(8,128)(2,1)S(1)}, u32[]{:S(2)}, u32[]{:S(2)}) collective-permute-start(bf16[8,8192]{1,0:T(8,128)(2,1)S(1)} %bitcast.63), channel_id=1, source_target_pairs={{0,2},{1,3},{2,0},{3,1},{4,6},{5,7},{6,4},{7,5},{8,10},{9,11},{10,... | collective-permute-start | bytes 393224 | tf_op jit(solution)/shard_map/ppermute | solution.py:724
  47.8 2.0 %collective-permute-done.14 = bf16[192,128]{1,0:T(8,128)(2,1)S(1)} collective-permute-done((bf16[192,128]{1,0:T(8,128)(2,1)S(1)}, bf16[192,128]{1,0:T(8,128)(2,1)S(1)}, u32[]{:S(2)}, u32[]{:S(2)}) %collective-permute-start.14) | collective-permute-done | bytes 49184 | tf_op jit(solution)/shard_map/ppermute | solution.py:724
  49.9 1.6 %collective-permute-start.16 = (bf16[4,192,128]{2,1,0:T(8,128)(2,1)S(1)}, bf16[4,192,128]{2,1,0:T(8,128)(2,1)S(1)}, u32[]{:S(2)}, u32[]{:S(2)}) collective-permute-start(bf16[4,192,128]{2,1,0:T(8,128)(2,1)S(1)} %pad_maximum_fusion.p_ref.refs_0_), channel_id=1, source_target_pairs={{0,2},{1,3},{2,0},{3,1},{4,6},{5,7},{6,4},{7,5},{8,10},{9,11},{10,... | collective-permute-start | bytes 589832 | tf_op jit(solution)/shard_map/ppermute | solution.py:724
  54.3 1.9 %collective-permute-done.16.refs_1_ = bf16[4,192,128]{2,1,0:T(8,128)(2,1)S(1)} collective-permute-done((bf16[4,192,128]{2,1,0:T(8,128)(2,1)S(1)}, bf16[4,192,128]{2,1,0:T(8,128)(2,1)S(1)}, u32[]{:S(2)}, u32[]{:S(2)}) %collective-permute-start.16) | collective-permute-done | bytes 196640 | tf_op jit(solution)/shard_map/ppermute | solution.py:724
  56.4 2.7 %collective-permute-start.23 = (bf16[8,4224]{1,0:T(8,128)(2,1)S(1)}, bf16[8,4224]{1,0:T(8,128)(2,1)S(1)}, u32[]{:S(2)}, u32[]{:S(2)}) collective-permute-start(bf16[8,4224]{1,0:T(8,128)(2,1)S(1)} %get-tuple-element.69), channel_id=1, source_target_pairs={{0,8},{1,9},{2,10},{3,11},{4,12},{5,13},{6,14},{7,15},{8,0},{9,1},... | collective-permute-start | bytes 202760 | tf_op jit(solution)/shard_map/ppermute | solution.py:724
  59.1 1.5 %collective-permute-start.24 = (bf16[8,4224]{1,0:T(8,128)(2,1)S(1)}, bf16[8,4224]{1,0:T(8,128)(2,1)S(1)}, u32[]{:S(2)}, u32[]{:S(2)}) collective-permute-start(bf16[8,4224]{1,0:T(8,128)(2,1)S(1)} %get-tuple-element.70), channel_id=1, source_target_pairs={{0,12},{1,13},{2,14},{3,15},{4,8},{5,9},{6,10},{7,11},{8,4},{9,5},... | collective-permute-start | bytes 202760 | tf_op jit(solution)/shard_map/ppermute | solution.py:724
  60.6 3.8 %shard_map.142 = (bf16[48,8192]{1,0:T(8,128)(2,1)S(1)}, f32[48,1024]{1,0:T(8,128)S(1)}) custom-call(bf16[4,192,128]{2,1,0:T(8,128)(2,1)S(1)} %pad_maximum_fusion.p_ref.refs_0_, bf16[4,192,128]{2,1,0:T(8,128)(2,1)S(1)} %collective-permute-done.16.refs_1_, bf16[4,192,128]{2,1,0:T(8,128)(2,1)S(1)} %collective-permute-done.20.refs_2_, ...), custom_call_target="tpu_custom_call" | custom-call | flops 402653184 | bytes 8388608 | tf_op jit(solution)/shard_map/pallas_call | solution.py:510
  65.5 1.5 %collective-permute-start.25 = (bf16[32,2176]{1,0:T(8,128)(2,1)S(1)}, bf16[32,2176]{1,0:T(8,128)(2,1)S(1)}, u32[]{:S(2)}, u32[]{:S(2)}) collective-permute-start(bf16[32,2176]{1,0:T(8,128)(2,1)S(1)} %get-tuple-element.75.refs_2_), channel_id=1, source_target_pairs={{0,2},{1,3},{2,0},{3,1},{4,6},{5,7},{6,4},{7,5},{8,10},{9,11},{10,... | collective-permute-start | bytes 417800 | tf_op jit(solution)/shard_map/ppermute | solution.py:724
  67.0 3.2 %shard_map.144.refs_3_ = f32[48,1024]{1,0:T(8,128)S(1)} custom-call(bf16[48,8192]{1,0:T(8,128)(2,1)S(1)} %get-tuple-element.65.refs_0_, bf16[8192,1024]{1,0:T(8,128)(2,1)} %refs_1_.7, bf16[32,2176]{1,0:T(8,128)(2,1)S(1)} %get-tuple-element.75.refs_2_, f32[48,1024]{1,0:T(8,128)S(1)} %get-tuple-element.76.refs_3_), custom_call_target="tpu_custom_call" | custom-call | flops 301989888 | bytes 6291456 | tf_op jit(solution)/shard_map/pallas_call | solution.py:332
  70.8 1.9 %shard_map.145.m_ref = f32[48,1024]{1,0:T(8,128)S(1)} custom-call(bf16[48,8192]{1,0:T(8,128)(2,1)S(1)} %get-tuple-element.65.refs_0_, bf16[8192,1024]{1,0:T(8,128)(2,1)} %refs_1_.7, f32[2,12,8]{2,1,0:T(8,128)S(1)} %get-tuple-element.112.refs_2_, f32[48,1024]{1,0:T(8,128)S(1)} %shard_map.144.refs_3_), custom_call_target="tpu_custom_call" | custom-call | flops 100663296 | bytes 2097152 | tf_op jit(solution)/shard_map/pallas_call | solution.py:332
  73.4 1.5 %collective-permute-start.27 = (bf16[24,1040]{1,0:T(8,128)(2,1)S(1)}, bf16[24,1040]{1,0:T(8,128)(2,1)S(1)}, u32[]{:S(2)}, u32[]{:S(2)}) collective-permute-start(bf16[24,1040]{1,0:T(8,128)(2,1)S(1)} %concatenate.29), channel_id=1, source_target_pairs={{0,16},{1,17},{2,18},{3,19},{4,20},{5,21},{6,22},{7,23},{8,24},{9,... | collective-permute-start | bytes 149768 | tf_op jit(solution)/shard_map/ppermute | solution.py:724
  74.9 2.7 %collective-permute-done.27.r_ref = bf16[24,1040]{1,0:T(8,128)(2,1)S(1)} collective-permute-done((bf16[24,1040]{1,0:T(8,128)(2,1)S(1)}, bf16[24,1040]{1,0:T(8,128)(2,1)S(1)}, u32[]{:S(2)}, u32[]{:S(2)}) %collective-permute-start.27) | collective-permute-done | bytes 49952 | tf_op jit(solution)/shard_map/ppermute | solution.py:724
  (125 shorter events, 18.1 us)
Async XLA Ops:
  2.9 11.3 %collective-permute-start.1 = (bf16[16,2560]{1,0:T(8,128)(2,1)}, bf16[16,2560]{1,0:T(8,128)(2,1)S(1)}, u32[]{:S(2)}, u32[]{:S(2)}) collective-permute-start(bf16[16,2560]{1,0:T(8,128)(2,1)} %get-tuple-element.44.a_ref), channel_id=1, source_target_pairs={{0,8},{1,9},{2,10},{3,11},{4,12},{5,13},{6,14},{7,15},{8,0},{9,1},... | collective-permute-start | bytes 245768 | tf_op jit(solution)/shard_map/ppermute | solution.py:724
  7.0 7.2 %collective-permute-start.2 = (bf16[16,2560]{1,0:T(8,128)(2,1)}, bf16[16,2560]{1,0:T(8,128)(2,1)S(1)}, u32[]{:S(2)}, u32[]{:S(2)}) collective-permute-start(bf16[16,2560]{1,0:T(8,128)(2,1)} %get-tuple-element.45), channel_id=1, source_target_pairs={{0,12},{1,13},{2,14},{3,15},{4,8},{5,9},{6,10},{7,11},{8,4},{9,5},... | collective-permute-start | bytes 245768 | tf_op jit(solution)/shard_map/ppermute | solution.py:724
  8.3 6.0 %collective-permute-start = (bf16[16,2560]{1,0:T(8,128)(2,1)}, bf16[16,2560]{1,0:T(8,128)(2,1)S(1)}, u32[]{:S(2)}, u32[]{:S(2)}) collective-permute-start(bf16[16,2560]{1,0:T(8,128)(2,1)} %get-tuple-element.45), channel_id=1, source_target_pairs={{0,4},{1,5},{2,6},{3,7},{4,0},{5,1},{6,2},{7,3},{8,12},{9,13},{10,... | collective-permute-start | bytes 245768 | tf_op jit(solution)/shard_map/ppermute | solution.py:724
  14.7 5.3 %collective-permute-start.3 = (bf16[32,2432]{1,0:T(8,128)(2,1)S(1)}, bf16[32,2432]{1,0:T(8,128)(2,1)S(1)}, u32[]{:S(2)}, u32[]{:S(2)}) collective-permute-start(bf16[32,2432]{1,0:T(8,128)(2,1)S(1)} %get-tuple-element.48.refs_3_), channel_id=1, source_target_pairs={{0,2},{1,3},{2,0},{3,1},{4,6},{5,7},{6,4},{7,5},{8,10},{9,11},{10,... | collective-permute-start | bytes 466952 | tf_op jit(solution)/shard_map/ppermute | solution.py:724
  20.1 3.9 %collective-permute-start.5 = (f32[48,32]{1,0:T(8,128)S(1)}, f32[48,32]{1,0:T(8,128)S(1)}, u32[]{:S(2)}, u32[]{:S(2)}) collective-permute-start(f32[48,32]{1,0:T(8,128)S(1)} %fusion.6), channel_id=1, source_target_pairs={{0,1},{1,0},{2,3},{3,2},{4,5},{5,4},{6,7},{7,6},{8,9},{9,8},{10,11... | collective-permute-start | bytes 18440 | tf_op jit(solution)/shard_map/ppermute | solution.py:724
  20.2 7.6 %collective-permute-start.4 = (bf16[24,1152]{1,0:T(8,128)(2,1)S(1)}, bf16[24,1152]{1,0:T(8,128)(2,1)S(1)}, u32[]{:S(2)}, u32[]{:S(2)}) collective-permute-start(bf16[24,1152]{1,0:T(8,128)(2,1)S(1)} %dynamic-slice_convert_fusion), channel_id=1, source_target_pairs={{0,8},{1,9},{2,10},{3,11},{4,12},{5,13},{6,14},{7,15},{8,0},{9,1},... | collective-permute-start | bytes 165896 | tf_op jit(solution)/shard_map/ppermute | solution.py:724
  27.9 4.2 %collective-permute-start.6 = (bf16[24,1216]{1,0:T(8,128)(2,1)S(1)}, bf16[24,1216]{1,0:T(8,128)(2,1)S(1)}, u32[]{:S(2)}, u32[]{:S(2)}) collective-permute-start(bf16[24,1216]{1,0:T(8,128)(2,1)S(1)} %concatenate.25), channel_id=1, source_target_pairs={{0,16},{1,17},{2,18},{3,19},{4,20},{5,21},{6,22},{7,23},{8,24},{9,... | collective-permute-start | bytes 175112 | tf_op jit(solution)/shard_map/ppermute | solution.py:724
  32.6 4.7 %collective-permute-start.11 = (bf16[54,128]{1,0:T(8,128)(2,1)S(1)}, bf16[54,128]{1,0:T(8,128)(2,1)S(1)}, u32[]{:S(2)}, u32[]{:S(2)}) collective-permute-start(bf16[54,128]{1,0:T(8,128)(2,1)S(1)} %get-tuple-element.96), channel_id=1, source_target_pairs={{0,6},{1,7},{2,4},{3,5},{4,2},{5,3},{6,0},{7,1},{8,14},{9,15},{10,... | collective-permute-start | bytes 41480 | tf_op jit(solution)/shard_map/ppermute | solution.py:724
  33.3 3.9 %collective-permute-start.10 = (bf16[54,128]{1,0:T(8,128)(2,1)S(1)}, bf16[54,128]{1,0:T(8,128)(2,1)S(1)}, u32[]{:S(2)}, u32[]{:S(2)}) collective-permute-start(bf16[54,128]{1,0:T(8,128)(2,1)S(1)} %get-tuple-element.97), channel_id=1, source_target_pairs={{0,2},{1,3},{2,0},{3,1},{4,6},{5,7},{6,4},{7,5},{8,10},{9,11},{10,... | collective-permute-start | bytes 41480 | tf_op jit(solution)/shard_map/ppermute | solution.py:724
  34.2 3.7 %collective-permute-start.9 = (bf16[54,128]{1,0:T(8,128)(2,1)S(1)}, bf16[54,128]{1,0:T(8,128)(2,1)S(1)}, u32[]{:S(2)}, u32[]{:S(2)}) collective-permute-start(bf16[54,128]{1,0:T(8,128)(2,1)S(1)} %get-tuple-element.98), channel_id=1, source_target_pairs={{0,4},{1,5},{2,6},{3,7},{4,0},{5,1},{6,2},{7,3},{8,12},{9,13},{10,... | collective-permute-start | bytes 41480 | tf_op jit(solution)/shard_map/ppermute | solution.py:724
  41.4 6.4 %collective-permute-start.15 = (bf16[192,128]{1,0:T(8,128)(2,1)S(1)}, bf16[192,128]{1,0:T(8,128)(2,1)S(1)}, u32[]{:S(2)}, u32[]{:S(2)}) collective-permute-start(bf16[192,128]{1,0:T(8,128)(2,1)S(1)} %bitcast.83), channel_id=1, source_target_pairs={{0,12},{1,13},{2,14},{3,15},{4,8},{5,9},{6,10},{7,11},{8,4},{9,5},... | collective-permute-start | bytes 147464 | tf_op jit(solution)/shard_map/ppermute | solution.py:724
  44.2 5.6 %collective-permute-start.14 = (bf16[192,128]{1,0:T(8,128)(2,1)S(1)}, bf16[192,128]{1,0:T(8,128)(2,1)S(1)}, u32[]{:S(2)}, u32[]{:S(2)}) collective-permute-start(bf16[192,128]{1,0:T(8,128)(2,1)S(1)} %bitcast.84), channel_id=1, source_target_pairs={{0,8},{1,9},{2,10},{3,11},{4,12},{5,13},{6,14},{7,15},{8,0},{9,1},... | collective-permute-start | bytes 147464 | tf_op jit(solution)/shard_map/ppermute | solution.py:724
  44.8 5.1 %collective-permute-start.13 = (bf16[192,128]{1,0:T(8,128)(2,1)S(1)}, bf16[192,128]{1,0:T(8,128)(2,1)S(1)}, u32[]{:S(2)}, u32[]{:S(2)}) collective-permute-start(bf16[192,128]{1,0:T(8,128)(2,1)S(1)} %bitcast.85), channel_id=1, source_target_pairs={{0,4},{1,5},{2,6},{3,7},{4,0},{5,1},{6,2},{7,3},{8,12},{9,13},{10,... | collective-permute-start | bytes 147464 | tf_op jit(solution)/shard_map/ppermute | solution.py:724
  45.8 5.7 %collective-permute-start.18 = (bf16[8,8192]{1,0:T(8,128)(2,1)S(1)}, bf16[8,8192]{1,0:T(8,128)(2,1)S(1)}, u32[]{:S(2)}, u32[]{:S(2)}) collective-permute-start(bf16[8,8192]{1,0:T(8,128)(2,1)S(1)} %bitcast.63), channel_id=1, source_target_pairs={{0,2},{1,3},{2,0},{3,1},{4,6},{5,7},{6,4},{7,5},{8,10},{9,11},{10,... | collective-permute-start | bytes 393224 | tf_op jit(solution)/shard_map/ppermute | solution.py:724
  49.9 6.4 %collective-permute-start.16 = (bf16[4,192,128]{2,1,0:T(8,128)(2,1)S(1)}, bf16[4,192,128]{2,1,0:T(8,128)(2,1)S(1)}, u32[]{:S(2)}, u32[]{:S(2)}) collective-permute-start(bf16[4,192,128]{2,1,0:T(8,128)(2,1)S(1)} %pad_maximum_fusion.p_ref.refs_0_), channel_id=1, source_target_pairs={{0,2},{1,3},{2,0},{3,1},{4,6},{5,7},{6,4},{7,5},{8,10},{9,11},{10,... | collective-permute-start | bytes 589832 | tf_op jit(solution)/shard_map/ppermute | solution.py:724
  52.1 8.5 %collective-permute-start.20 = (bf16[4,192,128]{2,1,0:T(8,128)(2,1)S(1)}, bf16[4,192,128]{2,1,0:T(8,128)(2,1)S(1)}, u32[]{:S(2)}, u32[]{:S(2)}) collective-permute-start(bf16[4,192,128]{2,1,0:T(8,128)(2,1)S(1)} %pad_maximum_fusion.p_ref.refs_0_), channel_id=1, source_target_pairs={{0,1},{1,0},{2,3},{3,2},{4,5},{5,4},{6,7},{7,6},{8,9},{9,8},{10,11... | collective-permute-start | bytes 589832 | tf_op jit(solution)/shard_map/ppermute | solution.py:724
  56.2 4.4 %collective-permute-start.21 = (bf16[4,192,128]{2,1,0:T(8,128)(2,1)S(1)}, bf16[4,192,128]{2,1,0:T(8,128)(2,1)S(1)}, u32[]{:S(2)}, u32[]{:S(2)}) collective-permute-start(bf16[4,192,128]{2,1,0:T(8,128)(2,1)S(1)} %collective-permute-done.16.refs_1_), channel_id=1, source_target_pairs={{0,1},{1,0},{2,3},{3,2},{4,5},{5,4},{6,7},{7,6},{8,9},{9,8},{10,11... | collective-permute-start | bytes 589832 | tf_op jit(solution)/shard_map/ppermute | solution.py:724
  56.3 8.2 %collective-permute-start.22 = (bf16[8,4224]{1,0:T(8,128)(2,1)S(1)}, bf16[8,4224]{1,0:T(8,128)(2,1)S(1)}, u32[]{:S(2)}, u32[]{:S(2)}) collective-permute-start(bf16[8,4224]{1,0:T(8,128)(2,1)S(1)} %get-tuple-element.68), channel_id=1, source_target_pairs={{0,4},{1,5},{2,6},{3,7},{4,0},{5,1},{6,2},{7,3},{8,12},{9,13},{10,... | collective-permute-start | bytes 202760 | tf_op jit(solution)/shard_map/ppermute | solution.py:724
  56.4 8.0 %collective-permute-start.23 = (bf16[8,4224]{1,0:T(8,128)(2,1)S(1)}, bf16[8,4224]{1,0:T(8,128)(2,1)S(1)}, u32[]{:S(2)}, u32[]{:S(2)}) collective-permute-start(bf16[8,4224]{1,0:T(8,128)(2,1)S(1)} %get-tuple-element.69), channel_id=1, source_target_pairs={{0,8},{1,9},{2,10},{3,11},{4,12},{5,13},{6,14},{7,15},{8,0},{9,1},... | collective-permute-start | bytes 202760 | tf_op jit(solution)/shard_map/ppermute | solution.py:724
  59.1 6.1 %collective-permute-start.24 = (bf16[8,4224]{1,0:T(8,128)(2,1)S(1)}, bf16[8,4224]{1,0:T(8,128)(2,1)S(1)}, u32[]{:S(2)}, u32[]{:S(2)}) collective-permute-start(bf16[8,4224]{1,0:T(8,128)(2,1)S(1)} %get-tuple-element.70), channel_id=1, source_target_pairs={{0,12},{1,13},{2,14},{3,15},{4,8},{5,9},{6,10},{7,11},{8,4},{9,5},... | collective-permute-start | bytes 202760 | tf_op jit(solution)/shard_map/ppermute | solution.py:724
  65.5 5.1 %collective-permute-start.25 = (bf16[32,2176]{1,0:T(8,128)(2,1)S(1)}, bf16[32,2176]{1,0:T(8,128)(2,1)S(1)}, u32[]{:S(2)}, u32[]{:S(2)}) collective-permute-start(bf16[32,2176]{1,0:T(8,128)(2,1)S(1)} %get-tuple-element.75.refs_2_), channel_id=1, source_target_pairs={{0,2},{1,3},{2,0},{3,1},{4,6},{5,7},{6,4},{7,5},{8,10},{9,11},{10,... | collective-permute-start | bytes 417800 | tf_op jit(solution)/shard_map/ppermute | solution.py:724
  67.0 7.9 %collective-permute-start.28 = (bf16[32,1024]{1,0:T(8,128)(2,1)S(1)}, bf16[32,1024]{1,0:T(8,128)(2,1)S(1)}, u32[]{:S(2)}, u32[]{:S(2)}) collective-permute-start(bf16[32,1024]{1,0:T(8,128)(2,1)S(1)} %get-tuple-element.81), channel_id=1, source_target_pairs={{0,1},{1,0},{2,3},{3,2},{4,5},{5,4},{6,7},{7,6},{8,9},{9,8},{10,11... | collective-permute-start | bytes 196616 | tf_op jit(solution)/shard_map/ppermute | solution.py:724
  73.0 4.5 %collective-permute-start.29 = (bf16[32,1024]{1,0:T(8,128)(2,1)S(1)}, bf16[32,1024]{1,0:T(8,128)(2,1)S(1)}, u32[]{:S(2)}, u32[]{:S(2)}) collective-permute-start(bf16[32,1024]{1,0:T(8,128)(2,1)S(1)} %get-tuple-element.82), channel_id=1, source_target_pairs={{0,1},{1,0},{2,3},{3,2},{4,5},{5,4},{6,7},{7,6},{8,9},{9,8},{10,11... | collective-permute-start | bytes 196616 | tf_op jit(solution)/shard_map/ppermute | solution.py:724
  73.4 4.2 %collective-permute-start.27 = (bf16[24,1040]{1,0:T(8,128)(2,1)S(1)}, bf16[24,1040]{1,0:T(8,128)(2,1)S(1)}, u32[]{:S(2)}, u32[]{:S(2)}) collective-permute-start(bf16[24,1040]{1,0:T(8,128)(2,1)S(1)} %concatenate.29), channel_id=1, source_target_pairs={{0,16},{1,17},{2,18},{3,19},{4,20},{5,21},{6,22},{7,23},{8,24},{9,... | collective-permute-start | bytes 149768 | tf_op jit(solution)/shard_map/ppermute | solution.py:724
  (17 other events, 113.6 us)
